TPU v7x, 32 devices: a whole 2x2x4 slice. The times are simulated.
32 devices in a mesh: gz: 4 (over y, x), xy: 8 (over z, core).
Axes of the slice: x: 2, y: 2, z: 4, core: 2. Of those that a mesh axis runs over, the one named last changes fastest.
Arguments:
- solution: float32 [16, 1536, 1536], P('gz', 'xy'), may hold values from -6 to 6
- residual: float32 [16, 1536, 1536], P('gz', 'xy'), may hold values from -14 to 14
- direction: float32 [16, 1536, 1536], P('gz', 'xy'), may hold values from -14 to 14
- volume_fraction: float32 [16, 1536, 1536], P('gz', 'xy'), may hold values from 0 to 1, as said below
- density: float32 [2], replicated, may hold values from 0.08 to 1.25, as said below
Outputs:
- new_solution: float32 [16, 1536, 1536], P('gz', 'xy')
- new_residual: float32 [16, 1536, 1536], P('gz', 'xy')
- new_direction: float32 [16, 1536, 1536], P('gz', 'xy')
Inputs may be any that keep to these rules, and one draw needn't show every extreme that they name: `volume_fraction`: 0 marks a cell filled with liquid and 1 a cell filled with gas; cells in between hold both. Entry 0 is the liquid's density and entry 1 the gas's.
All inputs are finite; a program needn't handle non-finite values.
Results may differ from a plain program's by a relative error of at most 0.0003.
Values sent between devices are 32-bit elements; how exact they have to be, the bound alone decides.
No kernel may reach another device: no remote copies, remote signals or barrier semaphores. Data moves between devices by JAX's collectives and lax.ppermute only.
A program may use at most 128 MiB of HBM per device.

v0:
```python
import jax
import jax.numpy as jnp
from jax import lax
from jax.sharding import PartitionSpec as P

HIGHEST_PRECISION = lax.Precision.HIGHEST


def with_halo(shard, sides, width):
    for axis, dim in sides:
        peers, length = (lax.axis_size(axis), shard.shape[dim])
        up = [(i, (i + 1) % peers) for i in range(peers - 1)]
        down = [(j, i) for i, j in up]
        last = lax.slice_in_dim(shard, length - width, length, axis=dim)
        first = lax.slice_in_dim(shard, 0, width, axis=dim)
        before = lax.ppermute(last, axis, up)
        after = lax.ppermute(first, axis, down)
        shard = jnp.concatenate([before, shard, after], axis=dim)
    return shard


def cosine_table(length):
    freq_ids = jnp.arange(length, dtype=jnp.int32)[:, None]
    cell_ids = jnp.arange(length, dtype=jnp.int32)[None, :]
    phase_ids = freq_ids * (2 * cell_ids + 1) % (4 * length)
    angles = jnp.pi / (2 * length) * phase_ids.astype(jnp.float32)
    weights = jnp.where(freq_ids == 0, jnp.sqrt(1.0 / length), jnp.sqrt(2.0 / length)).astype(
        jnp.float32
    )
    return weights * jnp.cos(angles)


def eigenvalues(length):
    halves = jnp.sin(
        jnp.pi / (2 * length) * jnp.arange(length, dtype=jnp.int32).astype(jnp.float32)
    )
    return 4.0 * halves * halves


def level_rows(height, total_depth, stiffness, spectrum):
    nothing = 0.0 * stiffness
    subdiagonal_entries = jnp.where(height > 0, -stiffness, nothing)
    super_diag = jnp.where(height < total_depth - 1, -stiffness, nothing)
    main_diag = (
        stiffness * spectrum
        + jnp.where(height > 0, stiffness, nothing)
        + jnp.where(height < total_depth - 1, stiffness, 2.0 * stiffness)
    )
    return (subdiagonal_entries, main_diag, super_diag)


def tridiagonal_solve(source_terms, column_heights, total_depth, stiffness, spectrum):

    def forward_pass(carried_state, step_element):
        ratio_before, elimination_before = carried_state
        source_term, height = step_element
        subdiagonal_entries, main_diag, super_diag = level_rows(
            height, total_depth, stiffness, spectrum
        )
        pivot_current = main_diag - subdiagonal_entries * ratio_before
        ratio_current = super_diag / pivot_current
        elimination_current = (
            source_term - subdiagonal_entries * elimination_before
        ) / pivot_current
        return ((ratio_current, elimination_current), (ratio_current, elimination_current))

    initial_state = (jnp.zeros_like(spectrum), jnp.zeros_like(source_terms[0]))
    unused_slot, (ratio_values, elimination_values) = lax.scan(
        forward_pass, initial_state, (source_terms, column_heights)
    )

    def backward_pass(value_following, step_element):
        ratio_current, elimination_current = step_element
        value_current = elimination_current - ratio_current * value_following
        return (value_current, value_current)

    unused_slot, solved_values = lax.scan(
        backward_pass,
        jnp.zeros_like(source_terms[0]),
        (ratio_values, elimination_values),
        reverse=True,
    )
    return solved_values


def apply_operator(padded, dense_pad, level_base, column_base, total_width):
    centre = padded[1:-1, 1:-1, :]
    dense_mid = dense_pad[1:-1, 1:-1, :]
    shape_mid = centre.shape
    level_ids = level_base + lax.broadcasted_iota(jnp.int32, shape_mid, 0)
    column_ids = column_base + lax.broadcasted_iota(jnp.int32, shape_mid, 1)
    row_ids = lax.broadcasted_iota(jnp.int32, shape_mid, 2)
    side_pad = jnp.pad(centre, ((0, 0), (0, 0), (1, 1)))
    dense_side = jnp.pad(dense_mid, ((0, 0), (0, 0), (1, 1)))
    pairs = [
        (padded[2:, 1:-1, :], dense_pad[2:, 1:-1, :], level_ids >= 0),
        (padded[:-2, 1:-1, :], dense_pad[:-2, 1:-1, :], level_ids > 0),
        (padded[1:-1, 2:, :], dense_pad[1:-1, 2:, :], column_ids < total_width - 1),
        (padded[1:-1, :-2, :], dense_pad[1:-1, :-2, :], column_ids > 0),
        (side_pad[:, :, 2:], dense_side[:, :, 2:], row_ids < shape_mid[2] - 1),
        (side_pad[:, :, :-2], dense_side[:, :, :-2], row_ids > 0),
    ]
    result = jnp.zeros(shape_mid, jnp.float32)
    for neighbour, dense_next, inside in pairs:
        result = result + jnp.where(
            inside, 2.0 / (dense_mid + dense_next) * (centre - neighbour), 0.0
        )
    return result


def body(solution, residual, direction, volume_fraction, density):
    slab_depth, slab_width, span_len = residual.shape
    groups = lax.axis_size("gz")
    plane_parts = lax.axis_size("xy")
    total_depth = slab_depth * groups
    total_width = slab_width * plane_parts
    block_rows = span_len // plane_parts
    level_base = lax.axis_index("gz") * slab_depth
    column_base = lax.axis_index("xy") * slab_width
    density_field = volume_fraction * density[1] + (1.0 - volume_fraction) * density[0]
    stiffness = 0.5 * (1.0 / density[0] + 1.0 / density[1])
    table_x = cosine_table(total_width)
    table_y = cosine_table(span_len)
    eigen_x = eigenvalues(total_width)
    eigen_y = eigenvalues(span_len)
    split_x = table_x.reshape(total_width, plane_parts, slab_width)
    split_y = table_y.reshape(plane_parts, block_rows, span_len)
    along_y = jnp.einsum("zxy,bjy->zbjx", residual, split_y, precision=HIGHEST_PRECISION)
    sub_rows = block_rows // groups
    packed = along_y.reshape(slab_depth, plane_parts, groups, sub_rows * slab_width)
    column_data = lax.all_to_all(
        lax.all_to_all(packed, "gz", split_axis=2, concat_axis=0, tiled=True),
        "xy",
        split_axis=1,
        concat_axis=1,
        tiled=True,
    )
    column_data = column_data.reshape(total_depth, plane_parts, sub_rows, slab_width)
    column_spec = jnp.einsum("zbjx,kbx->zjk", column_data, split_x, precision=HIGHEST_PRECISION)
    first_row = lax.axis_index("xy") * block_rows + lax.axis_index("gz") * sub_rows
    spectrum = lax.dynamic_slice_in_dim(eigen_y, first_row, sub_rows)[:, None] + eigen_x[None, :]
    column_heights = jnp.arange(total_depth, dtype=jnp.int32)
    column_sol = tridiagonal_solve(column_spec, column_heights, total_depth, stiffness, spectrum)
    back_x = jnp.einsum("zjk,kbx->zbjx", column_sol, split_x, precision=HIGHEST_PRECISION)
    back_x = back_x.reshape(total_depth, plane_parts, 1, sub_rows * slab_width)
    returned = lax.all_to_all(
        lax.all_to_all(back_x, "gz", split_axis=0, concat_axis=2, tiled=True),
        "xy",
        split_axis=1,
        concat_axis=1,
        tiled=True,
    )
    returned = returned.reshape(slab_depth, plane_parts, block_rows, slab_width)
    precond = jnp.einsum("zbjx,bjy->zxy", returned, split_y, precision=HIGHEST_PRECISION)
    padded_all = (
        with_halo(density_field, (("gz", 0), ("xy", 1)), 1),
        with_halo(direction, (("gz", 0), ("xy", 1)), 1),
        with_halo(precond, (("gz", 0), ("xy", 1)), 1),
    )
    image_old = apply_operator(padded_all[1], padded_all[0], level_base, column_base, total_width)
    image_new = apply_operator(padded_all[2], padded_all[0], level_base, column_base, total_width)
    local_products = jnp.stack(
        [
            jnp.sum(direction * image_old),
            jnp.sum(precond * image_old),
            jnp.sum(residual * precond),
            jnp.sum(residual * direction),
            jnp.sum(precond * image_new),
            jnp.sum(direction * image_new),
        ]
    )
    totals = lax.psum(local_products, ("gz", "xy"))
    conjugate = -totals[1] / totals[0]
    along_r = totals[2] + conjugate * totals[3]
    curvature = totals[4] + conjugate * (totals[1] + totals[5]) + conjugate * conjugate * totals[0]
    step_len = along_r / curvature
    new_direction = precond + conjugate * direction
    new_solution = solution + step_len * new_direction
    new_residual = residual - step_len * (image_new + conjugate * image_old)
    return (new_solution, new_residual, new_direction)


def solution(mesh):
    placed = (
        P("gz", "xy", None),
        P("gz", "xy", None),
        P("gz", "xy", None),
        P("gz", "xy", None),
        P(),
    )
    return jax.shard_map(
        body,
        mesh=mesh,
        in_specs=placed,
        out_specs=(P("gz", "xy", None), P("gz", "xy", None), P("gz", "xy", None)),
        check_vma=False,
    )
```

profile of v0, /device:TPU:0, one launch (start us, length us, event | category | flops | bytes accessed | tf_op | source)
XLA Modules:
  0.0 883.4 jit_solution(9867686629141525420)
XLA Ops:
  0.7 69.6 %fusion.131 = f32[4,8,192,192]{3,2,0,1:T(8,128)} fusion(f32[4,192,1536]{2,1,0:T(8,128)} %param.10, s32[1536]{0:T(1024)S(1)} %multiply_add_fusion.3, s32[8,192]{1,0:T(8,128)S(1)} %multiply_add_fusion.5, f32[8,192]{1,0:T(8,128)S(1)} %compare_select_fusion), kind=kOutput, calls=%fused_computation.170 | convolution fusion | flops 21766864896 | bytes 9455616 | tf_op jit(solution)/shard_map/zxy,bjy->zbjx/dot_general | solution.py:128
  70.2 7.5 reshape.143
  77.7 5.1 copy.14
  82.8 58.4 %all_to_all.46 = f32[4,8,4,9216]{3,1,0,2:T(8,128)S(1)} all-to-all(f32[4,8,4,9216]{3,1,0,2:T(8,128)S(1)} %copy.14), channel_id=1, replica_groups=mesh['gz'=4,'xy'=8] {'gz'}, dimensions={2} | all-to-all | bytes 9437184 | tf_op jit(solution)/shard_map/all_to_all | solution.py:132
  141.2 4.9 copy.15
  146.2 5.2 all-to-all-start.1
  153.6 37.3 %fusion.183 = f32[1536,8,192,1]{0,2,1,3:T(8,128)} fusion(s32[8,192]{1,0:T(8,128)S(1)} %multiply_add_fusion.4, f32[1536]{0:T(1024)S(1)} %fusion.141), kind=kLoop, calls=%fused_computation.32.clone.clone.clone.clone.1 | loop fusion | flops 23592960 | bytes 9449472 | tf_op jit(solution)/shard_map/zbjx,kbx->zjk/dot_general | solution.py:139
  190.9 37.3 %fusion.185 = f32[1536,8,192,1]{0,2,3,1:T(8,128)} fusion(s32[8,192]{1,0:T(8,128)S(1)} %multiply_add_fusion.4, f32[1536]{0:T(1024)S(1)} %fusion.141), kind=kLoop, calls=%fused_computation.22.clone.clone.clone.clone.1 | loop fusion | flops 23592960 | bytes 9449472 | tf_op jit(solution)/shard_map/zjk,kbx->zbjx/dot_general | solution.py:144
  228.2 28.5 %all-to-all-done.1 = f32[16,8,1,9216]{3,0,2,1:T(8,128)} async-done(((f32[16,8,1,9216]{3,0,2,1:T(8,128)}), f32[16,8,1,9216]{3,0,2,1:T(8,128)}, u32[]{:S(2)}, u32[]{:S(2)}) %all-to-all-start.1) | async-done | bytes 4718624 | tf_op jit(solution)/shard_map/all_to_all | solution.py:131
  256.7 7.3 copy.16
  263.9 6.8 reshape.144
  270.7 38.9 %fusion.128 = f32[16,48,1536]{2,1,0:T(8,128)} fusion(f32[16,8,48,192]{3,2,1,0:T(8,128)} %reshape.144, f32[1536,8,192,1]{0,2,1,3:T(8,128)} %fusion.183), kind=kOutput, calls=%fused_computation.169 | convolution fusion | flops 21743271936 | bytes 18874368 | tf_op jit(solution)/shard_map/zbjx,kbx->zjk/dot_general | solution.py:139
  309.6 2.8 broadcast.282.clone
  312.4 2.8 broadcast.282.clone.1
  315.1 61.9 %while.35 = (s32[]{:T(128)}, f32[48,1536]{1,0:T(8,128)S(1)}, f32[48,1536]{1,0:T(8,128)S(1)}, f32[16,48,1536]{2,1,0:T(8,128)}, f32[16,48,1536]{2,1,0:T(8,128)}, /...) while((s32[]{:T(128)}, f32[48,1536]{1,0:T(8,128)S(1)}, ...), condition=%wide.region_2.3_spmd.clone, body=%wide.region_1.2_spmd.clone.sunk | while | flops 884745 | bytes 2072009 | solution.py:68
  377.0 2.8 broadcast.282
  379.8 32.3 %while.36 = (s32[]{:T(128)}, f32[48,1536]{1,0:T(8,128)S(1)}, f32[16,48,1536]{2,1,0:T(8,128)}, f32[16,48,1536]{2,1,0:T(8,128)}, f32[16,48,1536]{2,1,0:T(8,128)}, /*index=5*/s32[]{:T(128)}, s32[]{:T(128)}, s32[]{:T(128)}) while((s32[]{:T(128)}, f32[48,1536]{1,0:T(8,128)S(1)}, f32[16,48,1536]{2,1,0:T(8,128)}, ...), condition=%wide.region_4.5_spmd.clone, body=%wide.region_3.4_spmd.clone.sunk | while | flops 221188 | bytes 1474671 | solution.py:77
  379.8 2.0 bitcast_dynamic-update-slice_fusion.6
  381.8 2.0 bitcast_dynamic-update-slice_fusion.6
  387.9 2.0 bitcast_dynamic-update-slice_fusion.6
  389.9 2.0 bitcast_dynamic-update-slice_fusion.6
  391.9 2.0 bitcast_dynamic-update-slice_fusion.6
  398.0 2.0 bitcast_dynamic-update-slice_fusion.6
  412.1 34.6 %fusion.136 = f32[16,8,48,192]{3,2,0,1:T(8,128)} fusion(f32[16,48,1536]{2,1,0:T(8,128)} %get-tuple-element.203, f32[1536,8,192,1]{0,2,3,1:T(8,128)} %fusion.185), kind=kOutput, calls=%fused_computation.171 | convolution fusion | flops 21743271936 | bytes 18874368 | tf_op jit(solution)/shard_map/zjk,kbx->zbjx/dot_general | solution.py:144
  446.7 6.5 reshape.145
  453.2 5.1 copy.17
  458.3 56.3 %all_to_all.47 = f32[16,8,1,9216]{3,1,2,0:T(8,128)S(1)} all-to-all(f32[16,8,1,9216]{3,1,2,0:T(8,128)S(1)} %copy.17), channel_id=1, replica_groups=mesh['gz'=4,'xy'=8] {'gz'}, dimensions={0} | all-to-all | bytes 9437184 | tf_op jit(solution)/shard_map/all_to_all | solution.py:147
  514.6 5.2 copy.18
  519.8 4.7 all-to-all-start.3
  524.6 4.7 multiply_add_fusion.2
  532.3 5.6 collective-permute-start.2
  539.5 2.8 collective-permute-start.3
  543.7 18.3 %collective-permute-done = f32[1,192,1536]{2,1,0:T(8,128)} collective-permute-done((f32[1,192,1536]{2,1,0:T(8,128)}, f32[1,192,1536]{2,1,0:T(8,128)}, u32[]{:S(2)}, u32[]{:S(2)}) %collective-permute-start) | collective-permute-done | bytes 1179680 | tf_op jit(solution)/shard_map/ppermute | solution.py:17
  565.9 3.0 collective-permute-start.6
  569.0 60.9 %all-to-all-done.3 = f32[4,8,4,9216]{3,0,2,1:T(4,128)} async-done(((f32[4,8,4,9216]{3,0,2,1:T(4,128)}), f32[4,8,4,9216]{3,0,2,1:T(4,128)}, u32[]{:S(2)}, u32[]{:S(2)}) %all-to-all-start.3) | async-done | bytes 4718624 | tf_op jit(solution)/shard_map/all_to_all | solution.py:146
  629.8 7.6 copy.19
  637.4 7.4 reshape.146
  644.8 70.1 %fusion.125 = f32[4,192,1536]{2,1,0:T(8,128)S(1)} fusion(f32[4,8,192,192]{3,2,1,0:T(8,128)} %reshape.146, s32[1536]{0:T(1024)S(1)} %multiply_add_fusion.3, s32[8,192]{1,0:T(8,128)S(1)} %multiply_add_fusion.5, f32[8,192]{1,0:T(8,128)S(1)} %compare_select_fusion), kind=kOutput, calls=%fused_computation.168 | convolution fusion | flops 21766864896 | bytes 9455616 | tf_op jit(solution)/shard_map/zbjx,bjy->zxy/dot_general | solution.py:154
  716.4 4.6 collective-permute-start.9
  721.1 2.7 constant_dynamic-update-slice_fusion.1
  725.1 2.9 copy-done.4
  729.4 16.5 %collective-permute-done.8 = f32[1,192,1536]{2,1,0:T(8,128)S(1)} collective-permute-done((f32[1,192,1536]{2,1,0:T(8,128)S(1)}, f32[1,192,1536]{2,1,0:T(8,128)S(1)}, u32[]{:S(2)}, u32[]{:S(2)}) %collective-permute-start.8) | collective-permute-done | bytes 1179680 | tf_op jit(solution)/shard_map/ppermute | solution.py:17
  749.5 3.0 collective-permute-start.11
  753.4 40.0 %multiply_reduce_fusion = (f32[]{:T(128)}, f32[]{:T(128)}, f32[]{:T(128)}, f32[]{:T(128)}, f32[]{:T(128)}, /*index=5*/f32[]{:T(128)}, f32[4,192,1536]{2,1,0:T(8,128)}, f32[4,192,1536]{2,1,0:T(8,128)}) fusion(f32[4,192,1536]{2,1,0:T(8,128)} %param.11, f32[4,192,1536]{2,1,0:T(8,128)S(1)} %fusion.125, f32[4,192,1536]{2,1,0:T(8,128)} %param.10, ...), kind=kLoop, calls=%fused_computation.139 | loop fusion | flops 110886912 | bytes 42692000 | tf_op jit(solution)/shard_map/reduce_sum | solution.py:169
  793.4 3.8 stack.27
  797.2 63.1 %psum.7 = f32[6]{0:T(128)S(1)} all-reduce(f32[6]{0:T(128)S(1)} %stack.27), channel_id=1, replica_groups=mesh['gz'=4,'xy'=8] {'gz','xy'}, use_global_device_ids=true, to_apply=%region_10.11 | all-reduce | flops 6 | bytes 48 | tf_op jit(solution)/shard_map/psum | solution.py:172
  866.2 10.8 %multiply_add_fusion = (f32[4,192,1536]{2,1,0:T(8,128)}, f32[4,192,1536]{2,1,0:T(8,128)}) fusion(f32[4,192,1536]{2,1,0:T(8,128)} %param.9, f32[]{:T(128)S(6)} %div.57, f32[4,192,1536]{2,1,0:T(8,128)} %copy-done, f32[4,192,1536]{2,1,0:T(8,128)} %param.11, f32[]{:T(128)S(6)} %div.56), kind=kLoop, calls=%fused_computation.137 | loop fusion | flops 4718592 | bytes 23592968 | tf_op jit(solution)/shard_map/add | solution.py:178
  877.0 6.2 multiply_subtract_fusion
  (103 shorter events, 81.3 us)
Async XLA Ops:
  146.2 5.3 copy-start.7
  146.2 110.5 %all-to-all-start.1 = ((f32[16,8,1,9216]{3,0,2,1:T(8,128)}), f32[16,8,1,9216]{3,0,2,1:T(8,128)}, u32[]{:S(2)}, u32[]{:S(2)}) async-start(f32[16,8,1,9216]{3,0,2,1:T(8,128)} %copy.15), calls=%async_computation.1 | async-start | bytes 9437184 | tf_op jit(solution)/shard_map/all_to_all | solution.py:131
  519.8 18.0 %slice-start = ((s8[4718592]{0:T(1024)(128)(4,1)}), s8[524288]{0:T(1024)(128)(4,1)S(1)}, s32[]{:S(2)}) async-start(s8[4718592]{0:T(1024)(128)(4,1)} %bitcast.131), calls=%async_computation.4 | async-start | bytes 1048576
  519.8 110.0 %all-to-all-start.3 = ((f32[4,8,4,9216]{3,0,2,1:T(4,128)}), f32[4,8,4,9216]{3,0,2,1:T(4,128)}, u32[]{:S(2)}, u32[]{:S(2)}) async-start(f32[4,8,4,9216]{3,0,2,1:T(4,128)} %copy.18), calls=%async_computation.3 | async-start | bytes 9437184 | tf_op jit(solution)/shard_map/all_to_all | solution.py:146
  524.6 13.3 %slice-start.1 = ((s8[4718592]{0:T(1024)(128)(4,1)}), s8[4194304]{0:T(1024)(128)(4,1)S(1)}, s32[]{:S(2)}) async-start(s8[4718592]{0:T(1024)(128)(4,1)} %bitcast.131), calls=%async_computation.5 | async-start | bytes 8388608
  529.3 10.2 %copy-start.1 = (f32[4,192,1536]{2,1,0:T(8,128)}, f32[4,192,1536]{2,1,0:T(8,128)S(1)}, u32[]{:S(2)}) copy-start(f32[4,192,1536]{2,1,0:T(8,128)S(1)} %multiply_add_fusion.2) | copy-start | bytes 14155780
  531.0 31.0 %collective-permute-start = (f32[1,192,1536]{2,1,0:T(8,128)}, f32[1,192,1536]{2,1,0:T(8,128)}, u32[]{:S(2)}, u32[]{:S(2)}) collective-permute-start(f32[1,192,1536]{2,1,0:T(8,128)} %get-tuple-element.331), channel_id=1, source_target_pairs={{8,0},{16,8},{24,16},{9,1},{17,9},{25,17},{10,2},{18,10},{26,18},{... | collective-permute-start | bytes 3538952 | tf_op jit(solution)/shard_map/ppermute | solution.py:17
  532.3 31.2 %collective-permute-start.2 = (f32[1,192,1536]{2,1,0:T(8,128)}, f32[1,192,1536]{2,1,0:T(8,128)}, u32[]{:S(2)}, u32[]{:S(2)}) collective-permute-start(f32[1,192,1536]{2,1,0:T(8,128)} %get-tuple-element.330), channel_id=1, source_target_pairs={{0,8},{8,16},{16,24},{1,9},{9,17},{17,25},{2,10},{10,18},{18,26},{... | collective-permute-start | bytes 3538952 | tf_op jit(solution)/shard_map/ppermute | solution.py:16
  539.5 176.9 %collective-permute-start.3 = (f32[1,192,1536]{2,1,0:T(8,128)}, f32[1,192,1536]{2,1,0:T(8,128)S(1)}, u32[]{:S(2)}, u32[]{:S(2)}) collective-permute-start(f32[1,192,1536]{2,1,0:T(8,128)} %get-tuple-element.333), channel_id=1, source_target_pairs={{0,8},{8,16},{16,24},{1,9},{9,17},{17,25},{2,10},{10,18},{18,26},{... | collective-permute-start | bytes 3538952 | tf_op jit(solution)/shard_map/ppermute | solution.py:16
  542.3 181.4 %collective-permute-start.1 = (f32[1,192,1536]{2,1,0:T(8,128)}, f32[1,192,1536]{2,1,0:T(8,128)}, u32[]{:S(2)}, u32[]{:S(2)}) collective-permute-start(f32[1,192,1536]{2,1,0:T(8,128)} %get-tuple-element.332), channel_id=1, source_target_pairs={{8,0},{16,8},{24,16},{9,1},{17,9},{25,17},{10,2},{18,10},{26,18},{... | collective-permute-start | bytes 3538952 | tf_op jit(solution)/shard_map/ppermute | solution.py:17
  564.6 184.9 %collective-permute-start.4 = (f32[6,1,1536]{2,1,0:T(1,128)S(1)}, f32[6,1,1536]{2,1,0:T(1,128)S(1)}, u32[]{:S(2)}, u32[]{:S(2)}) collective-permute-start(f32[6,1,1536]{2,1,0:T(1,128)S(1)} %get-tuple-element.324), channel_id=1, source_target_pairs={{1,0},{2,1},{3,2},{4,3},{5,4},{6,5},{7,6},{9,8},{10,9},{11,10},{12... | collective-permute-start | bytes 110600 | tf_op jit(solution)/shard_map/ppermute | solution.py:17
  565.9 186.6 %collective-permute-start.6 = (f32[6,1,1536]{2,1,0:T(1,128)S(1)}, f32[6,1,1536]{2,1,0:T(1,128)S(1)}, u32[]{:S(2)}, u32[]{:S(2)}) collective-permute-start(f32[6,1,1536]{2,1,0:T(1,128)S(1)} %get-tuple-element.325), channel_id=1, source_target_pairs={{0,1},{1,2},{2,3},{3,4},{4,5},{5,6},{6,7},{8,9},{9,10},{10,11},{11... | collective-permute-start | bytes 110600 | tf_op jit(solution)/shard_map/ppermute | solution.py:16
  714.9 38.5 %copy-start = (f32[4,192,1536]{2,1,0:T(8,128)}, f32[4,192,1536]{2,1,0:T(8,128)S(1)}, u32[]{:S(2)}) copy-start(f32[4,192,1536]{2,1,0:T(8,128)S(1)} %fusion.125) | copy-start | bytes 14155780
  715.1 30.8 %collective-permute-start.8 = (f32[1,192,1536]{2,1,0:T(8,128)S(1)}, f32[1,192,1536]{2,1,0:T(8,128)S(1)}, u32[]{:S(2)}, u32[]{:S(2)}) collective-permute-start(f32[1,192,1536]{2,1,0:T(8,128)S(1)} %get-tuple-element.329), channel_id=1, source_target_pairs={{8,0},{16,8},{24,16},{9,1},{17,9},{25,17},{10,2},{18,10},{26,18},{... | collective-permute-start | bytes 3538952 | tf_op jit(solution)/shard_map/ppermute | solution.py:17
  716.4 30.8 %collective-permute-start.9 = (f32[1,192,1536]{2,1,0:T(8,128)S(1)}, f32[1,192,1536]{2,1,0:T(8,128)S(1)}, u32[]{:S(2)}, u32[]{:S(2)}) collective-permute-start(f32[1,192,1536]{2,1,0:T(8,128)S(1)} %get-tuple-element.328), channel_id=1, source_target_pairs={{0,8},{8,16},{16,24},{1,9},{9,17},{17,25},{2,10},{10,18},{18,26},{... | collective-permute-start | bytes 3538952 | tf_op jit(solution)/shard_map/ppermute | solution.py:16
  725.1 2.9 copy-start.4
  728.1 24.5 %collective-permute-start.5 = (f32[6,1,1536]{2,1,0:T(1,128)S(1)}, f32[6,1,1536]{2,1,0:T(1,128)S(1)}, u32[]{:S(2)}, u32[]{:S(2)}) collective-permute-start(f32[6,1,1536]{2,1,0:T(1,128)S(1)} %get-tuple-element.326), channel_id=1, source_target_pairs={{1,0},{2,1},{3,2},{4,3},{5,4},{6,5},{7,6},{9,8},{10,9},{11,10},{12... | collective-permute-start | bytes 110600 | tf_op jit(solution)/shard_map/ppermute | solution.py:17
  745.8 1.3 copy-start.5
  745.9 6.7 collective-permute-start.7
  747.2 1.0 copy-start.6
  748.2 4.4 collective-permute-start.10
  749.5 3.9 collective-permute-start.11
  866.2 10.8 %copy-start.2 = (f32[4,192,1536]{2,1,0:T(8,128)S(1)}, f32[4,192,1536]{2,1,0:T(8,128)}, u32[]{:S(2)}) copy-start(f32[4,192,1536]{2,1,0:T(8,128)} %get-tuple-element.318) | copy-start | bytes 14155780
  866.2 10.8 %copy-start.3 = (f32[4,192,1536]{2,1,0:T(8,128)S(1)}, f32[4,192,1536]{2,1,0:T(8,128)}, u32[]{:S(2)}) copy-start(f32[4,192,1536]{2,1,0:T(8,128)} %get-tuple-element.319) | copy-start | bytes 14155780
where the time goes:
time: 900 us; the launch traced here: 883 us
  matrix products  213 us (24%)
  other arithmetic  201 us (22%)
  blocking collectives  178 us (20%)
  waiting for transfers between devices  126 us (14%)
  local copies, waits for them, and re-layouts  98 us (11%)
  starting transfers between devices  38.1 us (4%)
  loops' own time  20.7 us (2%)
    dot_general x1, matrix products, body(): jnp.einsum('zbjx,bjy->zxy', returned, split_y, precision=HIGHEST_PRECISION)  70.1 us
    dot_general x1, matrix products, body(): jnp.einsum('zxy,bjy->zbjx', residual, split_y, precision=HIGHEST_PRECISION)  69.6 us
    dynamic_update_slice x32, other arithmetic, tridiagonal_solve(): lax.scan(forward_pass, initial_state, (source_terms, column_heights))  63.7 us
    psum x1, blocking collectives, body(): totals = lax.psum(local_products, ('gz', 'xy'))  63.1 us
    all_to_all x1, waiting for transfers between devices, body(): lax.all_to_all(lax.all_to_all(back_x, 'gz', split_axis=0, concat_axis=2,...  60.9 us
    all_to_all x1, blocking collectives, body(): lax.all_to_all(packed, 'gz', split_axis=2, concat_axis=0, tiled=True)  58.4 us
    all_to_all x1, blocking collectives, body(): lax.all_to_all(back_x, 'gz', split_axis=0, concat_axis=2, tiled=True)  56.3 us
    reduce_sum x1, other arithmetic, body(): jnp.sum(direction * image_new)  40 us
  transfers between devices with their start and end apart: 14, of which 6 were waited for; matrix products, arithmetic and copies ran while one was open for 20% of the time, Pallas kernels for 0%

commit v1 on v0

v1 whole, which is shorter than its diff:
```python
import functools

import jax
import jax.numpy as jnp
import numpy as np
from jax import lax
from jax.experimental import pallas as pl
from jax.experimental.pallas import tpu as pltpu
from jax.sharding import PartitionSpec as P

F32 = jnp.float32
BF16 = jnp.bfloat16
MIB = 1024 * 1024


def divisor_of(length, unit, largest):
    return max(t for t in range(unit, largest + 1, unit) if length % t == 0)


def halves_of(table):
    high = table.astype(BF16)
    low = (table - high.astype(np.float64)).astype(BF16)
    return high, low


def split(values):
    high = values.astype(BF16)
    return high, (values - high.astype(F32)).astype(BF16)


def dot(a, b):
    return jnp.dot(a, b, preferred_element_type=F32)


def dot3(a_high, a_low, b_high, b_low):
    return dot(a_high, b_high) + (dot(a_low, b_high) + dot(a_high, b_low))


def cosine_table(length):
    freq = np.arange(length)[:, None]
    cell = np.arange(length)[None, :]
    angles = np.pi / (2 * length) * (freq * (2 * cell + 1) % (4 * length))
    return np.where(freq == 0, np.sqrt(1.0 / length), np.sqrt(2.0 / length)) * np.cos(angles)


def spectral_order(length):
    return np.concatenate([np.arange(0, length, 2), np.arange(1, length, 2)])


def half_tables(length):
    half = length // 2
    return cosine_table(length)[spectral_order(length), :half].reshape(2, half, half)


def eigenvalues(length):
    return 4.0 * np.sin(np.pi * np.arange(length) / (2 * length)) ** 2


def level_table(depth):
    modes = np.arange(depth)[:, None]
    levels = np.arange(depth)[None, :]
    return np.sqrt(2.0 / depth) * np.cos(np.pi * (2 * modes + 1) * (2 * levels + 1) / (4 * depth))


def decay_table(length, depth):
    mu = eigenvalues(length)[spectral_order(length)]
    lam = 4.0 * np.sin(np.pi * (2 * np.arange(depth) + 1) / (4 * depth)) ** 2
    excess = lam[:, None] + mu[None, :]
    return (1.0 + excess / 2 - np.sqrt(excess + excess * excess / 4)).astype(np.float32)


def flip_matrix(size):
    return np.eye(size)[::-1].astype(BF16)


def flipped(high, low, flip):
    size = flip.shape[0]
    count = high.shape[1] // size
    blocks = []
    for i in range(count):
        part = slice((count - 1 - i) * size, (count - i) * size)
        blocks.append(dot(high[:, part], flip) + dot(low[:, part], flip))
    return jnp.concatenate(blocks, axis=1)


def power(base, exponent):
    result = None
    while exponent:
        if exponent & 1:
            result = base if result is None else result * base
        base = base * base
        exponent >>= 1
    return result


def fixed(shape):
    return pl.BlockSpec(shape, lambda *_: (0,) * len(shape))


def in_hbm(array):
    return pltpu.with_memory_space_constraint(array, pltpu.HBM)


def hbm(shape):
    return pltpu.HBM(shape, F32)


def params(mib=24):
    return pltpu.CompilerParams(vmem_limit_bytes=mib * MIB)


def cost(flops, count):
    return pl.CostEstimate(flops=int(flops) // 16, bytes_accessed=int(count) // 4, transcendentals=0)


def forward_kernel(scale_ref, rows_ref, high_ref, low_ref, flip_ref, out_ref):
    half = rows_ref.shape[1] // 2
    first, second = rows_ref[:, :half], rows_ref[:, half:]
    mirror = flipped(*split(second), flip_ref[...])
    scale = scale_ref[0]
    for parity, folded in enumerate((first + mirror, first - mirror)):
        out = dot3(*split(folded), high_ref[parity], low_ref[parity])
        out_ref[:, parity * half : (parity + 1) * half] = scale * out


def flip_of(half):
    return flip_matrix(256 if half % 256 == 0 else 128)


def forward_rows(rows, scale):
    count, length = rows.shape
    half = length // 2
    tile = divisor_of(count, 8, 256)
    high, low = halves_of(half_tables(length).transpose(0, 2, 1))
    flip = flip_of(half)
    return pl.pallas_call(
        forward_kernel,
        grid=(count // tile,),
        in_specs=[
            pl.BlockSpec(memory_space=pltpu.SMEM),
            pl.BlockSpec((tile, length), lambda i: (i, 0)),
            fixed(high.shape),
            fixed(low.shape),
            fixed(flip.shape),
        ],
        out_specs=pl.BlockSpec((tile, length), lambda i: (i, 0)),
        out_shape=hbm((count, length)),
        compiler_params=params(28),
        cost_estimate=cost(6 * count * length * half, 2 * count * length),
        name="forward_rows",
    )(scale, in_hbm(rows), in_hbm(high), in_hbm(low), flip)


def own_rows(place_ref, jump_ref, slab):
    rows = []
    for side in range(2):
        for level in range(slab):
            at = pl.ds(place_ref[0] * slab + level, 1)
            rows.append(jnp.concatenate([jump_ref[g, side, at] for g in range(jump_ref.shape[0])], axis=1))
    return jnp.concatenate(rows, axis=0)


def inverse_kernel(first_call, place_ref, density_ref, even_ref, odd_ref, high_ref, low_ref, flip_ref, *refs):
    half = even_ref.shape[1]

    def joined(even_part, odd_part):
        even = dot3(*split(even_part), high_ref[0], low_ref[0])
        odd = dot3(*split(odd_part), high_ref[1], low_ref[1])
        return even + odd, flipped(*split(even - odd), flip_ref[...])

    out_ref = refs[-3] if first_call else refs[0]
    first, second = joined(even_ref[...], odd_ref[...])
    out_ref[:, :half] = first
    out_ref[:, half:] = second
    if first_call:
        even_jump, odd_jump, below_ref, bottom_ref, _, out_rows_ref, face_ref = refs
        width, slab = face_ref.shape[1], out_rows_ref.shape[0] // 2
        pair = [own_rows(place_ref, jump, slab) for jump in (even_jump, odd_jump)]
        first, second = joined(*pair)
        out_rows_ref[:, 0, :half] = first
        out_rows_ref[:, 0, half:] = second
        liquid, gas = density_ref[0], density_ref[1]
        fractions = below_ref[0] + bottom_ref[0]
        total = fractions * gas + (2.0 - fractions) * liquid
        face_ref[0] = twice_inverse(total) * (out_ref[:width] - out_ref[width:])


def inverse_rows(solved, all_jumps, below, fraction, density, place, width):
    count, length = solved.shape
    half = length // 2
    slab = count // width - 1
    groups, _, depth, lanes = all_jumps.shape
    high, low = halves_of(half_tables(2 * half))
    flip = flip_of(half)
    tables = [fixed(high.shape)] * 2 + [fixed(flip.shape)]
    solved, high, low = in_hbm(solved), in_hbm(high), in_hbm(low)
    smem = pl.BlockSpec(memory_space=pltpu.SMEM)

    def jump(parity):
        return pl.BlockSpec((groups // 2, 2, depth, lanes), lambda i, p: (parity, 0, 0, 0))

    rows = [pl.BlockSpec((2 * width, half), lambda i, p, k=k: (0, k)) for k in range(2)]
    plane = fixed((1, width, 2 * half))
    lower, jump_rows, face = pl.pallas_call(
        functools.partial(inverse_kernel, True),
        grid_spec=pltpu.PrefetchScalarGridSpec(
            num_scalar_prefetch=1,
            grid=(1,),
            in_specs=[smem] + rows + tables + [jump(0), jump(1), plane, plane],
            out_specs=[fixed((2 * width, 2 * half)), fixed((2 * slab, 1, 2 * half)), plane],
        ),
        out_shape=[
            jax.ShapeDtypeStruct((2 * width, 2 * half), F32),
            jax.ShapeDtypeStruct((2 * slab, 1, 2 * half), F32),
            jax.ShapeDtypeStruct((1, width, 2 * half), F32),
        ],
        compiler_params=params(36),
        cost_estimate=cost(28 * width * half * half, 8 * width * half),
        name="inverse_lower",
    )(place, density, solved, solved, high, low, flip, all_jumps, all_jumps, below, fraction)
    rest = (slab - 1) * width
    tile = max(t for t in (width, 2 * width, rest) if rest % t == 0 and t <= 384)
    skip = 2 * width // tile if 2 * width % tile == 0 else None
    if skip is None:
        tile, skip = width, 2
    rows = [pl.BlockSpec((tile, half), lambda i, p, k=k: (skip + i, k)) for k in range(2)]
    upper = pl.pallas_call(
        functools.partial(inverse_kernel, False),
        grid_spec=pltpu.PrefetchScalarGridSpec(
            num_scalar_prefetch=1,
            grid=(rest // tile,),
            in_specs=[smem] + rows + tables,
            out_specs=pl.BlockSpec((tile, 2 * half), lambda i, p: (i, 0)),
        ),
        out_shape=jax.ShapeDtypeStruct((rest, 2 * half), F32),
        compiler_params=params(36),
        cost_estimate=cost(14 * rest * half * half, 4 * rest * half),
        name="inverse_upper",
    )(place, density, solved, solved, high, low, flip)
    return (
        lower.reshape(2, width, 2 * half), upper.reshape(slab - 1, width, 2 * half), jump_rows, face
    )


def ends_kernel(cells, place_ref, field_ref, mixer_ref, ratio_ref, order_ref, out_ref):
    slab, width, lanes = field_ref.shape
    depth = ratio_ref.shape[0]
    ratio = ratio_ref[...]
    step_power = power(ratio, cells)

    def chunk(c, carry):
        right, left, weight = carry
        at = pl.multiple_of(c * cells, cells)
        stacked = field_ref[:, pl.ds(at, cells), :].reshape(slab * cells, lanes)
        high, low = split(stacked)
        modes = dot(mixer_ref[0], jnp.concatenate([high, low, high], axis=0))
        inner = modes[(cells - 1) * depth :]
        for k in reversed(range(cells - 1)):
            inner = inner * ratio + modes[k * depth : (k + 1) * depth]
        for k in range(cells):
            right = right * ratio + modes[k * depth : (k + 1) * depth]
        return right, left + weight * inner, weight * step_power

    zero = jnp.zeros((depth, lanes), F32)
    right, left, _ = lax.fori_loop(0, width // cells, chunk, (zero, zero, zero + 1.0), unroll=2)
    gain = ratio / (1.0 - ratio * ratio)
    left, right = left * gain, right * gain
    per, _, _, part = out_ref.shape
    for g in range(per):
        out_ref[g, 0] = left[:, g * part : (g + 1) * part]
        out_ref[g, 1] = right[:, g * part : (g + 1) * part]


def mode_mixers(depth, groups, cells):
    table = level_table(depth)
    slab = depth // groups
    mixers = []
    for me in range(groups):
        own = table[:, me * slab : (me + 1) * slab]
        mixed = np.einsum("kz,ab->akzb", own, np.eye(cells)).reshape(cells * depth, slab * cells)
        high, low = halves_of(mixed)
        mixers.append(np.concatenate([high, high, low], axis=1))
    return np.stack(mixers)


def end_responses(field, order, place, groups):
    slab, width, length = field.shape
    depth, lanes = slab * groups, length // groups
    cells = divisor_of(width, 8, 16)
    mixers = mode_mixers(depth, groups, cells)
    return pl.pallas_call(
        functools.partial(ends_kernel, cells),
        grid_spec=pltpu.PrefetchScalarGridSpec(
            num_scalar_prefetch=1,
            grid=(groups // 2,),
            in_specs=[
                pl.BlockSpec((slab, width, 2 * lanes), lambda i, p: (0, 0, i)),
                pl.BlockSpec((1,) + mixers.shape[1:], lambda i, p: (p[0], 0, 0)),
                pl.BlockSpec((depth, 2 * lanes), lambda i, p: (0, i)),
                pl.BlockSpec(memory_space=pl.ANY),
            ],
            out_specs=pl.BlockSpec((2, 2, depth, lanes), lambda i, p: (i, 0, 0, 0)),
        ),
        out_shape=jax.ShapeDtypeStruct((groups, 2, depth, lanes), F32),
        compiler_params=params(),
        cost_estimate=cost(2 * mixers[0].size * length * (width // cells), field.size),
        name="end_responses",
    )(place, in_hbm(field), mixers, decay_table(length, depth), order)


def jumps_kernel(width, place_ref, ends_ref, ratio_ref, table_ref, order_ref, order_too_ref, out_ref):
    blocks = ends_ref.shape[0]
    here = place_ref[1]
    ratio = ratio_ref[0]
    block_power = power(ratio, width)
    gain = 1.0 / (1.0 - power(block_power, 2 * blocks))

    def end_of(block, side):
        mirrored = block >= blocks
        source = jnp.where(mirrored, 2 * blocks - 1 - block, block)
        return ends_ref[source, jnp.where(mirrored, 1 - side, side)]

    from_left = jnp.zeros_like(ratio)
    from_right = jnp.zeros_like(ratio)
    for k in range(2 * blocks):
        from_left = from_left * block_power + end_of((here + k) % (2 * blocks), 1)
        from_right = from_right * block_power + end_of((here + 2 * blocks - k) % (2 * blocks), 0)
    from_left = from_left * gain
    from_right = from_right * gain
    jump_left = from_left - (ends_ref[here, 0] + from_right * block_power)
    jump_right = (ends_ref[here, 1] + from_left * block_power) - from_right
    jump_left = jnp.where(place_ref[2] == 1, 0.0, (1.0 - ratio) * jump_left)
    jump_right = jnp.where(place_ref[3] == 1, 0.0, (1.0 - ratio) * jump_right)
    for side, jump in enumerate((jump_left, jump_right)):
        levels = jnp.dot(
            table_ref[...], jump, preferred_element_type=F32, precision=lax.Precision.HIGHEST
        )
        for g in range(out_ref.shape[0]):
            out_ref[g, side] = levels


def jumps(all_ends, orders, place, width, groups):
    _, _, depth, lanes = all_ends.shape
    ratio = decay_table(lanes * groups, depth).reshape(depth, groups, lanes).transpose(1, 0, 2)
    out = (groups, 2, depth, lanes)
    return pl.pallas_call(
        functools.partial(jumps_kernel, width),
        grid_spec=pltpu.PrefetchScalarGridSpec(
            num_scalar_prefetch=1,
            grid=(1,),
            in_specs=[
                fixed(all_ends.shape),
                pl.BlockSpec((1, depth, lanes), lambda i, p: (p[0], 0, 0)),
                fixed((depth, depth)),
                pl.BlockSpec(memory_space=pl.ANY),
                pl.BlockSpec(memory_space=pl.ANY),
            ],
            out_specs=fixed(out),
        ),
        out_shape=jax.ShapeDtypeStruct(out, F32),
        compiler_params=params(),
        cost_estimate=cost(20 * all_ends.size, all_ends.size),
        name="jumps",
    )(place, all_ends, ratio, level_table(depth).T.astype(np.float32), *orders)


def border_kernel(rows, place_ref, jump_ref, nu_ref, mu_ref, ends_ref, order_ref, out_ref, *refs):
    c_ref, prefix_ref, source_ref = refs
    _, _, depth, lanes = jump_ref.shape
    levels, width, _ = out_ref.shape
    first = place_ref[0] * (levels - 1) - 1
    aligned = (width // 2) % rows == 0
    for z in range(depth):
        left, right = jump_ref[0, 0, z : z + 1], jump_ref[0, 1, z : z + 1]
        source_ref[0, z] = jnp.broadcast_to(left - right, (8, lanes))
        source_ref[1, z] = jnp.broadcast_to(left + right, (8, lanes))

    def group(i, carry):
        at = pl.ds(pl.multiple_of(i * rows, rows), rows)
        sigma = nu_ref[at, 0:1] + mu_ref[...]
        if aligned:
            parity = (i * rows) // (width // 2)
        else:
            even = i * rows + lax.broadcasted_iota(jnp.int32, (rows, lanes), 0) < width // 2

        def source(z):
            if aligned:
                return jnp.concatenate([source_ref[parity, z]] * (rows // 8), axis=0)
            pair = [jnp.concatenate([source_ref[k, z]] * (rows // 8), axis=0) for k in range(2)]
            return jnp.where(even, *pair)

        zero = sigma * 0.0
        one = zero + 1.0
        c_ref[0], prefix_ref[0] = zero, zero

        def rise(z, state):
            c, slope, prefix = state
            slope = slope + sigma * c
            return c + slope, slope, prefix + c * source(z)

        def first_level(z, state):
            c, _, prefix = state
            c_ref[0], prefix_ref[0] = c, prefix + c * source(z)
            return rise(z, state)

        state = lax.fori_loop(0, first, rise, (one, zero, zero))
        c, slope, prefix = lax.fori_loop(jnp.maximum(first, 0), first + 1, first_level, state)
        for k in range(1, levels):
            prefix = prefix + c * source(first + k)
            slope = slope + sigma * c
            c_ref[k], prefix_ref[k] = c, prefix
            c = c + slope

        def fall(k, state):
            d, slope, suffix = state
            suffix = suffix + d * source(depth - 1 - k)
            slope = slope + sigma * d
            return d + slope, slope, suffix

        above = depth - first - levels
        d, fall_slope, suffix = lax.fori_loop(0, above, fall, (one, one + one, zero))
        top = levels - 1
        scale = slope * d + c_ref[top] * fall_slope
        inverse = pl.reciprocal(scale, approx=True)
        inverse = inverse * (2.0 - scale * inverse)
        inverse = inverse * (2.0 - scale * inverse)
        inverse = inverse * ends_ref[at, 0:1]
        for k in reversed(range(levels)):
            out_ref[k, at] = inverse * (d * prefix_ref[k] + c_ref[k] * suffix)
            if k:
                suffix = suffix + d * source(first + k)
                fall_slope = fall_slope + sigma * d
                d = d + fall_slope
        return carry

    lax.fori_loop(0, width // rows, group, 0)


def border_solve(all_jumps, order, place, width, length, slab):
    groups, _, depth, lanes = all_jumps.shape
    rows = divisor_of(width, 8, 32)
    modes = spectral_order(width)
    nu = eigenvalues(width)[modes][:, None].astype(np.float32)
    mu = eigenvalues(length)[spectral_order(length)][None, :].astype(np.float32)
    ends = cosine_table(width)[modes][:, :1].astype(np.float32)
    return pl.pallas_call(
        functools.partial(border_kernel, rows),
        grid_spec=pltpu.PrefetchScalarGridSpec(
            num_scalar_prefetch=1,
            grid=(groups,),
            in_specs=[
                pl.BlockSpec((1, 2, depth, lanes), lambda i, p: (i, 0, 0, 0)),
                fixed(nu.shape),
                pl.BlockSpec((1, lanes), lambda i, p: (0, i)),
                fixed(ends.shape),
                pl.BlockSpec(memory_space=pl.ANY),
            ],
            out_specs=pl.BlockSpec((slab + 1, width, lanes), lambda i, p: (0, 0, i)),
            scratch_shapes=[pltpu.VMEM((slab + 1, rows, lanes), F32)] * 2
            + [pltpu.VMEM((2, depth, 8, lanes), F32)],
        ),
        out_shape=jax.ShapeDtypeStruct((slab + 1, width, length), F32),
        compiler_params=params(),
        cost_estimate=cost(20 * depth * width * length, (slab + 1) * width * length),
        name="border_solve",
    )(place, all_jumps, nu, mu, ends, order)


def block_dot(high_ref, low_ref, values):
    high, low = split(values)
    if values.shape[0] % 16 == 0:
        table = jnp.concatenate([high_ref[...], high_ref[...], low_ref[...]], axis=1)
        return dot(table, jnp.concatenate([high, low, high], axis=0))
    return dot(high_ref[...], high) + (dot(high_ref[...], low) + dot(low_ref[...], high))


def eliminate_kernel(place_ref, field_ref, ratio_ref, order_ref, high_ref, low_ref, *refs):
    modes_ref, last_ref, outer_ref, weight_ref = refs
    t, steps = pl.program_id(0), pl.num_programs(0)
    modes = block_dot(high_ref, low_ref, field_ref[0])
    modes_ref[0] = modes
    ratio = ratio_ref[0]

    @pl.when(t == 0)
    def _():
        running = ratio * modes
        last_ref[...], outer_ref[...], weight_ref[...] = running, running, ratio

    @pl.when(t > 0)
    def _():
        running = ratio * (modes + last_ref[...])
        last_ref[...] = running

        @pl.when(t < steps - 1)
        def _():
            outer_ref[...] += weight_ref[...] * running
            weight_ref[...] *= ratio


def eliminate(field, ratios, order, place):
    slab, width, length = field.shape
    lanes = length
    high, low = halves_of(cosine_table(width)[spectral_order(width)])
    plane = fixed((width, lanes))
    return pl.pallas_call(
        eliminate_kernel,
        grid_spec=pltpu.PrefetchScalarGridSpec(
            num_scalar_prefetch=1,
            grid=(slab,),
            in_specs=[
                pl.BlockSpec(
                    (1, width, lanes),
                    lambda t, p: (jnp.where(p[4] == 1, slab - 1 - t, t), 0, 0),
                ),
                pl.BlockSpec((1, width, lanes), lambda t, p: (t, 0, 0)),
                pl.BlockSpec(memory_space=pl.ANY),
                fixed(high.shape),
                fixed(low.shape),
            ],
            out_specs=[pl.BlockSpec((1, width, lanes), lambda t, p: (t, 0, 0)), plane, plane],
            scratch_shapes=[pltpu.VMEM((width, lanes), F32)],
        ),
        out_shape=[hbm((slab, width, lanes)), hbm((width, lanes)), hbm((width, lanes))],
        compiler_params=params(32),
        cost_estimate=cost(6 * width * field.size, 3 * field.size),
        name="eliminate",
    )(place, in_hbm(field), in_hbm(ratios), order, high, low)


def substitute_kernel(place_ref, modes_ref, ratio_ref, prev_ratio_ref, in_ref, next_ref, back_ref, border_ref, order_ref, high_ref, low_ref, out_ref, kept):
    slab = modes_ref.shape[0]
    upper = place_ref[4] == 1
    running = in_ref[...]
    for t in range(slab):
        running = ratio_ref[t] * (modes_ref[t] + running)
        kept[t] = running

    def emit(t, values):
        level = jnp.where(upper, slab - t, t + 1)
        out_ref[level] = block_dot(high_ref, low_ref, values + border_ref[level])

    beyond = next_ref[...] + back_ref[...]
    following = beyond
    for t in reversed(range(slab)):
        following = kept[t] + ratio_ref[t] * following
        emit(t, following)
    outside = in_ref[...] + prev_ratio_ref[0] * following
    values = jnp.where(upper, beyond, outside) + border_ref[0]
    out_ref[0] = block_dot(high_ref, low_ref, values)


def substitute(modes, ratios, incoming, following, back, border, order, place):
    slab, width, size = modes.shape
    lanes = divisor_of(size, 128, 384)
    per = size // lanes
    high, low = halves_of(cosine_table(width)[spectral_order(width)].T)
    plane = pl.BlockSpec((width, lanes), lambda i, p: (0, i))
    return pl.pallas_call(
        substitute_kernel,
        grid_spec=pltpu.PrefetchScalarGridSpec(
            num_scalar_prefetch=1,
            grid=(per,),
            in_specs=[
                pl.BlockSpec((slab, width, lanes), lambda i, p: (0, 0, i)),
                pl.BlockSpec((slab, width, lanes), lambda i, p: (0, 0, i)),
                pl.BlockSpec((1, width, lanes), lambda i, p: (slab, 0, i)),
                plane,
                plane,
                plane,
                pl.BlockSpec((slab + 1, width, lanes), lambda i, p: (0, 0, i)),
                pl.BlockSpec(memory_space=pl.ANY),
                fixed(high.shape),
                fixed(low.shape),
            ],
            out_specs=pl.BlockSpec((slab + 1, width, lanes), lambda i, p: (0, 0, i)),
            scratch_shapes=[pltpu.VMEM((slab, width, lanes), F32)],
        ),
        out_shape=hbm((slab + 1, width, size)),
        compiler_params=params(),
        cost_estimate=cost(9 * width * modes.size, 4 * modes.size),
        name="substitute",
    )(
        place, in_hbm(modes), in_hbm(ratios), in_hbm(ratios), incoming, following, back, border,
        order, high, low,
    )


def relay_kernel(last_ref, through_ref, in_ref, order_ref, out_ref):
    through = through_ref[0]
    for t in range(1, through_ref.shape[0]):
        through = through * through_ref[t]
    out_ref[...] = last_ref[...] + through * in_ref[...]


def row_tile(width):
    return divisor_of(width, 8, 48)


def relay(last, ratios, slab, incoming, order, chunk):
    width, lanes = last.shape
    tile = row_tile(width)
    own = pl.BlockSpec((tile, lanes), lambda i: (i, 0))
    return pl.pallas_call(
        relay_kernel,
        grid=(width // tile,),
        in_specs=[
            own,
            pl.BlockSpec((slab, tile, lanes), lambda i: (0, i, chunk)),
            own,
            pl.BlockSpec(memory_space=pl.ANY),
        ],
        out_specs=own,
        out_shape=jax.ShapeDtypeStruct(last.shape, F32),
        compiler_params=params(),
        cost_estimate=cost(2 * last.size, 4 * last.size),
        name="relay",
    )(in_hbm(last), in_hbm(ratios), incoming, order)


def turn_kernel(slab, place_ref, mine_ref, theirs_ref, in_ref, outer_ref, next_ref, ratios_ref, *refs):
    message_ref, follow_ref = refs[-2:]
    innermost = place_ref[5] == 1

    mine, theirs, follow = mine_ref[...], theirs_ref[...], next_ref[...]
    through = ratios_ref[0]
    weight, outer_in = through, through
    for t in range(1, slab):
        ratio = ratios_ref[t]
        through = through * ratio
        if t < slab - 1:
            outer_in = outer_in + weight * through
            weight = weight * ratio
    other = ratios_ref[slab + 1]
    meet = inverted(1.0 - ratio * other)
    inner = jnp.where(innermost, (mine + ratio * theirs) * meet, mine + ratio * follow)
    follow_ref[...] = jnp.where(innermost, (theirs + other * mine) * meet, follow)
    message_ref[...] = outer_ref[...] + outer_in * in_ref[...] + weight * inner


def turn(mine, theirs, incoming, outer, following, ratios, orders, place, chunk):
    width, lanes = mine.shape
    tile = row_tile(width)
    own = pl.BlockSpec((tile, lanes), lambda i, p: (i, 0))
    planes = ratios.shape[0]
    return pl.pallas_call(
        functools.partial(turn_kernel, planes - 2),
        grid_spec=pltpu.PrefetchScalarGridSpec(
            num_scalar_prefetch=1,
            grid=(width // tile,),
            in_specs=[own] * 5
            + [
                pl.BlockSpec((planes, tile, lanes), lambda i, p: (0, i, chunk)),
            ]
            + [pl.BlockSpec(memory_space=pl.ANY)] * len(orders),
            out_specs=[own] * 2,
        ),
        out_shape=[jax.ShapeDtypeStruct(mine.shape, F32), hbm(mine.shape)],
        compiler_params=params(),
        cost_estimate=cost(12 * mine.size, 12 * mine.size),
        name="turn",
    )(place, mine, theirs, incoming, in_hbm(outer), following, in_hbm(ratios), *orders)


def inverted(value):
    guess = pl.reciprocal(value, approx=True)
    guess = guess * (2.0 - value * guess)
    return guess * (2.0 - value * guess)


def sequence(sigma, upper, steps):
    zero = sigma * 0.0
    slope = zero + jnp.where(upper, 2.0, 0.0).astype(F32)

    def advance(_, state):
        value, slope = state
        slope = slope + sigma * value
        return value + slope, slope

    return lax.fori_loop(0, steps, advance, (zero + 1.0, slope))


def ratio_kernel(steps, lanes, place_ref, nu_ref, mu_ref, ratios_ref):
    planes, rows, length = ratios_ref.shape
    slab = planes - 2
    upper, rank = place_ref[4] == 1, place_ref[8]

    def group(i, carry):
        at = pl.ds(pl.multiple_of(i * lanes, lanes), lanes)
        sigma = nu_ref[...] + mu_ref[:, at]
        value, slope = sequence(sigma, upper, rank * slab)
        ratios_ref[slab, :, at] = jnp.where(rank == 0, 0.0, (value - slope) * inverted(value))
        for t in range(slab):
            slope = slope + sigma * value
            following = value + slope
            ratios_ref[t, :, at] = value * inverted(following)
            value = following
        value, slope = sequence(sigma, jnp.logical_not(upper), steps)
        ratios_ref[slab + 1, :, at] = (value - slope) * inverted(value)
        return carry

    lax.fori_loop(0, length // lanes, group, 0)


def pivots(width, length, slab, groups, place):
    rows = divisor_of(width, 8, 32)
    lanes = divisor_of(length, 128, 512)
    nu = eigenvalues(width)[spectral_order(width)][:, None].astype(np.float32)
    mu = eigenvalues(length)[spectral_order(length)][None, :].astype(np.float32)
    return pl.pallas_call(
        functools.partial(ratio_kernel, groups // 2 * slab, lanes),
        grid_spec=pltpu.PrefetchScalarGridSpec(
            num_scalar_prefetch=1,
            grid=(width // rows,),
            in_specs=[pl.BlockSpec((rows, 1), lambda i, p: (i, 0)), fixed(mu.shape)],
            out_specs=pl.BlockSpec((slab + 2, rows, length), lambda i, p: (0, i, 0)),
        ),
        out_shape=hbm((slab + 2, width, length)),
        compiler_params=params(),
        cost_estimate=cost(120 * width * length, 6 * width * length),
        name="ratios",
    )(place, nu, mu)


def cut_kernel(d_top, f_top, d_first, f_first, d_last, f_last, top_ref, fraction_ref, first_ref, last_ref):
    slab = d_first.shape[0]
    top_ref[...] = d_top[...]
    fraction_ref[...] = f_top[...]
    first_ref[:slab] = d_first[:, 0:1]
    first_ref[slab:] = f_first[:, 0:1]
    last_ref[:slab] = d_last[:, 7:8]
    last_ref[slab:] = f_last[:, 7:8]


def cut_borders(direction, fraction):
    slab, width, lanes = direction.shape
    top = pl.BlockSpec((1, width, lanes), lambda i: (slab - 1, 0, 0))
    first = pl.BlockSpec((slab, 8, lanes), lambda i: (0, 0, 0))
    last = pl.BlockSpec((slab, 8, lanes), lambda i: (0, width // 8 - 1, 0))
    shapes = [(1, width, lanes)] * 2 + [(2 * slab, 1, lanes)] * 2
    direction, fraction = in_hbm(direction), in_hbm(fraction)
    return pl.pallas_call(
        cut_kernel,
        grid=(1,),
        in_specs=[top, top, first, first, last, last],
        out_specs=[fixed(shape) for shape in shapes],
        out_shape=[jax.ShapeDtypeStruct(shape, F32) for shape in shapes],
        compiler_params=params(),
        cost_estimate=cost(0, 4 * width * lanes),
        name="cut_borders",
    )(direction, fraction, direction, fraction, direction, fraction)


def neighbours(length):
    up = [(i, i + 1) for i in range(length - 1)]
    return up, [(j, i) for i, j in up]


def twice_inverse(total):
    guess = pl.reciprocal(total, approx=True)
    guess = guess * (2.0 - total * guess)
    return guess + guess


def operator_kernel(n_dots, n_kept, with_levels, place_ref, density_ref, *refs):
    if with_levels:
        (f_low, f_low_prev, f_low_next, f_ref, f_prev, f_next), refs = refs[:6], refs[6:]
    else:
        (f_ref, f_prev, f_next, f_below, f_below_too), refs = refs[:5], refs[5:]
    (f_lo, f_hi, d_ref, d_prev, d_next, d_below, d_lo, d_hi), refs = refs[:8], refs[8:]
    dot_refs = refs[:n_dots]
    face_ref, kept_ref, _, image_ref, out_sums_ref, out_face_ref = refs[n_dots : 6 + n_dots]
    field, dense, before_ref, sums_ref = refs[6 + n_dots :]
    slab, tile, lanes = image_ref.shape
    step, steps = pl.program_id(0), pl.num_programs(0)
    at_left = jnp.logical_and(place_ref[2] == 1, step == 0)
    at_right = jnp.logical_and(place_ref[3] == 1, step == steps - 1)
    at_bottom, at_top = place_ref[6] == 1, place_ref[7] == 1
    liquid, gas = density_ref[0], density_ref[1]

    def mixed(fraction):
        return fraction * gas + (1.0 - fraction) * liquid

    own = slice(8, 8 + tile)
    if with_levels:
        field[0:2, own] = f_low[...]
        field[2:, own] = f_ref[...]
    else:
        field[0:1, own] = f_below[...] + f_below_too[...]
        field[1:, own] = f_ref[...]
    dense[1:, own] = mixed(d_ref[...])
    dense[0:1, own] = mixed(d_below[...])

    @pl.when(step == 0)
    def _():
        field[1:, 7:8] = field[1:, 8:9] + f_lo[...] if with_levels else f_lo[...]
        dense[1:, 7:8] = mixed(d_lo[...])
        sums_ref[...] = jnp.zeros_like(sums_ref)

    @pl.when(step > 0)
    def _():
        if with_levels:
            field[1:2, 7:8] = f_low_prev[1:2, 7:8]
            field[2:, 7:8] = f_prev[:, 7:8]
        else:
            field[1:, 7:8] = f_prev[:, 7:8]
        dense[1:, 7:8] = mixed(d_prev[:, 7:8])

    @pl.when(step == steps - 1)
    def _():
        last_row = field[1:, 7 + tile : 8 + tile]
        field[1:, 8 + tile : 9 + tile] = last_row - f_hi[...] if with_levels else f_hi[...]
        dense[1:, 8 + tile : 9 + tile] = mixed(d_hi[...])

    @pl.when(step < steps - 1)
    def _():
        if with_levels:
            field[1:2, 8 + tile : 9 + tile] = f_low_next[1:2, 0:1]
            field[2:, 8 + tile : 9 + tile] = f_next[:, 0:1]
        else:
            field[1:, 8 + tile : 9 + tile] = f_next[:, 0:1]
        dense[1:, 8 + tile : 9 + tile] = mixed(d_next[:, 0:1])

    lane_ids = lax.broadcasted_iota(jnp.int32, (8, lanes), 1)
    row_ids = lax.broadcasted_iota(jnp.int32, (8, lanes), 0)
    has_right = (lane_ids < lanes - 1).astype(F32)

    def face(mid, rho, neighbour, rho_next):
        return twice_inverse(rho + rho_next) * (mid - neighbour)

    def next_row(ref, z, at, mid):
        following = ref[z, pl.ds(at + 8, 8)]
        return jnp.where(row_ids == 7, pltpu.roll(following, 7, 0), pltpu.roll(mid, 7, 0))

    def face_after(z, at, mid, rho):
        return face(mid, rho, next_row(field, z, at, mid), next_row(dense, z, at, rho))

    for level in range(slab):
        first = face_after(level + 1, 0, field[level + 1, 0:8], dense[level + 1, 0:8])
        before_ref[level] = jnp.where(at_left, 0.0, pltpu.roll(first, 1, 0))

    def rows(i, carry):
        at = pl.multiple_of(8 + 8 * i, 8)
        own = pl.ds(pl.multiple_of(8 * i, 8), 8)
        at_end = jnp.logical_and(at_right, i == tile // 8 - 1)
        mid, rho = field[0, pl.ds(at, 8)], dense[0, pl.ds(at, 8)]
        up, rho_up = field[1, pl.ds(at, 8)], dense[1, pl.ds(at, 8)]
        above = jnp.where(at_bottom, 0.0, face(mid, rho, up, rho_up))
        out_face_ref[0, own] = above
        totals = [mid * above] + [jnp.zeros((8, lanes), F32)] * n_dots
        if n_dots > 1:
            totals[-1] = jnp.where(at_bottom, 0.0, mid * face_ref[0, own])
        for level in range(slab):
            below = above
            mid, rho = up, rho_up
            if level < slab - 1:
                up, rho_up = field[level + 2, pl.ds(at, 8)], dense[level + 2, pl.ds(at, 8)]
                above = face(mid, rho, up, rho_up)
            else:
                above = jnp.where(at_top, twice_inverse(rho) * mid, 0.0)
            after = face_after(level + 1, at, mid, rho)
            after = jnp.where(jnp.logical_and(at_end, row_ids == 7), 0.0, after)
            shifted = pltpu.roll(after, 1, 0)
            before = jnp.where(row_ids == 0, before_ref[level], shifted)
            before_ref[level] = shifted
            right = has_right * face(
                mid, rho, pltpu.roll(mid, lanes - 1, 1), pltpu.roll(rho, lanes - 1, 1)
            )
            image = (above - below) + (after - before) + (right - pltpu.roll(right, 1, 1))
            image_ref[level, own] = image
            totals[0] = totals[0] + mid * image
            for k in range(n_dots):
                totals[k + 1] = totals[k + 1] + mid * dot_refs[k][level, own]
        for k in range(n_dots + 1):
            sums_ref[k] += totals[k]
        return carry

    lax.fori_loop(0, tile // 8, rows, 0)

    @pl.when(step == steps - 1)
    def _():
        group_ids = lax.broadcasted_iota(jnp.int32, (1, 128), 1) // 16
        packed = jnp.where(group_ids < n_kept, kept_ref[0], 0.0)
        for k in range(n_dots + 1):
            line = jnp.sum(sums_ref[k], axis=0, keepdims=True)
            line = sum(line[:, j : j + 128] for j in range(0, lanes, 128))
            for shift in (64, 32, 16):
                line = line + pltpu.roll(line, shift, 1)
            packed = jnp.where(group_ids == n_kept + k, line, packed)
        for k in range(out_sums_ref.shape[0]):
            out_sums_ref[k] = packed


def apply_operator(fields, belows, sides, fraction, border, density, others, face, kept, n_kept, copies, order, place, name):
    slab, width, lanes = fraction.shape
    with_levels = len(fields) > 1
    tile = divisor_of(width, 8, 48)
    per = tile // 8
    last = width // 8 - 1

    def triple(levels):
        return [
            pl.BlockSpec((levels, tile, lanes), lambda i, p: (0, i, 0)),
            pl.BlockSpec((levels, 8, lanes), lambda i, p: (0, jnp.maximum(i * per - 1, 0), 0)),
            pl.BlockSpec((levels, 8, lanes), lambda i, p: (0, jnp.minimum((i + 1) * per, last), 0)),
        ]

    plane = pl.BlockSpec((1, tile, lanes), lambda i, p: (0, i, 0))

    def borders(planes, *places):
        return [plane] * planes + [
            pl.BlockSpec((slab, 1, lanes), lambda i, p, k=k: (k, 0, 0)) for k in places
        ]

    own = pl.BlockSpec((slab, tile, lanes), lambda i, p: (0, i, 0))
    specs = [pl.BlockSpec(memory_space=pltpu.SMEM)]
    for field in fields:
        specs += triple(field.shape[0])
    specs += borders(0, 0, 1) if with_levels else borders(2, 0, 0)
    specs += triple(slab) + borders(1, 1, 1)
    specs += [own] * len(others)
    specs += [plane, fixed((1, 1, 128)), pl.BlockSpec(memory_space=pl.ANY)]
    planes = slab * (3 + len(others)) + 1
    operands = [field for field in fields for _ in range(3)] + ([] if with_levels else list(belows))
    return pl.pallas_call(
        functools.partial(operator_kernel, len(others), n_kept, with_levels),
        grid_spec=pltpu.PrefetchScalarGridSpec(
            num_scalar_prefetch=1,
            grid=(width // tile,),
            in_specs=specs,
            out_specs=[own, fixed((copies, 1, 128)), plane],
            scratch_shapes=[pltpu.VMEM((slab + 1, tile + 16, lanes), F32)] * 2
            + [
                pltpu.VMEM((slab, 8, lanes), F32),
                pltpu.VMEM((len(others) + 1, 8, lanes), F32),
            ],
        ),
        out_shape=[
            jax.ShapeDtypeStruct((slab, width, lanes), F32) if with_levels else hbm((slab, width, lanes)),
            jax.ShapeDtypeStruct((copies, 1, 128), F32),
            hbm((1, width, lanes)),
        ],
        compiler_params=params(28),
        cost_estimate=cost(100 * slab * width * lanes, planes * width * lanes),
        name=name,
    )(
        place, density, *operands, *sides,
        fraction, fraction, fraction, *border, *others, face, kept, order,
    )


def update_kernel(sums_ref, low_ref, high_ref, direction_ref, solution_ref, residual_ref, old_ref, new_ref, old_face_ref, new_face_ref, *refs):
    solution_out, residual_out, direction_out = refs
    slab, _, lanes = direction_ref.shape
    packed = jnp.sum(sums_ref[...], axis=0)
    group_ids = lax.broadcasted_iota(jnp.int32, (1, 128), 1) // 16
    t0, t3, t4, t2, t1 = (
        jnp.broadcast_to(
            jnp.sum(jnp.where(group_ids == k, packed, 0.0), axis=1, keepdims=True), (1, 128)
        )
        for k in range(5)
    )
    t5 = t1
    conjugate = -t1 / t0
    along_r = t2 + conjugate * t3
    curvature = t4 + conjugate * (t1 + t5) + conjugate * conjugate * t0
    step_len = along_r / curvature
    conjugate = jnp.concatenate([conjugate] * (lanes // 128), axis=1)
    step_len = jnp.concatenate([step_len] * (lanes // 128), axis=1)
    for level in range(slab):
        precond = high_ref[level - 1] if level else low_ref[0]
        turned = precond + conjugate * direction_ref[level]
        direction_out[level] = turned
        solution_out[level] = solution_ref[level] + step_len * turned
        image = new_ref[level] + conjugate * old_ref[level]
        if level == slab - 1:
            image = image + (new_face_ref[0] + conjugate * old_face_ref[0])
        residual_out[level] = residual_ref[level] - step_len * image


def update(sums, precond_low, precond_high, direction, solution, residual, image_old, image_new, old_face, new_face):
    slab, width, lanes = direction.shape
    tile = divisor_of(width, 8, 24)
    own = pl.BlockSpec((slab, tile, lanes), lambda i: (0, i, 0))
    return pl.pallas_call(
        update_kernel,
        grid=(width // tile,),
        in_specs=[
            fixed(sums.shape),
            pl.BlockSpec((1, tile, lanes), lambda i: (1, i, 0)),
            pl.BlockSpec((slab - 1, tile, lanes), lambda i: (0, i, 0)),
        ]
        + [own] * 5
        + [pl.BlockSpec((1, tile, lanes), lambda i: (0, i, 0))] * 2,
        out_specs=[own] * 3,
        out_shape=[jax.ShapeDtypeStruct(direction.shape, F32)] * 3,
        compiler_params=params(28),
        cost_estimate=cost(10 * direction.size, 10 * direction.size),
        name="update",
    )(
        sums, precond_low, precond_high, in_hbm(direction), in_hbm(solution), in_hbm(residual),
        in_hbm(image_old), image_new, old_face, new_face,
    )


def body(solution, residual, direction, volume_fraction, density):
    slab, width, length = residual.shape
    groups, plane_parts = lax.axis_size("gz"), lax.axis_size("xy")
    half = groups // 2
    me, here = lax.axis_index("gz"), lax.axis_index("xy")
    upper = me >= half
    rank = jnp.where(upper, groups - 1 - me, me)
    innermost = rank == half - 1
    flags = [me, here, here == 0, here == plane_parts - 1, upper, innermost, me == 0, me == groups - 1]
    place = jnp.stack(flags + [rank]).astype(jnp.int32)
    scale = (2.0 / (1.0 / density[0] + 1.0 / density[1])).reshape(1)

    up, down = neighbours(groups)
    left, right = neighbours(plane_parts)[::-1]
    top, fraction_top, first_rows, last_rows = cut_borders(direction, volume_fraction)
    fraction_below = lax.ppermute(fraction_top, "gz", up)
    below = lax.ppermute(top, "gz", up[1:]) if up[1:] else jnp.zeros_like(top)
    sides = (lax.ppermute(last_rows, "xy", right), lax.ppermute(first_rows, "xy", left))

    spectral = forward_rows(residual.reshape(slab * width, length), scale)
    spectral = spectral.reshape(slab, width, length)
    ratios = pivots(width, length, slab, groups, place)
    inward = [[(s - 1, s), (groups - s, groups - 1 - s)] for s in range(1, half)]
    outward = [[(j, i) for i, j in pairs] for pairs in reversed(inward)]
    across = [(half - 1, half), (half, half - 1)]
    modes, last, outer = eliminate(spectral, ratios, fraction_below, place)
    zero = jnp.zeros_like(last)
    parts = end_responses(spectral, last, place, groups)
    late_top, parts = lax.optimization_barrier((top, parts))
    below_too = lax.ppermute(late_top, "gz", up[:1])
    ends = jnp.sum(lax.all_to_all(parts, "gz", 0, 0, tiled=True), axis=0)
    incoming, mine = zero, last
    for k, pairs in enumerate(inward):
        arrived = lax.ppermute(mine, "gz", pairs)
        incoming = incoming + arrived if k else arrived
        mine = relay(last, ratios, slab, incoming, below, 0)
    ends, mine = lax.optimization_barrier((ends, mine))
    all_ends = lax.all_to_all(
        jnp.broadcast_to(ends[None], (plane_parts,) + ends.shape), "xy", 0, 0, tiled=True
    )
    all_jumps = lax.all_to_all(jumps(all_ends, sides, place, width, groups), "gz", 0, 0, tiled=True)
    theirs = lax.ppermute(mine, "gz", across)
    orders = (below_too, all_jumps)
    message, following = turn(mine, theirs, incoming, outer, zero, ratios, orders, place, 0)
    back = zero
    for k, pairs in enumerate(outward):
        if k:
            message, following = turn(
                mine, theirs, incoming, outer, following + back, ratios, orders, place, 0
            )
        back = lax.ppermute(message, "gz", pairs)

    belows = (below, below_too)
    border = (fraction_below,) + sides
    nothing = jnp.zeros((1, 1, 128), F32)
    image_old, sums_old, old_face = apply_operator(
        [in_hbm(direction)], belows, sides, in_hbm(volume_fraction), border, density,
        [in_hbm(residual)], below, nothing, 0, 1, message, place, "image_old"
    )
    old_above = lax.ppermute(old_face, "gz", down)
    jumped = border_solve(all_jumps, message, place, width, length, slab)
    solved = substitute(modes, ratios, incoming, following, back, jumped, sums_old, place)
    precond_low, precond_high, jump_rows, new_face = inverse_rows(
        solved.reshape((slab + 1) * width, length), all_jumps, fraction_below,
        in_hbm(volume_fraction), density, place, width
    )
    new_above = lax.ppermute(new_face, "gz", down)
    image_new, sums, _ = apply_operator(
        [precond_low, precond_high], belows, (jump_rows, jump_rows),
        in_hbm(volume_fraction), border, density, [in_hbm(residual), in_hbm(image_old)],
        in_hbm(old_face), sums_old, 2, groups * plane_parts, sums_old, place, "image_new"
    )
    gathered = lax.all_to_all(sums, ("gz", "xy"), 0, 0, tiled=True)
    new_solution, new_residual, new_direction = update(
        gathered, precond_low, precond_high, direction, solution, residual, image_old, image_new,
        old_above, new_above
    )
    return (new_solution, new_residual, new_direction)


def solution(mesh):
    placed = P("gz", "xy", None)
    return jax.shard_map(
        body,
        mesh=mesh,
        in_specs=(placed, placed, placed, placed, P()),
        out_specs=(placed, placed, placed),
        check_vma=False,
    )
```

time: 900 us -> 244 us (0.27); the launches traced: 883 us -> 242 us
  matrix products: 213 us -> 0 us
  other arithmetic: 201 us -> 1.56 us
  blocking collectives: 178 us -> 0 us
  Pallas kernels: 0 us -> 142 us
  waiting for transfers between devices: 126 us -> 32.7 us
  local copies, waits for them, and re-layouts: 98 us -> 15.5 us
  loops' own time: 20.7 us -> 0 us
  starting transfers between devices: 38.1 us -> 47.7 us
    dot_general x4 -> x0, matrix products: 213 us -> none  [the longest x1 70.1 us: body(): jnp.einsum('zbjx,bjy->zxy', returned, split_y, precision=HIGHEST_PRECISION)]
    pallas_call x0 -> x15, Pallas kernels: none -> 142 us  [the longest x2 30.7 us: apply_operator(): pl.pallas_call(functools.partial(operator_kernel, len(others), n_kept, wi...]
    all_to_all x2 -> x0, blocking collectives: 115 us -> none  [the longest x1 58.4 us: body(): lax.all_to_all(packed, 'gz', split_axis=2, concat_axis=0, tiled=True)]
    dot_general x2 -> x0, other arithmetic: 74.6 us -> none  [the longest x1 37.3 us: body(): jnp.einsum('zbjx,kbx->zjk', column_data, split_x, precision=HIGHEST_PRECI...]
    dynamic_update_slice x32 -> x0, other arithmetic: 63.7 us -> none  [tridiagonal_solve(): lax.scan(forward_pass, initial_state, (source_terms, column_heights))]
    psum x1 -> x0, blocking collectives: 63.1 us -> none  [body(): totals = lax.psum(local_products, ('gz', 'xy'))]
    all_to_all x2 -> x4, waiting for transfers between devices: 89.4 us -> 27.5 us  [the longest x1 9.86 us: body(): ends = jnp.sum(lax.all_to_all(parts, 'gz', 0, 0, tiled=True), axis=0)]
    reduce_sum x1, other arithmetic: 40 us -> 1.56 us  [body(): ends = jnp.sum(lax.all_to_all(parts, 'gz', 0, 0, tiled=True), axis=0)]
  transfers between devices with their start and end apart: 14 -> 14, of which waited for: 6 -> 6; matrix products, arithmetic and copies ran while one was open for 20% -> 1% of each run, Pallas kernels for 0% -> 49%
where the time goes in v1:
time: 244 us; the launch traced here: 242 us
  Pallas kernels  142 us (58%)
  starting transfers between devices  47.7 us (20%)
  waiting for transfers between devices  32.7 us (13%)
  local copies, waits for them, and re-layouts  15.5 us (6%)
  between operations  2.49 us (1%)
    pallas_call x2, Pallas kernels, apply_operator(): pl.pallas_call(functools.partial(operator_kernel, len(others), n_kept, wi...  30.7 us
    pallas_call x1, Pallas kernels, border_solve(): pl.pallas_call(functools.partial(border_kernel, rows), grid_spec=pltpu.Pr...  14.6 us
    pallas_call x1, Pallas kernels, update(): pl.pallas_call(update_kernel, grid=(width // tile,), in_specs=[fixed(sums...  14.2 us
    unnamed x70, local copies, waits for them, and re-layouts  13.9 us
    pallas_call x1, Pallas kernels, forward_rows(): pl.pallas_call(forward_kernel, grid=(count // tile,), in_specs=[pl.BlockS...  11.7 us
    pallas_call x1, Pallas kernels, inverse_rows(): pl.pallas_call(functools.partial(inverse_kernel, True), grid_spec=pltpu.P...  10.8 us
    all_to_all x1, waiting for transfers between devices, body(): ends = jnp.sum(lax.all_to_all(parts, 'gz', 0, 0, tiled=True), axis=0)  9.86 us
    pallas_call x1, Pallas kernels, inverse_rows(): pl.pallas_call(functools.partial(inverse_kernel, False), grid_spec=pltpu....  9.67 us
  transfers between devices with their start and end apart: 14, of which 6 were waited for; matrix products, arithmetic and copies ran while one was open for 1% of the time, Pallas kernels for 49%

profile of v1, /device:TPU:0, one launch (start us, length us, event | category | flops | bytes accessed | tf_op | source)
XLA Modules:
  0.0 242.3 jit_solution(11882909222869839038)
XLA Ops:
  0.7 3.3 %cut_borders.1 = (f32[1,192,1536]{2,1,0:T(8,128)}, f32[1,192,1536]{2,1,0:T(8,128)}, f32[8,1,1536]{2,1,0:T(1,128)S(1)}, f32[8,1,1536]{2,1,0:T(1,128)S(1)}) custom-call(f32[4,192,1536]{2,1,0:T(8,128)} %direction_ref.1, f32[4,192,1536]{2,1,0:T(8,128)} %refs_10_.1, f32[4,192,1536]{2,1,0:T(8,128)} %direction_ref.1, f32[4,192,1536]{2,1,0:T(8,128)} %refs_10_.1, ...), custom_call_target="tpu_custom_call" | custom-call | bytes 294912 | tf_op jit(solution)/shard_map/cut_borders/pallas_call | solution.py:741
  4.0 4.9 %collective-permute-start = (f32[1,192,1536]{2,1,0:T(8,128)}, f32[1,192,1536]{2,1,0:T(8,128)S(1)}, u32[]{:S(2)}, u32[]{:S(2)}) collective-permute-start(f32[1,192,1536]{2,1,0:T(8,128)} %get-tuple-element.24), channel_id=1, source_target_pairs={{0,8},{8,16},{16,24},{1,9},{9,17},{17,25},{2,10},{10,18},{18,26},{... | collective-permute-start | bytes 3538952 | tf_op jit(solution)/shard_map/ppermute | solution.py:1020
  8.9 0.7 collective-permute-start.2
  11.8 8.2 %ratios.1.ratio_ref.through_ref.ratios_ref.prev_ratio_ref = f32[6,192,1536]{2,1,0:T(8,128)} custom-call(s32[9]{0:T(128)S(1)} %stack.63.place_ref, f32[192,1]{1,0:T(8,128)S(1)} %copy-done.19, f32[1,1536]{1,0:T(1,128)S(1)} %copy-done.28), custom_call_target="tpu_custom_call" | custom-call | flops 2211840 | bytes 442368 | tf_op jit(solution)/shard_map/ratios/pallas_call | solution.py:709
  20.1 11.7 %forward_rows.1 = f32[768,1536]{1,0:T(8,128)} custom-call(f32[1]{0:T(128)S(6)} %div.14.scale_ref, f32[768,1536]{1,0:T(8,128)} %bitcast.26, bf16[2,768,768]{2,1,0:T(8,128)(2,1)} %constant.61.clone.high_ref, bf16[2,768,768]{2,1,0:T(8,128)(2,1)} %constant.62.clone.low_ref, bf16[256,256]{1,0:T(8,128)(2,1)S(1)} %copy-done.7), custom_call_target="tpu_custom_call" | custom-call | flops 339738624 | bytes 589824 | tf_op jit(solution)/shard_map/forward_rows/pallas_call | solution.py:136
  31.8 2.6 %collective-permute-done.order_ref.refs_10_.refs_2_.refs_11_ = f32[1,192,1536]{2,1,0:T(8,128)S(1)} collective-permute-done((f32[1,192,1536]{2,1,0:T(8,128)}, f32[1,192,1536]{2,1,0:T(8,128)S(1)}, u32[]{:S(2)}, u32[]{:S(2)}) %collective-permute-start) | collective-permute-done | bytes 1179680 | tf_op jit(solution)/shard_map/ppermute | solution.py:1020
  34.4 9.4 %eliminate.1 = (f32[4,192,1536]{2,1,0:T(8,128)}, f32[192,1536]{1,0:T(8,128)}, f32[192,1536]{1,0:T(8,128)}) custom-call(s32[9]{0:T(128)S(1)} %stack.63.place_ref, f32[4,192,1536]{2,1,0:T(8,128)} %bitcast.27, f32[6,192,1536]{2,1,0:T(8,128)} %ratios.1.ratio_ref.through_ref.ratios_ref.prev_ratio_ref, ...), custom_call_target="tpu_custom_call" | custom-call | flops 84934656 | bytes 884736 | tf_op jit(solution)/shard_map/eliminate/pallas_call | solution.py:505
  43.8 4.6 %collective-permute-start.1 = (f32[192,1536]{1,0:T(8,128)}, f32[192,1536]{1,0:T(8,128)S(1)}, u32[]{:S(2)}, u32[]{:S(2)}) collective-permute-start(f32[192,1536]{1,0:T(8,128)} %get-tuple-element.26.order_ref.last_ref), channel_id=1, source_target_pairs={{0,8},{24,16},{1,9},{25,17},{2,10},{26,18},{3,11},{27,19},{4,12},{... | collective-permute-start | bytes 3538952 | tf_op jit(solution)/shard_map/ppermute | solution.py:1038
  48.5 1.3 copy-done.6
  49.7 7.4 %end_responses.1 = f32[4,2,16,384]{3,2,1,0:T(8,128)S(1)} custom-call(s32[9]{0:T(128)S(1)} %stack.63.place_ref, f32[4,192,1536]{2,1,0:T(8,128)} %bitcast.28, bf16[4,256,192]{2,1,0:T(8,128)(2,1)S(1)} %copy-done.18, f32[16,1536]{1,0:T(8,128)S(1)} %copy-done.27, f32[192,1536]{1,0:T(8,128)S(1)} %copy-done.6), custom_call_target="tpu_custom_call" | custom-call | flops 113246208 | bytes 294912 | tf_op jit(solution)/shard_map/end_responses/pallas_call | solution.py:291
  57.1 0.7 copy-done.11
  57.8 4.5 %all-to-all-start = ((f32[4,2,16,384]{3,2,1,0:T(8,128)}), f32[4,2,16,384]{3,2,1,0:T(8,128)}, u32[]{:S(2)}, u32[]{:S(2)}) async-start(f32[4,2,16,384]{3,2,1,0:T(8,128)} %copy-done.11), calls=%async_computation | async-start | bytes 393216 | tf_op jit(solution)/shard_map/all_to_all | solution.py:1035
  62.3 5.0 %collective-permute-start.4 = (f32[1,192,1536]{2,1,0:T(8,128)}, f32[1,192,1536]{2,1,0:T(8,128)}, u32[]{:S(2)}, u32[]{:S(2)}) collective-permute-start(f32[1,192,1536]{2,1,0:T(8,128)} %get-tuple-element.31), channel_id=1, source_target_pairs={{0,8},{1,9},{2,10},{3,11},{4,12},{5,13},{6,14},{7,15}} | collective-permute-start | bytes 3538952 | tf_op jit(solution)/shard_map/ppermute | solution.py:1034
  67.3 9.9 %all-to-all-done = f32[4,2,16,384]{3,2,1,0:T(8,128)} async-done(((f32[4,2,16,384]{3,2,1,0:T(8,128)}), f32[4,2,16,384]{3,2,1,0:T(8,128)}, u32[]{:S(2)}, u32[]{:S(2)}) %all-to-all-start) | async-done | bytes 196640 | tf_op jit(solution)/shard_map/all_to_all | solution.py:1035
  77.2 1.6 reduce_sum.9
  78.8 4.4 %relay.1.mine_ref = f32[192,1536]{1,0:T(8,128)} custom-call(f32[192,1536]{1,0:T(8,128)} %get-tuple-element.26.order_ref.last_ref, f32[6,192,1536]{2,1,0:T(8,128)} %ratios.1.ratio_ref.through_ref.ratios_ref.prev_ratio_ref, f32[192,1536]{1,0:T(8,128)S(1)} %collective-permute-done.1.in_ref, f32[1,192,1536]{2,1,0:T(8,128)S(1)} %collective-permute-done.2.order_ref.refs_3_.refs_14_), custom_call_target="tpu_custom_call" | custom-call | flops 36864 | bytes 294912 | tf_op jit(solution)/shard_map/relay/pallas_call | solution.py:603
  83.2 1.7 collective-permute-start.3
  84.9 0.8 broadcast_in_dim.13
  85.7 4.9 %all-to-all-start.1 = ((f32[8,2,16,384]{3,2,1,0:T(8,128)}), f32[8,2,16,384]{3,2,1,0:T(8,128)}, u32[]{:S(2)}, u32[]{:S(2)}) async-start(f32[8,2,16,384]{3,2,1,0:T(8,128)} %broadcast_in_dim.13), calls=%async_computation.1 | async-start | bytes 786432 | tf_op jit(solution)/shard_map/all_to_all | solution.py:1042
  90.5 2.4 collective-permute-start.5
  92.9 1.3 collective-permute-start.6
  94.9 2.5 %collective-permute-done.6.order_too_ref.refs_6_.refs_12_.refs_13_ = f32[8,1,1536]{2,1,0:T(1,128)S(1)} collective-permute-done((f32[8,1,1536]{2,1,0:T(1,128)}, f32[8,1,1536]{2,1,0:T(1,128)S(1)}, u32[]{:S(2)}, u32[]{:S(2)}) %collective-permute-start.6) | collective-permute-done | bytes 49184 | tf_op jit(solution)/shard_map/ppermute | solution.py:1022
  97.4 0.6 copy-done.15
  98.0 5.2 %all-to-all-done.1.ends_ref = f32[8,2,16,384]{3,2,1,0:T(8,128)} async-done(((f32[8,2,16,384]{3,2,1,0:T(8,128)}), f32[8,2,16,384]{3,2,1,0:T(8,128)}, u32[]{:S(2)}, u32[]{:S(2)}) %all-to-all-start.1) | async-done | bytes 393248 | tf_op jit(solution)/shard_map/all_to_all | solution.py:1042
  103.2 0.8 copy-done.13
  104.0 0.8 copy-done.16
  104.8 0.9 copy-done.26
  105.7 0.7 copy-done.31
  106.4 1.8 jumps.1
  108.2 0.7 copy-done.10
  108.9 4.7 %all-to-all-start.2 = ((f32[4,2,16,384]{3,2,1,0:T(8,128)}), f32[4,2,16,384]{3,2,1,0:T(8,128)}, u32[]{:S(2)}, u32[]{:S(2)}) async-start(f32[4,2,16,384]{3,2,1,0:T(8,128)} %copy-done.10), calls=%async_computation.2 | async-start | bytes 393216 | tf_op jit(solution)/shard_map/all_to_all | solution.py:1045
  113.6 5.4 %all-to-all-done.2.refs_1_.jump_ref.refs_0_ = f32[4,2,16,384]{3,2,1,0:T(8,128)} async-done(((f32[4,2,16,384]{3,2,1,0:T(8,128)}), f32[4,2,16,384]{3,2,1,0:T(8,128)}, u32[]{:S(2)}, u32[]{:S(2)}) %all-to-all-start.2) | async-done | bytes 196640 | tf_op jit(solution)/shard_map/all_to_all | solution.py:1045
  119.1 6.3 %turn.1 = (f32[192,1536]{1,0:T(8,128)S(1)}, f32[192,1536]{1,0:T(8,128)}) custom-call(s32[9]{0:T(128)S(1)} %stack.63.place_ref, f32[192,1536]{1,0:T(8,128)} %relay.1.mine_ref, f32[192,1536]{1,0:T(8,128)} %collective-permute-done.3.theirs_ref, f32[192,1536]{1,0:T(8,128)S(1)} %collective-permute-done.1.in_ref, f32[192,1536]{1,0:T(8,128)} %get-tuple-element.30.outer_ref, ...), custom_call_target="tpu_custom_call" | custom-call | flops 221184 | bytes 884736 | tf_op jit(solution)/shard_map/turn/pallas_call | solution.py:645
  125.4 1.3 collective-permute-start.7
  126.8 15.1 %image_old.1 = (f32[4,192,1536]{2,1,0:T(8,128)}, f32[1,1,128]{2,1,0:T(1,128)S(1)}, f32[1,192,1536]{2,1,0:T(8,128)}) custom-call(s32[9]{0:T(128)S(1)} %stack.63.place_ref, f32[2]{0:T(128)S(1)} %copy-done.29, f32[4,192,1536]{2,1,0:T(8,128)} %direction_ref.1, f32[4,192,1536]{2,1,0:T(8,128)} %direction_ref.1, f32[4,192,1536]{2,1,0:T(8,128)} %direction_ref.1, ...), custom_call_target="tpu_custom_call" | custom-call | flops 7372800 | bytes 1253376 | tf_op jit(solution)/shard_map/image_old/pallas_call | solution.py:924
  141.9 1.6 collective-permute-start.8
  143.5 14.6 %border_solve.1.border_ref = f32[5,192,1536]{2,1,0:T(8,128)S(1)} custom-call(s32[9]{0:T(128)S(1)} %stack.63.place_ref, f32[4,2,16,384]{3,2,1,0:T(8,128)} %all-to-all-done.2.refs_1_.jump_ref.refs_0_, f32[192,1]{1,0:T(8,128)S(1)} %copy-done.20, f32[1,1536]{1,0:T(1,128)S(1)} %copy-done.28, f32[192,1]{1,0:T(8,128)S(1)} %copy-done.23, ...), custom_call_target="tpu_custom_call" | custom-call | flops 5898240 | bytes 368640 | tf_op jit(solution)/shard_map/border_solve/pallas_call | solution.py:446
  158.2 9.7 %substitute.1 = f32[5,192,1536]{2,1,0:T(8,128)} custom-call(s32[9]{0:T(128)S(1)} %stack.63.place_ref, f32[4,192,1536]{2,1,0:T(8,128)} %get-tuple-element.25.modes_ref, f32[6,192,1536]{2,1,0:T(8,128)} %ratios.1.ratio_ref.through_ref.ratios_ref.prev_ratio_ref, f32[6,192,1536]{2,1,0:T(8,128)} %ratios.1.ratio_ref.through_ref.ratios_ref.prev_ratio_ref, ...), custom_call_target="tpu_custom_call" | custom-call | flops 127401984 | bytes 1179648 | tf_op jit(solution)/shard_map/substitute/pallas_call | solution.py:558
  167.9 10.8 %inverse_lower.1 = (f32[384,1536]{1,0:T(8,128)S(1)}, f32[8,1,1536]{2,1,0:T(1,128)S(1)}, f32[1,192,1536]{2,1,0:T(8,128)}) custom-call(s32[9]{0:T(128)S(1)} %stack.63.place_ref, f32[2]{0:T(128)S(1)} %copy-done.29, f32[960,1536]{1,0:T(8,128)} %bitcast.22, f32[960,1536]{1,0:T(8,128)} %bitcast.23, bf16[2,768,768]{2,1,0:T(8,128)(2,1)} %constant.75.clone.high_ref, ...), custom_call_target="tpu_custom_call" | custom-call | flops 198180864 | bytes 294912 | tf_op jit(solution)/shard_map/inverse_lower/pallas_call | solution.py:204
  178.7 1.6 collective-permute-start.9
  180.3 9.7 %inverse_upper.1 = f32[576,1536]{1,0:T(8,128)S(1)} custom-call(s32[9]{0:T(128)S(1)} %stack.63.place_ref, f32[2]{0:T(128)S(1)} %copy-done.29, f32[960,1536]{1,0:T(8,128)} %bitcast.24, f32[960,1536]{1,0:T(8,128)} %bitcast.25, bf16[2,768,768]{2,1,0:T(8,128)(2,1)} %constant.75.clone.high_ref, bf16[2,768,768]{2,1,0:T(8,128)(2,1)} %constant.76.clone.low_ref, ...), custom_call_target="tpu_custom_call" | custom-call | flops 297271296 | bytes 442368 | tf_op jit(solution)/shard_map/inverse_upper/pallas_call | solution.py:227
  190.0 15.6 %image_new.1 = (f32[4,192,1536]{2,1,0:T(8,128)S(1)}, f32[32,1,128]{2,1,0:T(1,128)S(1)}, f32[1,192,1536]{2,1,0:T(8,128)}) custom-call(s32[9]{0:T(128)S(1)} %stack.63.place_ref, f32[2]{0:T(128)S(1)} %copy-done.29, f32[2,192,1536]{2,1,0:T(8,128)S(1)} %bitcast.18, f32[2,192,1536]{2,1,0:T(8,128)S(1)} %bitcast.19, f32[2,192,1536]{2,1,0:T(8,128)S(1)} %bitcast.20, ...), custom_call_target="tpu_custom_call" | custom-call | flops 7372800 | bytes 1548288 | tf_op jit(solution)/shard_map/image_new/pallas_call | solution.py:924
  205.6 2.2 copy-done.4
  208.4 8.6 %all-to-all-start.3 = ((f32[32,1,128]{2,1,0:T(1,128)}), f32[32,1,128]{2,1,0:T(1,128)S(1)}, u32[]{:S(2)}, u32[]{:S(2)}) async-start(f32[32,1,128]{2,1,0:T(1,128)} %copy-done.30), calls=%async_computation.3 | async-start | bytes 32768 | tf_op jit(solution)/shard_map/all_to_all | solution.py:1077
  217.0 7.1 %all-to-all-done.3.sums_ref = f32[32,1,128]{2,1,0:T(1,128)S(1)} async-done(((f32[32,1,128]{2,1,0:T(1,128)}), f32[32,1,128]{2,1,0:T(1,128)S(1)}, u32[]{:S(2)}, u32[]{:S(2)}) %all-to-all-start.3) | async-done | bytes 16416 | tf_op jit(solution)/shard_map/all_to_all | solution.py:1077
  224.1 1.7 copy-done.1
  225.8 2.3 copy-done.5
  228.1 14.2 %update.1 = (f32[4,192,1536]{2,1,0:T(8,128)}, f32[4,192,1536]{2,1,0:T(8,128)}, f32[4,192,1536]{2,1,0:T(8,128)}) custom-call(f32[32,1,128]{2,1,0:T(1,128)S(1)} %all-to-all-done.3.sums_ref, f32[2,192,1536]{2,1,0:T(8,128)S(1)} %bitcast.21, f32[3,192,1536]{2,1,0:T(8,128)S(1)} %bitcast.17, f32[4,192,1536]{2,1,0:T(8,128)} %direction_ref.1, ...), custom_call_target="tpu_custom_call" | custom-call | flops 737280 | bytes 2949120 | tf_op jit(solution)/shard_map/update/pallas_call | solution.py:984
  (71 shorter events, 2.2 us)
Async XLA Ops:
  0.6 11.2 %copy-start.19 = (f32[192,1]{1,0:T(8,128)S(1)}, f32[192,1]{1,0:T(8,128)}, u32[]{:S(2)}) copy-start(f32[192,1]{1,0:T(8,128)} %constant.64.clone.nu_ref) | copy-start | bytes 2308
  0.6 11.2 %copy-start.28 = (f32[1,1536]{1,0:T(1,128)S(1)}, f32[1,1536]{1,0:T(1,128)}, u32[]{:S(2)}) copy-start(f32[1,1536]{1,0:T(1,128)} %constant.65.clone.mu_ref) | copy-start | bytes 18436
  0.7 9.0 %copy-start.29 = (f32[2]{0:T(128)S(1)}, f32[2]{0:T(128)}, u32[]{:S(2)}) copy-start(f32[2]{0:T(128)} %density_ref.7) | copy-start | bytes 28
  4.0 4.9 %copy-start.32 = (f32[8,1,1536]{2,1,0:T(1,128)}, f32[8,1,1536]{2,1,0:T(1,128)S(1)}, u32[]{:S(2)}) copy-start(f32[8,1,1536]{2,1,0:T(1,128)S(1)} %get-tuple-element.34) | copy-start | bytes 147460
  4.0 16.1 %copy-start.33 = (f32[8,1,1536]{2,1,0:T(1,128)}, f32[8,1,1536]{2,1,0:T(1,128)S(1)}, u32[]{:S(2)}) copy-start(f32[8,1,1536]{2,1,0:T(1,128)S(1)} %get-tuple-element.33) | copy-start | bytes 147460
  4.0 30.4 %collective-permute-start = (f32[1,192,1536]{2,1,0:T(8,128)}, f32[1,192,1536]{2,1,0:T(8,128)S(1)}, u32[]{:S(2)}, u32[]{:S(2)}) collective-permute-start(f32[1,192,1536]{2,1,0:T(8,128)} %get-tuple-element.24), channel_id=1, source_target_pairs={{0,8},{8,16},{16,24},{1,9},{9,17},{17,25},{2,10},{10,18},{18,26},{... | collective-permute-start | bytes 3538952 | tf_op jit(solution)/shard_map/ppermute | solution.py:1020
  8.9 69.8 %collective-permute-start.2 = (f32[1,192,1536]{2,1,0:T(8,128)}, f32[1,192,1536]{2,1,0:T(8,128)S(1)}, u32[]{:S(2)}, u32[]{:S(2)}) collective-permute-start(f32[1,192,1536]{2,1,0:T(8,128)} %get-tuple-element.31), channel_id=1, source_target_pairs={{8,16},{16,24},{9,17},{17,25},{10,18},{18,26},{11,19},{19,27},{12,... | collective-permute-start | bytes 3538952 | tf_op jit(solution)/shard_map/ppermute | solution.py:1021
  11.8 8.3 %copy-start.7 = (bf16[256,256]{1,0:T(8,128)(2,1)S(1)}, bf16[256,256]{1,0:T(8,128)(2,1)}, u32[]{:S(2)}) copy-start(bf16[256,256]{1,0:T(8,128)(2,1)} %constant.63.clone.flip_ref) | copy-start | bytes 393220
  20.1 14.3 %copy-start.24 = (bf16[192,192]{1,0:T(8,128)(2,1)S(1)}, bf16[192,192]{1,0:T(8,128)(2,1)}, u32[]{:S(2)}) copy-start(bf16[192,192]{1,0:T(8,128)(2,1)} %constant.66.clone.high_ref) | copy-start | bytes 221188
  20.1 14.3 %copy-start.25 = (bf16[192,192]{1,0:T(8,128)(2,1)S(1)}, bf16[192,192]{1,0:T(8,128)(2,1)}, u32[]{:S(2)}) copy-start(bf16[192,192]{1,0:T(8,128)(2,1)} %constant.67.clone.low_ref) | copy-start | bytes 221188
  34.4 133.5 %copy-start.2 = (f32[1,192,1536]{2,1,0:T(8,128)}, f32[1,192,1536]{2,1,0:T(8,128)S(1)}, u32[]{:S(2)}) copy-start(f32[1,192,1536]{2,1,0:T(8,128)S(1)} %collective-permute-done.order_ref.refs_10_.refs_2_.refs_11_) | copy-start | bytes 3538948
  34.4 14.1 %copy-start.18 = (bf16[4,256,192]{2,1,0:T(8,128)(2,1)S(1)}, bf16[4,256,192]{2,1,0:T(8,128)(2,1)}, u32[]{:S(2)}) copy-start(bf16[4,256,192]{2,1,0:T(8,128)(2,1)} %constant.68.clone.mixer_ref) | copy-start | bytes 1179652
  34.4 14.1 %copy-start.27 = (f32[16,1536]{1,0:T(8,128)S(1)}, f32[16,1536]{1,0:T(8,128)}, u32[]{:S(2)}) copy-start(f32[16,1536]{1,0:T(8,128)} %constant.69.clone.ratio_ref) | copy-start | bytes 294916
  43.8 34.9 %collective-permute-start.1 = (f32[192,1536]{1,0:T(8,128)}, f32[192,1536]{1,0:T(8,128)S(1)}, u32[]{:S(2)}, u32[]{:S(2)}) collective-permute-start(f32[192,1536]{1,0:T(8,128)} %get-tuple-element.26.order_ref.last_ref), channel_id=1, source_target_pairs={{0,8},{24,16},{1,9},{25,17},{2,10},{26,18},{3,11},{27,19},{4,12},{... | collective-permute-start | bytes 3538952 | tf_op jit(solution)/shard_map/ppermute | solution.py:1038
  48.5 1.3 copy-start.6
  57.1 0.7 copy-start.11
  57.8 19.4 %all-to-all-start = ((f32[4,2,16,384]{3,2,1,0:T(8,128)}), f32[4,2,16,384]{3,2,1,0:T(8,128)}, u32[]{:S(2)}, u32[]{:S(2)}) async-start(f32[4,2,16,384]{3,2,1,0:T(8,128)} %copy-done.11), calls=%async_computation | async-start | bytes 393216 | tf_op jit(solution)/shard_map/all_to_all | solution.py:1035
  62.3 51.3 %collective-permute-start.4 = (f32[1,192,1536]{2,1,0:T(8,128)}, f32[1,192,1536]{2,1,0:T(8,128)}, u32[]{:S(2)}, u32[]{:S(2)}) collective-permute-start(f32[1,192,1536]{2,1,0:T(8,128)} %get-tuple-element.31), channel_id=1, source_target_pairs={{0,8},{1,9},{2,10},{3,11},{4,12},{5,13},{6,14},{7,15}} | collective-permute-start | bytes 3538952 | tf_op jit(solution)/shard_map/ppermute | solution.py:1034
  78.8 6.1 %copy-start.34 = (f32[2,16,384]{2,1,0:T(8,128)S(1)}, f32[2,16,384]{2,1,0:T(8,128)}, u32[]{:S(2)}) copy-start(f32[2,16,384]{2,1,0:T(8,128)} %reduce_sum.9) | copy-start | bytes 147460
  83.2 35.8 %collective-permute-start.3 = (f32[192,1536]{1,0:T(8,128)}, f32[192,1536]{1,0:T(8,128)}, u32[]{:S(2)}, u32[]{:S(2)}) collective-permute-start(f32[192,1536]{1,0:T(8,128)} %relay.1.mine_ref), channel_id=1, source_target_pairs={{8,16},{16,8},{9,17},{17,9},{10,18},{18,10},{11,19},{19,11},{12,20... | collective-permute-start | bytes 3538952 | tf_op jit(solution)/shard_map/ppermute | solution.py:1046
  85.7 17.5 %all-to-all-start.1 = ((f32[8,2,16,384]{3,2,1,0:T(8,128)}), f32[8,2,16,384]{3,2,1,0:T(8,128)}, u32[]{:S(2)}, u32[]{:S(2)}) async-start(f32[8,2,16,384]{3,2,1,0:T(8,128)} %broadcast_in_dim.13), calls=%async_computation.1 | async-start | bytes 786432 | tf_op jit(solution)/shard_map/all_to_all | solution.py:1042
  90.5 3.7 %collective-permute-start.5 = (f32[8,1,1536]{2,1,0:T(1,128)}, f32[8,1,1536]{2,1,0:T(1,128)S(1)}, u32[]{:S(2)}, u32[]{:S(2)}) collective-permute-start(f32[8,1,1536]{2,1,0:T(1,128)} %copy-done.33), channel_id=1, source_target_pairs={{0,1},{1,2},{2,3},{3,4},{4,5},{5,6},{6,7},{8,9},{9,10},{10,11},{11... | collective-permute-start | bytes 147464 | tf_op jit(solution)/shard_map/ppermute | solution.py:1022
  92.9 4.5 %collective-permute-start.6 = (f32[8,1,1536]{2,1,0:T(1,128)}, f32[8,1,1536]{2,1,0:T(1,128)S(1)}, u32[]{:S(2)}, u32[]{:S(2)}) collective-permute-start(f32[8,1,1536]{2,1,0:T(1,128)} %copy-done.32), channel_id=1, source_target_pairs={{1,0},{2,1},{3,2},{4,3},{5,4},{6,5},{7,6},{9,8},{10,9},{11,10},{12... | collective-permute-start | bytes 147464 | tf_op jit(solution)/shard_map/ppermute | solution.py:1022
  94.3 0.6 copy-start.12
  97.4 0.6 copy-start.15
  103.2 0.8 copy-start.13
  104.0 0.8 copy-start.16
  104.8 0.9 copy-start.26
  105.7 0.7 copy-start.31
  108.2 0.7 copy-start.10
  108.9 10.0 %all-to-all-start.2 = ((f32[4,2,16,384]{3,2,1,0:T(8,128)}), f32[4,2,16,384]{3,2,1,0:T(8,128)}, u32[]{:S(2)}, u32[]{:S(2)}) async-start(f32[4,2,16,384]{3,2,1,0:T(8,128)} %copy-done.10), calls=%async_computation.2 | async-start | bytes 393216 | tf_op jit(solution)/shard_map/all_to_all | solution.py:1045
  119.1 7.7 %copy-start.14 = (f32[8,1,1536]{2,1,0:T(1,128)S(1)}, f32[8,1,1536]{2,1,0:T(1,128)}, u32[]{:S(2)}) copy-start(f32[8,1,1536]{2,1,0:T(1,128)} %copy-done.12) | copy-start | bytes 147460
  119.1 7.7 %copy-start.17 = (f32[8,1,1536]{2,1,0:T(1,128)S(1)}, f32[8,1,1536]{2,1,0:T(1,128)}, u32[]{:S(2)}) copy-start(f32[8,1,1536]{2,1,0:T(1,128)} %copy-done.15) | copy-start | bytes 147460
  125.4 32.7 %collective-permute-start.7 = (f32[192,1536]{1,0:T(8,128)S(1)}, f32[192,1536]{1,0:T(8,128)S(1)}, u32[]{:S(2)}, u32[]{:S(2)}) collective-permute-start(f32[192,1536]{1,0:T(8,128)S(1)} %get-tuple-element.36.order_ref.refs_16_), channel_id=1, source_target_pairs={{8,0},{16,24},{9,1},{17,25},{10,2},{18,26},{11,3},{19,27},{12,4},{... | collective-permute-start | bytes 3538952 | tf_op jit(solution)/shard_map/ppermute | solution.py:1055
  126.8 16.7 %copy-start.20 = (f32[192,1]{1,0:T(8,128)S(1)}, f32[192,1]{1,0:T(8,128)}, u32[]{:S(2)}) copy-start(f32[192,1]{1,0:T(8,128)} %constant.64.clone.nu_ref) | copy-start | bytes 2308
  126.8 16.7 %copy-start.23 = (f32[192,1]{1,0:T(8,128)S(1)}, f32[192,1]{1,0:T(8,128)}, u32[]{:S(2)}) copy-start(f32[192,1]{1,0:T(8,128)} %constant.72.clone.ends_ref) | copy-start | bytes 2308
  141.8 16.3 %copy-start.9 = (f32[192,1536]{1,0:T(8,128)S(1)}, f32[192,1536]{1,0:T(8,128)}, u32[]{:S(2)}) copy-start(f32[192,1536]{1,0:T(8,128)} %get-tuple-element.35.next_ref) | copy-start | bytes 3538948
  141.9 16.3 %copy-start.21 = (bf16[192,192]{1,0:T(8,128)(2,1)S(1)}, bf16[192,192]{1,0:T(8,128)(2,1)}, u32[]{:S(2)}) copy-start(bf16[192,192]{1,0:T(8,128)(2,1)} %constant.73.clone.high_ref) | copy-start | bytes 221188
  141.9 16.3 %copy-start.22 = (bf16[192,192]{1,0:T(8,128)(2,1)S(1)}, bf16[192,192]{1,0:T(8,128)(2,1)}, u32[]{:S(2)}) copy-start(bf16[192,192]{1,0:T(8,128)(2,1)} %constant.74.clone.low_ref) | copy-start | bytes 221188
  141.9 75.1 %collective-permute-start.8 = (f32[1,192,1536]{2,1,0:T(8,128)}, f32[1,192,1536]{2,1,0:T(8,128)}, u32[]{:S(2)}, u32[]{:S(2)}) collective-permute-start(f32[1,192,1536]{2,1,0:T(8,128)} %get-tuple-element.41.refs_16_), channel_id=1, source_target_pairs={{8,0},{16,8},{24,16},{9,1},{17,9},{25,17},{10,2},{18,10},{26,18},{... | collective-permute-start | bytes 3538952 | tf_op jit(solution)/shard_map/ppermute | solution.py:1064
  158.2 9.7 %copy-start.8 = (bf16[256,256]{1,0:T(8,128)(2,1)S(1)}, bf16[256,256]{1,0:T(8,128)(2,1)}, u32[]{:S(2)}) copy-start(bf16[256,256]{1,0:T(8,128)(2,1)} %constant.63.clone.flip_ref) | copy-start | bytes 393220
  178.7 11.3 %copy-start = (f32[384,1536]{1,0:T(8,128)}, f32[384,1536]{1,0:T(8,128)S(1)}, u32[]{:S(2)}) copy-start(f32[384,1536]{1,0:T(8,128)S(1)} %get-tuple-element.38) | copy-start | bytes 7077892
  178.7 11.3 %copy-start.3 = (f32[1,192,1536]{2,1,0:T(8,128)S(1)}, f32[1,192,1536]{2,1,0:T(8,128)}, u32[]{:S(2)}) copy-start(f32[1,192,1536]{2,1,0:T(8,128)} %copy-done.2) | copy-start | bytes 3538948
  178.7 45.4 %collective-permute-start.9 = (f32[1,192,1536]{2,1,0:T(8,128)}, f32[1,192,1536]{2,1,0:T(8,128)}, u32[]{:S(2)}, u32[]{:S(2)}) collective-permute-start(f32[1,192,1536]{2,1,0:T(8,128)} %get-tuple-element.44), channel_id=1, source_target_pairs={{8,0},{16,8},{24,16},{9,1},{17,9},{25,17},{10,2},{18,10},{26,18},{... | collective-permute-start | bytes 3538952 | tf_op jit(solution)/shard_map/ppermute | solution.py:1071
  205.6 2.2 copy-start.4
  208.4 15.7 %all-to-all-start.3 = ((f32[32,1,128]{2,1,0:T(1,128)}), f32[32,1,128]{2,1,0:T(1,128)S(1)}, u32[]{:S(2)}, u32[]{:S(2)}) async-start(f32[32,1,128]{2,1,0:T(1,128)} %copy-done.30), calls=%async_computation.3 | async-start | bytes 32768 | tf_op jit(solution)/shard_map/all_to_all | solution.py:1077
  224.1 1.7 copy-start.1
  225.8 2.3 copy-start.5
  (1 other events, 0.6 us)

commit v2 on v1

--- a/solution.py
+++ b/solution.py
@@ -210,7 +210,7 @@
             out_specs=[fixed((2 * width, 2 * half)), fixed((2 * slab, 1, 2 * half)), plane],
         ),
         out_shape=[
-            jax.ShapeDtypeStruct((2 * width, 2 * half), F32),
+            hbm((2 * width, 2 * half)),
             jax.ShapeDtypeStruct((2 * slab, 1, 2 * half), F32),
             jax.ShapeDtypeStruct((1, width, 2 * half), F32),
         ],
@@ -232,7 +232,7 @@
             in_specs=[smem] + rows + tables,
             out_specs=pl.BlockSpec((tile, 2 * half), lambda i, p: (i, 0)),
         ),
-        out_shape=jax.ShapeDtypeStruct((rest, 2 * half), F32),
+        out_shape=hbm((rest, 2 * half)),
         compiler_params=params(36),
         cost_estimate=cost(14 * rest * half * half, 4 * rest * half),
         name="inverse_upper",
@@ -368,14 +368,13 @@
     c_ref, prefix_ref, source_ref = refs
     _, _, depth, lanes = jump_ref.shape
     levels, width, _ = out_ref.shape
-    first = place_ref[0] * (levels - 1) - 1
     aligned = (width // 2) % rows == 0
     for z in range(depth):
         left, right = jump_ref[0, 0, z : z + 1], jump_ref[0, 1, z : z + 1]
         source_ref[0, z] = jnp.broadcast_to(left - right, (8, lanes))
         source_ref[1, z] = jnp.broadcast_to(left + right, (8, lanes))
 
-    def group(i, carry):
+    def group(first, i, carry):
         at = pl.ds(pl.multiple_of(i * rows, rows), rows)
         sigma = nu_ref[at, 0:1] + mu_ref[...]
         if aligned:
@@ -391,54 +390,41 @@
 
         zero = sigma * 0.0
         one = zero + 1.0
-        c_ref[0], prefix_ref[0] = zero, zero
-
-        def rise(z, state):
-            c, slope, prefix = state
+        if first < 0:
+            c_ref[0], prefix_ref[0] = zero, zero
+        c, slope, prefix = one, zero, zero
+        for z in range(first + levels):
+            prefix = prefix + c * source(z)
             slope = slope + sigma * c
-            return c + slope, slope, prefix + c * source(z)
-
-        def first_level(z, state):
-            c, _, prefix = state
-            c_ref[0], prefix_ref[0] = c, prefix + c * source(z)
-            return rise(z, state)
-
-        state = lax.fori_loop(0, first, rise, (one, zero, zero))
-        c, slope, prefix = lax.fori_loop(jnp.maximum(first, 0), first + 1, first_level, state)
-        for k in range(1, levels):
-            prefix = prefix + c * source(first + k)
-            slope = slope + sigma * c
-            c_ref[k], prefix_ref[k] = c, prefix
+            if z >= first:
+                c_ref[z - first], prefix_ref[z - first] = c, prefix
             c = c + slope
-
-        def fall(k, state):
-            d, slope, suffix = state
-            suffix = suffix + d * source(depth - 1 - k)
-            slope = slope + sigma * d
-            return d + slope, slope, suffix
-
-        above = depth - first - levels
-        d, fall_slope, suffix = lax.fori_loop(0, above, fall, (one, one + one, zero))
-        top = levels - 1
-        scale = slope * d + c_ref[top] * fall_slope
-        inverse = pl.reciprocal(scale, approx=True)
-        inverse = inverse * (2.0 - scale * inverse)
-        inverse = inverse * (2.0 - scale * inverse)
-        inverse = inverse * ends_ref[at, 0:1]
+        d, fall, suffix = one, one + one, zero
+        for z in reversed(range(first + levels, depth)):
+            suffix = suffix + d * source(z)
+            fall = fall + sigma * d
+            d = d + fall
+        scale = slope * d + c_ref[levels - 1] * fall
+        inverse = inverted(scale) * ends_ref[at, 0:1]
         for k in reversed(range(levels)):
             out_ref[k, at] = inverse * (d * prefix_ref[k] + c_ref[k] * suffix)
-            if k:
+            if k and first + k >= 0:
                 suffix = suffix + d * source(first + k)
-                fall_slope = fall_slope + sigma * d
-                d = d + fall_slope
+                fall = fall + sigma * d
+                d = d + fall
         return carry
 
-    lax.fori_loop(0, width // rows, group, 0)
+    for slab_id in range(depth // (levels - 1)):
+        first = slab_id * (levels - 1) - 1
+
+        @pl.when(place_ref[0] == slab_id)
+        def _(first=first):
+            lax.fori_loop(0, width // rows, functools.partial(group, first), 0)
 
 
 def border_solve(all_jumps, order, place, width, length, slab):
     groups, _, depth, lanes = all_jumps.shape
-    rows = divisor_of(width, 8, 32)
+    rows = divisor_of(width, 8, 16)
     modes = spectral_order(width)
     nu = eigenvalues(width)[modes][:, None].astype(np.float32)
     mu = eigenvalues(length)[spectral_order(length)][None, :].astype(np.float32)
@@ -475,7 +461,7 @@
 
 
 def eliminate_kernel(place_ref, field_ref, ratio_ref, order_ref, high_ref, low_ref, *refs):
-    modes_ref, last_ref, outer_ref, weight_ref = refs
+    modes_ref, last_ref, outer_ref, through_ref, weight_ref = refs
     t, steps = pl.program_id(0), pl.num_programs(0)
     modes = block_dot(high_ref, low_ref, field_ref[0])
     modes_ref[0] = modes
@@ -495,6 +481,10 @@
         def _():
             outer_ref[...] += weight_ref[...] * running
             weight_ref[...] *= ratio
+
+        @pl.when(t == steps - 1)
+        def _():
+            through_ref[...] = weight_ref[...] * ratio
 
 
 def eliminate(field, ratios, order, place):
@@ -517,10 +507,10 @@
                 fixed(high.shape),
                 fixed(low.shape),
             ],
-            out_specs=[pl.BlockSpec((1, width, lanes), lambda t, p: (t, 0, 0)), plane, plane],
+            out_specs=[pl.BlockSpec((1, width, lanes), lambda t, p: (t, 0, 0)), plane, plane, plane],
             scratch_shapes=[pltpu.VMEM((width, lanes), F32)],
         ),
-        out_shape=[hbm((slab, width, lanes)), hbm((width, lanes)), hbm((width, lanes))],
+        out_shape=[hbm((slab, width, lanes))] + [hbm((width, lanes))] * 3,
         compiler_params=params(32),
         cost_estimate=cost(6 * width * field.size, 3 * field.size),
         name="eliminate",
@@ -586,17 +576,14 @@
 
 
 def relay_kernel(last_ref, through_ref, in_ref, order_ref, out_ref):
-    through = through_ref[0]
-    for t in range(1, through_ref.shape[0]):
-        through = through * through_ref[t]
-    out_ref[...] = last_ref[...] + through * in_ref[...]
+    out_ref[...] = last_ref[...] + through_ref[...] * in_ref[...]
 
 
 def row_tile(width):
     return divisor_of(width, 8, 48)
 
 
-def relay(last, ratios, slab, incoming, order, chunk):
+def relay(last, through, incoming, order):
     width, lanes = last.shape
     tile = row_tile(width)
     own = pl.BlockSpec((tile, lanes), lambda i: (i, 0))
@@ -605,7 +592,7 @@
         grid=(width // tile,),
         in_specs=[
             own,
-            pl.BlockSpec((slab, tile, lanes), lambda i: (0, i, chunk)),
+            own,
             own,
             pl.BlockSpec(memory_space=pl.ANY),
         ],
@@ -614,7 +601,7 @@
         compiler_params=params(),
         cost_estimate=cost(2 * last.size, 4 * last.size),
         name="relay",
-    )(in_hbm(last), in_hbm(ratios), incoming, order)
+    )(in_hbm(last), in_hbm(through), incoming, order)
 
 
 def turn_kernel(slab, place_ref, mine_ref, theirs_ref, in_ref, outer_ref, next_ref, ratios_ref, *refs):
@@ -668,46 +655,48 @@
 
 
 def sequence(sigma, upper, steps):
-    zero = sigma * 0.0
-    slope = zero + jnp.where(upper, 2.0, 0.0).astype(F32)
-
-    def advance(_, state):
-        value, slope = state
+    value, slope = sigma * 0.0 + 1.0, sigma * 0.0 + (2.0 if upper else 0.0)
+    for _ in range(steps):
         slope = slope + sigma * value
-        return value + slope, slope
-
-    return lax.fori_loop(0, steps, advance, (zero + 1.0, slope))
-
-
-def ratio_kernel(steps, lanes, place_ref, nu_ref, mu_ref, ratios_ref):
+        value = value + slope
+    return value, slope
+
+
+def ratio_kernel(groups, lanes, place_ref, nu_ref, mu_ref, ratios_ref):
     planes, rows, length = ratios_ref.shape
     slab = planes - 2
-    upper, rank = place_ref[4] == 1, place_ref[8]
-
-    def group(i, carry):
+    half = groups // 2
+
+    def part(me, i, carry):
+        upper = me >= half
+        rank = groups - 1 - me if upper else me
         at = pl.ds(pl.multiple_of(i * lanes, lanes), lanes)
         sigma = nu_ref[...] + mu_ref[:, at]
         value, slope = sequence(sigma, upper, rank * slab)
-        ratios_ref[slab, :, at] = jnp.where(rank == 0, 0.0, (value - slope) * inverted(value))
+        ratios_ref[slab, :, at] = (value - slope) * inverted(value) if rank else sigma * 0.0
         for t in range(slab):
             slope = slope + sigma * value
             following = value + slope
             ratios_ref[t, :, at] = value * inverted(following)
             value = following
-        value, slope = sequence(sigma, jnp.logical_not(upper), steps)
+        value, slope = sequence(sigma, not upper, half * slab)
         ratios_ref[slab + 1, :, at] = (value - slope) * inverted(value)
         return carry
 
-    lax.fori_loop(0, length // lanes, group, 0)
+    for me in range(groups):
+
+        @pl.when(place_ref[0] == me)
+        def _(me=me):
+            lax.fori_loop(0, length // lanes, functools.partial(part, me), 0)
 
 
 def pivots(width, length, slab, groups, place):
     rows = divisor_of(width, 8, 32)
-    lanes = divisor_of(length, 128, 512)
+    lanes = divisor_of(length, 128, 256)
     nu = eigenvalues(width)[spectral_order(width)][:, None].astype(np.float32)
     mu = eigenvalues(length)[spectral_order(length)][None, :].astype(np.float32)
     return pl.pallas_call(
-        functools.partial(ratio_kernel, groups // 2 * slab, lanes),
+        functools.partial(ratio_kernel, groups, lanes),
         grid_spec=pltpu.PrefetchScalarGridSpec(
             num_scalar_prefetch=1,
             grid=(width // rows,),
@@ -935,7 +924,7 @@
             ],
         ),
         out_shape=[
-            jax.ShapeDtypeStruct((slab, width, lanes), F32) if with_levels else hbm((slab, width, lanes)),
+            hbm((slab, width, lanes)),
             jax.ShapeDtypeStruct((copies, 1, 128), F32),
             hbm((1, width, lanes)),
         ],
@@ -997,8 +986,8 @@
         cost_estimate=cost(10 * direction.size, 10 * direction.size),
         name="update",
     )(
-        sums, precond_low, precond_high, in_hbm(direction), in_hbm(solution), in_hbm(residual),
-        in_hbm(image_old), image_new, old_face, new_face,
+        sums, in_hbm(precond_low), in_hbm(precond_high), in_hbm(direction), in_hbm(solution), in_hbm(residual),
+        in_hbm(image_old), in_hbm(image_new), old_face, new_face,
     )
 
 
@@ -1027,7 +1016,7 @@
     inward = [[(s - 1, s), (groups - s, groups - 1 - s)] for s in range(1, half)]
     outward = [[(j, i) for i, j in pairs] for pairs in reversed(inward)]
     across = [(half - 1, half), (half, half - 1)]
-    modes, last, outer = eliminate(spectral, ratios, fraction_below, place)
+    modes, last, outer, through = eliminate(spectral, ratios, fraction_below, place)
     zero = jnp.zeros_like(last)
     parts = end_responses(spectral, last, place, groups)
     late_top, parts = lax.optimization_barrier((top, parts))
@@ -1037,12 +1026,13 @@
     for k, pairs in enumerate(inward):
         arrived = lax.ppermute(mine, "gz", pairs)
         incoming = incoming + arrived if k else arrived
-        mine = relay(last, ratios, slab, incoming, below, 0)
+        mine = relay(last, through, incoming, below)
     ends, mine = lax.optimization_barrier((ends, mine))
     all_ends = lax.all_to_all(
         jnp.broadcast_to(ends[None], (plane_parts,) + ends.shape), "xy", 0, 0, tiled=True
     )
-    all_jumps = lax.all_to_all(jumps(all_ends, sides, place, width, groups), "gz", 0, 0, tiled=True)
+    own_jumps = jumps(all_ends, sides, place, width, groups)
+    all_jumps = lax.all_to_all(own_jumps, "gz", 0, 0, tiled=True)
     theirs = lax.ppermute(mine, "gz", across)
     orders = (below_too, all_jumps)
     message, following = turn(mine, theirs, incoming, outer, zero, ratios, orders, place, 0)
@@ -1070,7 +1060,7 @@
     )
     new_above = lax.ppermute(new_face, "gz", down)
     image_new, sums, _ = apply_operator(
-        [precond_low, precond_high], belows, (jump_rows, jump_rows),
+        [in_hbm(precond_low), in_hbm(precond_high)], belows, (jump_rows, jump_rows),
         in_hbm(volume_fraction), border, density, [in_hbm(residual), in_hbm(image_old)],
         in_hbm(old_face), sums_old, 2, groups * plane_parts, sums_old, place, "image_new"
     )

time: 244 us -> 239 us (0.980)
  local copies, waits for them, and re-layouts: 15.5 us -> 10.6 us
    unnamed x70 -> x58, local copies, waits for them, and re-layouts: 13.9 us -> 8.93 us
    pallas_call x1, Pallas kernels: 14.6 us -> 11 us  [border_solve(): pl.pallas_call(functools.partial(border_kernel, rows), grid_spec=pltpu.Pr...]
  transfers between devices with their start and end apart: 14 -> 14, of which waited for: 6 -> 7; matrix products, arithmetic and copies ran while one was open for 1% -> 1% of each run, Pallas kernels for 49% -> 49%
where the time goes in v2:
time: 239 us; the launch traced here: 238 us
  Pallas kernels  142 us (59%)
  starting transfers between devices  46.4 us (19%)
  waiting for transfers between devices  34.4 us (14%)
  local copies, waits for them, and re-layouts  10.6 us (4%)
    pallas_call x2, Pallas kernels, apply_operator(): pl.pallas_call(functools.partial(operator_kernel, len(others), n_kept, wi...  32.2 us
    pallas_call x1, Pallas kernels, update(): pl.pallas_call(update_kernel, grid=(width // tile,), in_specs=[fixed(sums...  15.8 us
    pallas_call x1, Pallas kernels, forward_rows(): pl.pallas_call(forward_kernel, grid=(count // tile,), in_specs=[pl.BlockS...  11.7 us
    pallas_call x1, Pallas kernels, border_solve(): pl.pallas_call(functools.partial(border_kernel, rows), grid_spec=pltpu.Pr...  11 us
    pallas_call x1, Pallas kernels, inverse_rows(): pl.pallas_call(functools.partial(inverse_kernel, True), grid_spec=pltpu.P...  10.8 us
    pallas_call x1, Pallas kernels, inverse_rows(): pl.pallas_call(functools.partial(inverse_kernel, False), grid_spec=pltpu....  10.7 us
    pallas_call x1, Pallas kernels, eliminate(): pl.pallas_call(eliminate_kernel, grid_spec=pltpu.PrefetchScalarGridSpec(n...  9.92 us
    all_to_all x1, waiting for transfers between devices, body(): ends = jnp.sum(lax.all_to_all(parts, 'gz', 0, 0, tiled=True), axis=0)  9.84 us
  transfers between devices with their start and end apart: 14, of which 7 were waited for; matrix products, arithmetic and copies ran while one was open for 1% of the time, Pallas kernels for 49%

profile of v2, /device:TPU:0, one launch (start us, length us, event | category | flops | bytes accessed | tf_op | source)
XLA Modules:
  0.0 237.5 jit_solution(9821513449375795843)
XLA Ops:
  0.7 3.3 %cut_borders.1 = (f32[1,192,1536]{2,1,0:T(8,128)}, f32[1,192,1536]{2,1,0:T(8,128)}, f32[8,1,1536]{2,1,0:T(1,128)S(1)}, f32[8,1,1536]{2,1,0:T(1,128)S(1)}) custom-call(f32[4,192,1536]{2,1,0:T(8,128)} %direction_ref.1, f32[4,192,1536]{2,1,0:T(8,128)} %refs_10_.1, f32[4,192,1536]{2,1,0:T(8,128)} %direction_ref.1, f32[4,192,1536]{2,1,0:T(8,128)} %refs_10_.1, ...), custom_call_target="tpu_custom_call" | custom-call | bytes 294912 | tf_op jit(solution)/shard_map/cut_borders/pallas_call | solution.py:730
  4.0 0.6 copy-done.26
  5.2 4.9 %collective-permute-start = (f32[1,192,1536]{2,1,0:T(8,128)}, f32[1,192,1536]{2,1,0:T(8,128)S(1)}, u32[]{:S(2)}, u32[]{:S(2)}) collective-permute-start(f32[1,192,1536]{2,1,0:T(8,128)} %get-tuple-element.25), channel_id=1, source_target_pairs={{0,8},{8,16},{16,24},{1,9},{9,17},{17,25},{2,10},{10,18},{18,26},{... | collective-permute-start | bytes 3538952 | tf_op jit(solution)/shard_map/ppermute | solution.py:1009
  10.1 0.7 collective-permute-start.2
  10.9 0.6 fusion
  13.0 7.8 %ratios.1.ratio_ref.ratios_ref.prev_ratio_ref = f32[6,192,1536]{2,1,0:T(8,128)} custom-call(s32[9]{0:T(128)S(1)} %stack.63.place_ref, f32[192,1]{1,0:T(8,128)S(1)} %copy-done.13, f32[1,1536]{1,0:T(1,128)S(1)} %copy-done.22), custom_call_target="tpu_custom_call" | custom-call | flops 2211840 | bytes 442368 | tf_op jit(solution)/shard_map/ratios/pallas_call | solution.py:698
  20.8 11.7 %forward_rows.1 = f32[768,1536]{1,0:T(8,128)} custom-call(f32[1]{0:T(128)S(6)} %div.14.scale_ref, f32[768,1536]{1,0:T(8,128)} %bitcast.22, bf16[2,768,768]{2,1,0:T(8,128)(2,1)} %constant.61.clone.high_ref, bf16[2,768,768]{2,1,0:T(8,128)(2,1)} %constant.62.clone.low_ref, bf16[256,256]{1,0:T(8,128)(2,1)S(1)} %copy-done.1), custom_call_target="tpu_custom_call" | custom-call | flops 339738624 | bytes 589824 | tf_op jit(solution)/shard_map/forward_rows/pallas_call | solution.py:136
  32.5 3.1 %collective-permute-done.order_ref.refs_10_.refs_2_.refs_11_ = f32[1,192,1536]{2,1,0:T(8,128)S(1)} collective-permute-done((f32[1,192,1536]{2,1,0:T(8,128)}, f32[1,192,1536]{2,1,0:T(8,128)S(1)}, u32[]{:S(2)}, u32[]{:S(2)}) %collective-permute-start) | collective-permute-done | bytes 1179680 | tf_op jit(solution)/shard_map/ppermute | solution.py:1009
  35.6 9.9 %eliminate.1 = (f32[4,192,1536]{2,1,0:T(8,128)}, f32[192,1536]{1,0:T(8,128)}, f32[192,1536]{1,0:T(8,128)}, f32[192,1536]{1,0:T(8,128)}) custom-call(s32[9]{0:T(128)S(1)} %stack.63.place_ref, f32[4,192,1536]{2,1,0:T(8,128)} %bitcast.23, f32[6,192,1536]{2,1,0:T(8,128)} %ratios.1.ratio_ref.ratios_ref.prev_ratio_ref, ...), custom_call_target="tpu_custom_call" | custom-call | flops 84934656 | bytes 884736 | tf_op jit(solution)/shard_map/eliminate/pallas_call | solution.py:495
  45.5 4.6 %collective-permute-start.1 = (f32[192,1536]{1,0:T(8,128)}, f32[192,1536]{1,0:T(8,128)S(1)}, u32[]{:S(2)}, u32[]{:S(2)}) collective-permute-start(f32[192,1536]{1,0:T(8,128)} %get-tuple-element.27.order_ref.last_ref), channel_id=1, source_target_pairs={{0,8},{24,16},{1,9},{25,17},{2,10},{26,18},{3,11},{27,19},{4,12},{... | collective-permute-start | bytes 3538952 | tf_op jit(solution)/shard_map/ppermute | solution.py:1027
  50.2 1.3 copy-done
  51.4 7.3 %end_responses.1 = f32[4,2,16,384]{3,2,1,0:T(8,128)S(1)} custom-call(s32[9]{0:T(128)S(1)} %stack.63.place_ref, f32[4,192,1536]{2,1,0:T(8,128)} %bitcast.24, bf16[4,256,192]{2,1,0:T(8,128)(2,1)S(1)} %copy-done.12, f32[16,1536]{1,0:T(8,128)S(1)} %copy-done.21, f32[192,1536]{1,0:T(8,128)S(1)} %copy-done), custom_call_target="tpu_custom_call" | custom-call | flops 113246208 | bytes 294912 | tf_op jit(solution)/shard_map/end_responses/pallas_call | solution.py:291
  58.8 0.7 copy-done.5
  59.5 4.5 %all-to-all-start = ((f32[4,2,16,384]{3,2,1,0:T(8,128)}), f32[4,2,16,384]{3,2,1,0:T(8,128)}, u32[]{:S(2)}, u32[]{:S(2)}) async-start(f32[4,2,16,384]{3,2,1,0:T(8,128)} %copy-done.5), calls=%async_computation | async-start | bytes 393216 | tf_op jit(solution)/shard_map/all_to_all | solution.py:1024
  64.0 5.1 %collective-permute-start.4 = (f32[1,192,1536]{2,1,0:T(8,128)}, f32[1,192,1536]{2,1,0:T(8,128)}, u32[]{:S(2)}, u32[]{:S(2)}) collective-permute-start(f32[1,192,1536]{2,1,0:T(8,128)} %get-tuple-element.33), channel_id=1, source_target_pairs={{0,8},{1,9},{2,10},{3,11},{4,12},{5,13},{6,14},{7,15}} | collective-permute-start | bytes 3538952 | tf_op jit(solution)/shard_map/ppermute | solution.py:1023
  69.0 9.8 %all-to-all-done = f32[4,2,16,384]{3,2,1,0:T(8,128)} async-done(((f32[4,2,16,384]{3,2,1,0:T(8,128)}), f32[4,2,16,384]{3,2,1,0:T(8,128)}, u32[]{:S(2)}, u32[]{:S(2)}) %all-to-all-start) | async-done | bytes 196640 | tf_op jit(solution)/shard_map/all_to_all | solution.py:1024
  78.9 1.6 reduce_sum.9
  80.5 3.7 %relay.1.mine_ref = f32[192,1536]{1,0:T(8,128)} custom-call(f32[192,1536]{1,0:T(8,128)} %get-tuple-element.27.order_ref.last_ref, f32[192,1536]{1,0:T(8,128)} %get-tuple-element.30.through_ref, f32[192,1536]{1,0:T(8,128)S(1)} %collective-permute-done.1.in_ref, f32[1,192,1536]{2,1,0:T(8,128)S(1)} %collective-permute-done.2.order_ref.refs_3_.refs_14_), custom_call_target="tpu_custom_call" | custom-call | flops 36864 | bytes 294912 | tf_op jit(solution)/shard_map/relay/pallas_call | solution.py:590
  84.1 1.7 collective-permute-start.3
  85.8 0.8 broadcast_in_dim.13
  86.6 4.9 %all-to-all-start.1 = ((f32[8,2,16,384]{3,2,1,0:T(8,128)}), f32[8,2,16,384]{3,2,1,0:T(8,128)}, u32[]{:S(2)}, u32[]{:S(2)}) async-start(f32[8,2,16,384]{3,2,1,0:T(8,128)} %broadcast_in_dim.13), calls=%async_computation.1 | async-start | bytes 786432 | tf_op jit(solution)/shard_map/all_to_all | solution.py:1031
  91.5 2.4 %collective-permute-start.5 = (f32[8,1,1536]{2,1,0:T(1,128)}, f32[8,1,1536]{2,1,0:T(1,128)S(1)}, u32[]{:S(2)}, u32[]{:S(2)}) collective-permute-start(f32[8,1,1536]{2,1,0:T(1,128)} %copy-done.27), channel_id=1, source_target_pairs={{0,1},{1,2},{2,3},{3,4},{4,5},{5,6},{6,7},{8,9},{9,10},{10,11},{11... | collective-permute-start | bytes 147464 | tf_op jit(solution)/shard_map/ppermute | solution.py:1011
  93.9 1.3 collective-permute-start.6
  95.8 2.6 %collective-permute-done.6.order_too_ref.refs_6_.refs_12_.refs_13_ = f32[8,1,1536]{2,1,0:T(1,128)S(1)} collective-permute-done((f32[8,1,1536]{2,1,0:T(1,128)}, f32[8,1,1536]{2,1,0:T(1,128)S(1)}, u32[]{:S(2)}, u32[]{:S(2)}) %collective-permute-start.6) | collective-permute-done | bytes 49184 | tf_op jit(solution)/shard_map/ppermute | solution.py:1011
  98.4 0.6 copy-done.9
  99.0 5.2 %all-to-all-done.1.ends_ref = f32[8,2,16,384]{3,2,1,0:T(8,128)} async-done(((f32[8,2,16,384]{3,2,1,0:T(8,128)}), f32[8,2,16,384]{3,2,1,0:T(8,128)}, u32[]{:S(2)}, u32[]{:S(2)}) %all-to-all-start.1) | async-done | bytes 393248 | tf_op jit(solution)/shard_map/all_to_all | solution.py:1031
  104.1 0.8 copy-done.7
  104.9 0.8 copy-done.10
  105.7 0.9 copy-done.20
  106.6 0.7 copy-done.25
  107.3 1.8 jumps.1
  109.2 0.7 copy-done.4
  109.9 4.7 %all-to-all-start.2 = ((f32[4,2,16,384]{3,2,1,0:T(8,128)}), f32[4,2,16,384]{3,2,1,0:T(8,128)}, u32[]{:S(2)}, u32[]{:S(2)}) async-start(f32[4,2,16,384]{3,2,1,0:T(8,128)} %copy-done.4), calls=%async_computation.2 | async-start | bytes 393216 | tf_op jit(solution)/shard_map/all_to_all | solution.py:1035
  114.5 5.4 %all-to-all-done.2.refs_1_.jump_ref.refs_0_ = f32[4,2,16,384]{3,2,1,0:T(8,128)} async-done(((f32[4,2,16,384]{3,2,1,0:T(8,128)}), f32[4,2,16,384]{3,2,1,0:T(8,128)}, u32[]{:S(2)}, u32[]{:S(2)}) %all-to-all-start.2) | async-done | bytes 196640 | tf_op jit(solution)/shard_map/all_to_all | solution.py:1035
  120.0 6.4 %turn.1 = (f32[192,1536]{1,0:T(8,128)S(1)}, f32[192,1536]{1,0:T(8,128)}) custom-call(s32[9]{0:T(128)S(1)} %stack.63.place_ref, f32[192,1536]{1,0:T(8,128)} %relay.1.mine_ref, f32[192,1536]{1,0:T(8,128)} %collective-permute-done.3.theirs_ref, f32[192,1536]{1,0:T(8,128)S(1)} %collective-permute-done.1.in_ref, f32[192,1536]{1,0:T(8,128)} %get-tuple-element.32.outer_ref, ...), custom_call_target="tpu_custom_call" | custom-call | flops 221184 | bytes 884736 | tf_op jit(solution)/shard_map/turn/pallas_call | solution.py:632
  126.4 1.3 collective-permute-start.7
  127.8 15.5 %image_old.1 = (f32[4,192,1536]{2,1,0:T(8,128)}, f32[1,1,128]{2,1,0:T(1,128)S(1)}, f32[1,192,1536]{2,1,0:T(8,128)}) custom-call(s32[9]{0:T(128)S(1)} %stack.63.place_ref, f32[2]{0:T(128)S(1)} %copy-done.23, f32[4,192,1536]{2,1,0:T(8,128)} %direction_ref.1, f32[4,192,1536]{2,1,0:T(8,128)} %direction_ref.1, f32[4,192,1536]{2,1,0:T(8,128)} %direction_ref.1, ...), custom_call_target="tpu_custom_call" | custom-call | flops 7372800 | bytes 1253376 | tf_op jit(solution)/shard_map/image_old/pallas_call | solution.py:913
  143.3 1.6 collective-permute-start.8
  144.9 11.0 %border_solve.1.border_ref = f32[5,192,1536]{2,1,0:T(8,128)S(1)} custom-call(s32[9]{0:T(128)S(1)} %stack.63.place_ref, f32[4,2,16,384]{3,2,1,0:T(8,128)} %all-to-all-done.2.refs_1_.jump_ref.refs_0_, f32[192,1]{1,0:T(8,128)S(1)} %copy-done.14, f32[1,1536]{1,0:T(1,128)S(1)} %copy-done.22, f32[192,1]{1,0:T(8,128)S(1)} %copy-done.17, ...), custom_call_target="tpu_custom_call" | custom-call | flops 5898240 | bytes 368640 | tf_op jit(solution)/shard_map/border_solve/pallas_call | solution.py:432
  155.9 1.3 collective-permute-done.7.back_ref
  157.3 9.8 %substitute.1 = f32[5,192,1536]{2,1,0:T(8,128)} custom-call(s32[9]{0:T(128)S(1)} %stack.63.place_ref, f32[4,192,1536]{2,1,0:T(8,128)} %get-tuple-element.26.modes_ref, f32[6,192,1536]{2,1,0:T(8,128)} %ratios.1.ratio_ref.ratios_ref.prev_ratio_ref, f32[6,192,1536]{2,1,0:T(8,128)} %ratios.1.ratio_ref.ratios_ref.prev_ratio_ref, ...), custom_call_target="tpu_custom_call" | custom-call | flops 127401984 | bytes 1179648 | tf_op jit(solution)/shard_map/substitute/pallas_call | solution.py:548
  167.1 10.8 %inverse_lower.1 = (f32[384,1536]{1,0:T(8,128)}, f32[8,1,1536]{2,1,0:T(1,128)S(1)}, f32[1,192,1536]{2,1,0:T(8,128)}) custom-call(s32[9]{0:T(128)S(1)} %stack.63.place_ref, f32[2]{0:T(128)S(1)} %copy-done.23, f32[960,1536]{1,0:T(8,128)} %bitcast.14, f32[960,1536]{1,0:T(8,128)} %bitcast.15, bf16[2,768,768]{2,1,0:T(8,128)(2,1)} %constant.75.clone.high_ref, ...), custom_call_target="tpu_custom_call" | custom-call | flops 198180864 | bytes 294912 | tf_op jit(solution)/shard_map/inverse_lower/pallas_call | solution.py:204
  177.9 1.3 collective-permute-start.9
  179.2 10.7 %inverse_upper.1 = f32[576,1536]{1,0:T(8,128)} custom-call(s32[9]{0:T(128)S(1)} %stack.63.place_ref, f32[2]{0:T(128)S(1)} %copy-done.23, f32[960,1536]{1,0:T(8,128)} %bitcast.16, f32[960,1536]{1,0:T(8,128)} %bitcast.17, bf16[2,768,768]{2,1,0:T(8,128)(2,1)} %constant.75.clone.high_ref, bf16[2,768,768]{2,1,0:T(8,128)(2,1)} %constant.76.clone.low_ref, ...), custom_call_target="tpu_custom_call" | custom-call | flops 297271296 | bytes 442368 | tf_op jit(solution)/shard_map/inverse_upper/pallas_call | solution.py:227
  189.8 16.8 %image_new.1 = (f32[4,192,1536]{2,1,0:T(8,128)}, f32[32,1,128]{2,1,0:T(1,128)S(1)}, f32[1,192,1536]{2,1,0:T(8,128)}) custom-call(s32[9]{0:T(128)S(1)} %stack.63.place_ref, f32[2]{0:T(128)S(1)} %copy-done.23, f32[2,192,1536]{2,1,0:T(8,128)} %bitcast.25, f32[2,192,1536]{2,1,0:T(8,128)} %bitcast.26, f32[2,192,1536]{2,1,0:T(8,128)} %bitcast.27, ...), custom_call_target="tpu_custom_call" | custom-call | flops 7372800 | bytes 1548288 | tf_op jit(solution)/shard_map/image_new/pallas_call | solution.py:913
  207.2 7.5 %all-to-all-start.3 = ((f32[32,1,128]{2,1,0:T(1,128)}), f32[32,1,128]{2,1,0:T(1,128)S(1)}, u32[]{:S(2)}, u32[]{:S(2)}) async-start(f32[32,1,128]{2,1,0:T(1,128)} %copy-done.24), calls=%async_computation.3 | async-start | bytes 32768 | tf_op jit(solution)/shard_map/all_to_all | solution.py:1067
  214.7 7.1 %all-to-all-done.3.sums_ref = f32[32,1,128]{2,1,0:T(1,128)S(1)} async-done(((f32[32,1,128]{2,1,0:T(1,128)}), f32[32,1,128]{2,1,0:T(1,128)S(1)}, u32[]{:S(2)}, u32[]{:S(2)}) %all-to-all-start.3) | async-done | bytes 16416 | tf_op jit(solution)/shard_map/all_to_all | solution.py:1067
  221.8 15.8 %update.1 = (f32[4,192,1536]{2,1,0:T(8,128)}, f32[4,192,1536]{2,1,0:T(8,128)}, f32[4,192,1536]{2,1,0:T(8,128)}) custom-call(f32[32,1,128]{2,1,0:T(1,128)S(1)} %all-to-all-done.3.sums_ref, f32[2,192,1536]{2,1,0:T(8,128)} %bitcast.28, f32[3,192,1536]{2,1,0:T(8,128)} %bitcast.21, f32[4,192,1536]{2,1,0:T(8,128)} %direction_ref.1, f32[4,192,1536]{2,1,0:T(8,128)} %solution_ref.1, ...), custom_call_target="tpu_custom_call" | custom-call | flops 737280 | bytes 2949120 | tf_op jit(solution)/shard_map/update/pallas_call | solution.py:973
  (59 shorter events, 2.1 us)
Async XLA Ops:
  0.6 12.4 %copy-start.13 = (f32[192,1]{1,0:T(8,128)S(1)}, f32[192,1]{1,0:T(8,128)}, u32[]{:S(2)}) copy-start(f32[192,1]{1,0:T(8,128)} %constant.64.clone.nu_ref) | copy-start | bytes 2308
  0.6 12.4 %copy-start.22 = (f32[1,1536]{1,0:T(1,128)S(1)}, f32[1,1536]{1,0:T(1,128)}, u32[]{:S(2)}) copy-start(f32[1,1536]{1,0:T(1,128)} %constant.65.clone.mu_ref) | copy-start | bytes 18436
  0.7 10.3 %copy-start.23 = (f32[2]{0:T(128)S(1)}, f32[2]{0:T(128)}, u32[]{:S(2)}) copy-start(f32[2]{0:T(128)} %density_ref.7) | copy-start | bytes 28
  4.0 0.6 copy-start.26
  4.6 0.6 copy-start.27
  5.2 30.4 %collective-permute-start = (f32[1,192,1536]{2,1,0:T(8,128)}, f32[1,192,1536]{2,1,0:T(8,128)S(1)}, u32[]{:S(2)}, u32[]{:S(2)}) collective-permute-start(f32[1,192,1536]{2,1,0:T(8,128)} %get-tuple-element.25), channel_id=1, source_target_pairs={{0,8},{8,16},{16,24},{1,9},{9,17},{17,25},{2,10},{10,18},{18,26},{... | collective-permute-start | bytes 3538952 | tf_op jit(solution)/shard_map/ppermute | solution.py:1009
  10.1 70.3 %collective-permute-start.2 = (f32[1,192,1536]{2,1,0:T(8,128)}, f32[1,192,1536]{2,1,0:T(8,128)S(1)}, u32[]{:S(2)}, u32[]{:S(2)}) collective-permute-start(f32[1,192,1536]{2,1,0:T(8,128)} %get-tuple-element.33), channel_id=1, source_target_pairs={{8,16},{16,24},{9,17},{17,25},{10,18},{18,26},{11,19},{19,27},{12,... | collective-permute-start | bytes 3538952 | tf_op jit(solution)/shard_map/ppermute | solution.py:1010
  13.0 7.8 %copy-start.1 = (bf16[256,256]{1,0:T(8,128)(2,1)S(1)}, bf16[256,256]{1,0:T(8,128)(2,1)}, u32[]{:S(2)}) copy-start(bf16[256,256]{1,0:T(8,128)(2,1)} %constant.63.clone.flip_ref) | copy-start | bytes 393220
  20.8 14.8 %copy-start.18 = (bf16[192,192]{1,0:T(8,128)(2,1)S(1)}, bf16[192,192]{1,0:T(8,128)(2,1)}, u32[]{:S(2)}) copy-start(bf16[192,192]{1,0:T(8,128)(2,1)} %constant.66.clone.high_ref) | copy-start | bytes 221188
  20.8 14.8 %copy-start.19 = (bf16[192,192]{1,0:T(8,128)(2,1)S(1)}, bf16[192,192]{1,0:T(8,128)(2,1)}, u32[]{:S(2)}) copy-start(bf16[192,192]{1,0:T(8,128)(2,1)} %constant.67.clone.low_ref) | copy-start | bytes 221188
  35.6 14.5 %copy-start.12 = (bf16[4,256,192]{2,1,0:T(8,128)(2,1)S(1)}, bf16[4,256,192]{2,1,0:T(8,128)(2,1)}, u32[]{:S(2)}) copy-start(bf16[4,256,192]{2,1,0:T(8,128)(2,1)} %constant.68.clone.mixer_ref) | copy-start | bytes 1179652
  35.6 14.5 %copy-start.21 = (f32[16,1536]{1,0:T(8,128)S(1)}, f32[16,1536]{1,0:T(8,128)}, u32[]{:S(2)}) copy-start(f32[16,1536]{1,0:T(8,128)} %constant.69.clone.ratio_ref) | copy-start | bytes 294916
  45.5 34.9 %collective-permute-start.1 = (f32[192,1536]{1,0:T(8,128)}, f32[192,1536]{1,0:T(8,128)S(1)}, u32[]{:S(2)}, u32[]{:S(2)}) collective-permute-start(f32[192,1536]{1,0:T(8,128)} %get-tuple-element.27.order_ref.last_ref), channel_id=1, source_target_pairs={{0,8},{24,16},{1,9},{25,17},{2,10},{26,18},{3,11},{27,19},{4,12},{... | collective-permute-start | bytes 3538952 | tf_op jit(solution)/shard_map/ppermute | solution.py:1027
  50.2 1.3 copy-start
  58.8 0.7 copy-start.5
  59.5 19.4 %all-to-all-start = ((f32[4,2,16,384]{3,2,1,0:T(8,128)}), f32[4,2,16,384]{3,2,1,0:T(8,128)}, u32[]{:S(2)}, u32[]{:S(2)}) async-start(f32[4,2,16,384]{3,2,1,0:T(8,128)} %copy-done.5), calls=%async_computation | async-start | bytes 393216 | tf_op jit(solution)/shard_map/all_to_all | solution.py:1024
  64.0 50.5 %collective-permute-start.4 = (f32[1,192,1536]{2,1,0:T(8,128)}, f32[1,192,1536]{2,1,0:T(8,128)}, u32[]{:S(2)}, u32[]{:S(2)}) collective-permute-start(f32[1,192,1536]{2,1,0:T(8,128)} %get-tuple-element.33), channel_id=1, source_target_pairs={{0,8},{1,9},{2,10},{3,11},{4,12},{5,13},{6,14},{7,15}} | collective-permute-start | bytes 3538952 | tf_op jit(solution)/shard_map/ppermute | solution.py:1023
  80.5 5.3 %copy-start.28 = (f32[2,16,384]{2,1,0:T(8,128)S(1)}, f32[2,16,384]{2,1,0:T(8,128)}, u32[]{:S(2)}) copy-start(f32[2,16,384]{2,1,0:T(8,128)} %reduce_sum.9) | copy-start | bytes 147460
  84.1 35.7 %collective-permute-start.3 = (f32[192,1536]{1,0:T(8,128)}, f32[192,1536]{1,0:T(8,128)}, u32[]{:S(2)}, u32[]{:S(2)}) collective-permute-start(f32[192,1536]{1,0:T(8,128)} %relay.1.mine_ref), channel_id=1, source_target_pairs={{8,16},{16,8},{9,17},{17,9},{10,18},{18,10},{11,19},{19,11},{12,20... | collective-permute-start | bytes 3538952 | tf_op jit(solution)/shard_map/ppermute | solution.py:1036
  86.6 17.5 %all-to-all-start.1 = ((f32[8,2,16,384]{3,2,1,0:T(8,128)}), f32[8,2,16,384]{3,2,1,0:T(8,128)}, u32[]{:S(2)}, u32[]{:S(2)}) async-start(f32[8,2,16,384]{3,2,1,0:T(8,128)} %broadcast_in_dim.13), calls=%async_computation.1 | async-start | bytes 786432 | tf_op jit(solution)/shard_map/all_to_all | solution.py:1031
  91.5 3.7 %collective-permute-start.5 = (f32[8,1,1536]{2,1,0:T(1,128)}, f32[8,1,1536]{2,1,0:T(1,128)S(1)}, u32[]{:S(2)}, u32[]{:S(2)}) collective-permute-start(f32[8,1,1536]{2,1,0:T(1,128)} %copy-done.27), channel_id=1, source_target_pairs={{0,1},{1,2},{2,3},{3,4},{4,5},{5,6},{6,7},{8,9},{9,10},{10,11},{11... | collective-permute-start | bytes 147464 | tf_op jit(solution)/shard_map/ppermute | solution.py:1011
  93.9 4.5 %collective-permute-start.6 = (f32[8,1,1536]{2,1,0:T(1,128)}, f32[8,1,1536]{2,1,0:T(1,128)S(1)}, u32[]{:S(2)}, u32[]{:S(2)}) collective-permute-start(f32[8,1,1536]{2,1,0:T(1,128)} %copy-done.26), channel_id=1, source_target_pairs={{1,0},{2,1},{3,2},{4,3},{5,4},{6,5},{7,6},{9,8},{10,9},{11,10},{12... | collective-permute-start | bytes 147464 | tf_op jit(solution)/shard_map/ppermute | solution.py:1011
  95.2 0.6 copy-start.6
  98.4 0.6 copy-start.9
  104.1 0.8 copy-start.7
  104.9 0.8 copy-start.10
  105.7 0.9 copy-start.20
  106.6 0.7 copy-start.25
  109.2 0.7 copy-start.4
  109.9 10.0 %all-to-all-start.2 = ((f32[4,2,16,384]{3,2,1,0:T(8,128)}), f32[4,2,16,384]{3,2,1,0:T(8,128)}, u32[]{:S(2)}, u32[]{:S(2)}) async-start(f32[4,2,16,384]{3,2,1,0:T(8,128)} %copy-done.4), calls=%async_computation.2 | async-start | bytes 393216 | tf_op jit(solution)/shard_map/all_to_all | solution.py:1035
  120.0 7.7 %copy-start.8 = (f32[8,1,1536]{2,1,0:T(1,128)S(1)}, f32[8,1,1536]{2,1,0:T(1,128)}, u32[]{:S(2)}) copy-start(f32[8,1,1536]{2,1,0:T(1,128)} %copy-done.6) | copy-start | bytes 147460
  120.0 7.7 %copy-start.11 = (f32[8,1,1536]{2,1,0:T(1,128)S(1)}, f32[8,1,1536]{2,1,0:T(1,128)}, u32[]{:S(2)}) copy-start(f32[8,1,1536]{2,1,0:T(1,128)} %copy-done.9) | copy-start | bytes 147460
  126.4 30.8 %collective-permute-start.7 = (f32[192,1536]{1,0:T(8,128)S(1)}, f32[192,1536]{1,0:T(8,128)S(1)}, u32[]{:S(2)}, u32[]{:S(2)}) collective-permute-start(f32[192,1536]{1,0:T(8,128)S(1)} %get-tuple-element.38.order_ref.refs_16_), channel_id=1, source_target_pairs={{8,0},{16,24},{9,1},{17,25},{10,2},{18,26},{11,3},{19,27},{12,4},{... | collective-permute-start | bytes 3538952 | tf_op jit(solution)/shard_map/ppermute | solution.py:1045
  127.8 17.1 %copy-start.14 = (f32[192,1]{1,0:T(8,128)S(1)}, f32[192,1]{1,0:T(8,128)}, u32[]{:S(2)}) copy-start(f32[192,1]{1,0:T(8,128)} %constant.64.clone.nu_ref) | copy-start | bytes 2308
  127.8 17.1 %copy-start.17 = (f32[192,1]{1,0:T(8,128)S(1)}, f32[192,1]{1,0:T(8,128)}, u32[]{:S(2)}) copy-start(f32[192,1]{1,0:T(8,128)} %constant.72.clone.ends_ref) | copy-start | bytes 2308
  143.2 14.0 %copy-start.3 = (f32[192,1536]{1,0:T(8,128)S(1)}, f32[192,1536]{1,0:T(8,128)}, u32[]{:S(2)}) copy-start(f32[192,1536]{1,0:T(8,128)} %get-tuple-element.37.next_ref) | copy-start | bytes 3538948
  143.3 14.0 %copy-start.15 = (bf16[192,192]{1,0:T(8,128)(2,1)S(1)}, bf16[192,192]{1,0:T(8,128)(2,1)}, u32[]{:S(2)}) copy-start(bf16[192,192]{1,0:T(8,128)(2,1)} %constant.73.clone.high_ref) | copy-start | bytes 221188
  143.3 14.0 %copy-start.16 = (bf16[192,192]{1,0:T(8,128)(2,1)S(1)}, bf16[192,192]{1,0:T(8,128)(2,1)}, u32[]{:S(2)}) copy-start(bf16[192,192]{1,0:T(8,128)(2,1)} %constant.74.clone.low_ref) | copy-start | bytes 221188
  143.3 71.4 %collective-permute-start.8 = (f32[1,192,1536]{2,1,0:T(8,128)}, f32[1,192,1536]{2,1,0:T(8,128)S(1)}, u32[]{:S(2)}, u32[]{:S(2)}) collective-permute-start(f32[1,192,1536]{2,1,0:T(8,128)} %get-tuple-element.43.refs_16_), channel_id=1, source_target_pairs={{8,0},{16,8},{24,16},{9,1},{17,9},{25,17},{10,2},{18,10},{26,18},{... | collective-permute-start | bytes 3538952 | tf_op jit(solution)/shard_map/ppermute | solution.py:1054
  157.2 9.8 %copy-start.2 = (bf16[256,256]{1,0:T(8,128)(2,1)S(1)}, bf16[256,256]{1,0:T(8,128)(2,1)}, u32[]{:S(2)}) copy-start(bf16[256,256]{1,0:T(8,128)(2,1)} %constant.63.clone.flip_ref) | copy-start | bytes 393220
  177.9 43.9 %collective-permute-start.9 = (f32[1,192,1536]{2,1,0:T(8,128)}, f32[1,192,1536]{2,1,0:T(8,128)S(1)}, u32[]{:S(2)}, u32[]{:S(2)}) collective-permute-start(f32[1,192,1536]{2,1,0:T(8,128)} %get-tuple-element.46), channel_id=1, source_target_pairs={{8,0},{16,8},{24,16},{9,1},{17,9},{25,17},{10,2},{18,10},{26,18},{... | collective-permute-start | bytes 3538952 | tf_op jit(solution)/shard_map/ppermute | solution.py:1061
  206.6 0.6 copy-start.24
  207.2 14.5 %all-to-all-start.3 = ((f32[32,1,128]{2,1,0:T(1,128)}), f32[32,1,128]{2,1,0:T(1,128)S(1)}, u32[]{:S(2)}, u32[]{:S(2)}) async-start(f32[32,1,128]{2,1,0:T(1,128)} %copy-done.24), calls=%async_computation.3 | async-start | bytes 32768 | tf_op jit(solution)/shard_map/all_to_all | solution.py:1067

commit v3 on v2

--- a/solution.py
+++ b/solution.py
@@ -242,7 +242,7 @@
     )
 
 
-def ends_kernel(cells, place_ref, field_ref, mixer_ref, ratio_ref, order_ref, out_ref):
+def ends_kernel(cells, place_ref, field_ref, mixer_ref, ratio_ref, out_ref):
     slab, width, lanes = field_ref.shape
     depth = ratio_ref.shape[0]
     ratio = ratio_ref[...]
@@ -283,7 +283,7 @@
     return np.stack(mixers)
 
 
-def end_responses(field, order, place, groups):
+def end_responses(field, place, groups):
     slab, width, length = field.shape
     depth, lanes = slab * groups, length // groups
     cells = divisor_of(width, 8, 16)
@@ -297,7 +297,6 @@
                 pl.BlockSpec((slab, width, 2 * lanes), lambda i, p: (0, 0, i)),
                 pl.BlockSpec((1,) + mixers.shape[1:], lambda i, p: (p[0], 0, 0)),
                 pl.BlockSpec((depth, 2 * lanes), lambda i, p: (0, i)),
-                pl.BlockSpec(memory_space=pl.ANY),
             ],
             out_specs=pl.BlockSpec((2, 2, depth, lanes), lambda i, p: (i, 0, 0, 0)),
         ),
@@ -305,10 +304,10 @@
         compiler_params=params(),
         cost_estimate=cost(2 * mixers[0].size * length * (width // cells), field.size),
         name="end_responses",
-    )(place, in_hbm(field), mixers, decay_table(length, depth), order)
-
-
-def jumps_kernel(width, place_ref, ends_ref, ratio_ref, table_ref, order_ref, order_too_ref, out_ref):
+    )(place, in_hbm(field), mixers, decay_table(length, depth))
+
+
+def jumps_kernel(width, place_ref, ends_ref, ratio_ref, table_ref, out_ref):
     blocks = ends_ref.shape[0]
     here = place_ref[1]
     ratio = ratio_ref[0]
@@ -339,7 +338,7 @@
             out_ref[g, side] = levels
 
 
-def jumps(all_ends, orders, place, width, groups):
+def jumps(all_ends, place, width, groups):
     _, _, depth, lanes = all_ends.shape
     ratio = decay_table(lanes * groups, depth).reshape(depth, groups, lanes).transpose(1, 0, 2)
     out = (groups, 2, depth, lanes)
@@ -352,8 +351,6 @@
                 fixed(all_ends.shape),
                 pl.BlockSpec((1, depth, lanes), lambda i, p: (p[0], 0, 0)),
                 fixed((depth, depth)),
-                pl.BlockSpec(memory_space=pl.ANY),
-                pl.BlockSpec(memory_space=pl.ANY),
             ],
             out_specs=fixed(out),
         ),
@@ -361,7 +358,7 @@
         compiler_params=params(),
         cost_estimate=cost(20 * all_ends.size, all_ends.size),
         name="jumps",
-    )(place, all_ends, ratio, level_table(depth).T.astype(np.float32), *orders)
+    )(place, all_ends, ratio, level_table(depth).T.astype(np.float32))
 
 
 def border_kernel(rows, place_ref, jump_ref, nu_ref, mu_ref, ends_ref, order_ref, out_ref, *refs):
@@ -460,8 +457,8 @@
     return dot(high_ref[...], high) + (dot(high_ref[...], low) + dot(low_ref[...], high))
 
 
-def eliminate_kernel(place_ref, field_ref, ratio_ref, order_ref, high_ref, low_ref, *refs):
-    modes_ref, last_ref, outer_ref, through_ref, weight_ref = refs
+def eliminate_kernel(place_ref, field_ref, ratio_ref, high_ref, low_ref, *refs):
+    modes_ref, last_ref, outer_ref, through_ref, weight_ref = refs[-5:]
     t, steps = pl.program_id(0), pl.num_programs(0)
     modes = block_dot(high_ref, low_ref, field_ref[0])
     modes_ref[0] = modes
@@ -487,7 +484,7 @@
             through_ref[...] = weight_ref[...] * ratio
 
 
-def eliminate(field, ratios, order, place):
+def eliminate(field, ratios, orders, place):
     slab, width, length = field.shape
     lanes = length
     high, low = halves_of(cosine_table(width)[spectral_order(width)])
@@ -503,10 +500,10 @@
                     lambda t, p: (jnp.where(p[4] == 1, slab - 1 - t, t), 0, 0),
                 ),
                 pl.BlockSpec((1, width, lanes), lambda t, p: (t, 0, 0)),
-                pl.BlockSpec(memory_space=pl.ANY),
                 fixed(high.shape),
                 fixed(low.shape),
-            ],
+            ]
+            + [pl.BlockSpec(memory_space=pl.ANY)] * len(orders),
             out_specs=[pl.BlockSpec((1, width, lanes), lambda t, p: (t, 0, 0)), plane, plane, plane],
             scratch_shapes=[pltpu.VMEM((width, lanes), F32)],
         ),
@@ -514,7 +511,7 @@
         compiler_params=params(32),
         cost_estimate=cost(6 * width * field.size, 3 * field.size),
         name="eliminate",
-    )(place, in_hbm(field), in_hbm(ratios), order, high, low)
+    )(place, in_hbm(field), in_hbm(ratios), high, low, *orders)
 
 
 def substitute_kernel(place_ref, modes_ref, ratio_ref, prev_ratio_ref, in_ref, next_ref, back_ref, border_ref, order_ref, high_ref, low_ref, out_ref, kept):
@@ -575,7 +572,8 @@
     )
 
 
-def relay_kernel(last_ref, through_ref, in_ref, order_ref, out_ref):
+def relay_kernel(last_ref, through_ref, in_ref, *refs):
+    out_ref = refs[-1]
     out_ref[...] = last_ref[...] + through_ref[...] * in_ref[...]
 
 
@@ -583,7 +581,7 @@
     return divisor_of(width, 8, 48)
 
 
-def relay(last, through, incoming, order):
+def relay(last, through, incoming, orders):
     width, lanes = last.shape
     tile = row_tile(width)
     own = pl.BlockSpec((tile, lanes), lambda i: (i, 0))
@@ -594,14 +592,14 @@
             own,
             own,
             own,
-            pl.BlockSpec(memory_space=pl.ANY),
-        ],
+        ]
+        + [pl.BlockSpec(memory_space=pl.ANY)] * len(orders),
         out_specs=own,
         out_shape=jax.ShapeDtypeStruct(last.shape, F32),
         compiler_params=params(),
         cost_estimate=cost(2 * last.size, 4 * last.size),
         name="relay",
-    )(in_hbm(last), in_hbm(through), incoming, order)
+    )(in_hbm(last), in_hbm(through), incoming, *orders)
 
 
 def turn_kernel(slab, place_ref, mine_ref, theirs_ref, in_ref, outer_ref, next_ref, ratios_ref, *refs):
@@ -750,15 +748,38 @@
     return guess + guess
 
 
-def operator_kernel(n_dots, n_kept, with_levels, place_ref, density_ref, *refs):
-    if with_levels:
-        (f_low, f_low_prev, f_low_next, f_ref, f_prev, f_next), refs = refs[:6], refs[6:]
-    else:
-        (f_ref, f_prev, f_next, f_below, f_below_too), refs = refs[:5], refs[5:]
-    (f_lo, f_hi, d_ref, d_prev, d_next, d_below, d_lo, d_hi), refs = refs[:8], refs[8:]
-    dot_refs = refs[:n_dots]
-    face_ref, kept_ref, _, image_ref, out_sums_ref, out_face_ref = refs[n_dots : 6 + n_dots]
-    field, dense, before_ref, sums_ref = refs[6 + n_dots :]
+def next_row(following, mid):
+    row_ids = lax.broadcasted_iota(jnp.int32, mid.shape, 0)
+    return jnp.where(row_ids == 7, pltpu.roll(following, 7, 0), pltpu.roll(mid, 7, 0))
+
+
+def previous_row(carried_ref, level, after):
+    row_ids = lax.broadcasted_iota(jnp.int32, after.shape, 0)
+    shifted = pltpu.roll(after, 1, 0)
+    before = jnp.where(row_ids == 0, carried_ref[level], shifted)
+    carried_ref[level] = shifted
+    return before
+
+
+def pack_sums(out_ref, kept, first, sums_ref):
+    group_ids = lax.broadcasted_iota(jnp.int32, (1, 128), 1) // 16
+    packed = kept
+    for k in range(sums_ref.shape[0]):
+        line = jnp.sum(sums_ref[k], axis=0, keepdims=True)
+        line = sum(line[:, j : j + 128] for j in range(0, line.shape[1], 128))
+        for shift in (64, 32, 16):
+            line = line + pltpu.roll(line, shift, 1)
+        packed = jnp.where(group_ids == first + k, line, packed)
+    for k in range(out_ref.shape[0]):
+        out_ref[k] = packed
+
+
+def old_image_kernel(
+    place_ref, density_ref, f_ref, f_prev, f_next, f_below, f_below_too, f_lo, f_hi,
+    d_ref, d_prev, d_next, d_below, d_lo, d_hi, residual_ref, order_ref,
+    image_ref, out_sums_ref, out_face_ref, z_ref, x_ref, x_first_ref, y_ref,
+    field, dense, before_ref, sums_ref,
+):
     slab, tile, lanes = image_ref.shape
     step, steps = pl.program_id(0), pl.num_programs(0)
     at_left = jnp.logical_and(place_ref[2] == 1, step == 0)
@@ -770,96 +791,86 @@
         return fraction * gas + (1.0 - fraction) * liquid
 
     own = slice(8, 8 + tile)
-    if with_levels:
-        field[0:2, own] = f_low[...]
-        field[2:, own] = f_ref[...]
-    else:
-        field[0:1, own] = f_below[...] + f_below_too[...]
-        field[1:, own] = f_ref[...]
+    field[0:1, own] = f_below[...] + f_below_too[...]
+    field[1:, own] = f_ref[...]
     dense[1:, own] = mixed(d_ref[...])
     dense[0:1, own] = mixed(d_below[...])
 
     @pl.when(step == 0)
     def _():
-        field[1:, 7:8] = field[1:, 8:9] + f_lo[...] if with_levels else f_lo[...]
+        field[1:, 7:8] = f_lo[...]
         dense[1:, 7:8] = mixed(d_lo[...])
         sums_ref[...] = jnp.zeros_like(sums_ref)
 
     @pl.when(step > 0)
     def _():
-        if with_levels:
-            field[1:2, 7:8] = f_low_prev[1:2, 7:8]
-            field[2:, 7:8] = f_prev[:, 7:8]
-        else:
-            field[1:, 7:8] = f_prev[:, 7:8]
+        field[1:, 7:8] = f_prev[:, 7:8]
         dense[1:, 7:8] = mixed(d_prev[:, 7:8])
 
     @pl.when(step == steps - 1)
     def _():
-        last_row = field[1:, 7 + tile : 8 + tile]
-        field[1:, 8 + tile : 9 + tile] = last_row - f_hi[...] if with_levels else f_hi[...]
+        field[1:, 8 + tile : 9 + tile] = f_hi[...]
         dense[1:, 8 + tile : 9 + tile] = mixed(d_hi[...])
 
     @pl.when(step < steps - 1)
     def _():
-        if with_levels:
-            field[1:2, 8 + tile : 9 + tile] = f_low_next[1:2, 0:1]
-            field[2:, 8 + tile : 9 + tile] = f_next[:, 0:1]
-        else:
-            field[1:, 8 + tile : 9 + tile] = f_next[:, 0:1]
+        field[1:, 8 + tile : 9 + tile] = f_next[:, 0:1]
         dense[1:, 8 + tile : 9 + tile] = mixed(d_next[:, 0:1])
 
     lane_ids = lax.broadcasted_iota(jnp.int32, (8, lanes), 1)
     row_ids = lax.broadcasted_iota(jnp.int32, (8, lanes), 0)
     has_right = (lane_ids < lanes - 1).astype(F32)
 
-    def face(mid, rho, neighbour, rho_next):
-        return twice_inverse(rho + rho_next) * (mid - neighbour)
-
-    def next_row(ref, z, at, mid):
-        following = ref[z, pl.ds(at + 8, 8)]
-        return jnp.where(row_ids == 7, pltpu.roll(following, 7, 0), pltpu.roll(mid, 7, 0))
-
-    def face_after(z, at, mid, rho):
-        return face(mid, rho, next_row(field, z, at, mid), next_row(dense, z, at, rho))
+    def after_faces(z, at, mid, rho):
+        below = pl.ds(at + 8, 8)
+        coefficient = twice_inverse(rho + next_row(dense[z, below], rho))
+        return coefficient, mid - next_row(field[z, below], mid)
 
     for level in range(slab):
-        first = face_after(level + 1, 0, field[level + 1, 0:8], dense[level + 1, 0:8])
-        before_ref[level] = jnp.where(at_left, 0.0, pltpu.roll(first, 1, 0))
+        coefficient, drop = after_faces(level + 1, 0, field[level + 1, 0:8], dense[level + 1, 0:8])
+        coefficient = jnp.where(at_left, 0.0, coefficient)
+        before_ref[level] = pltpu.roll(jnp.where(at_left, 0.0, coefficient * drop), 1, 0)
+
+        @pl.when(step == 0)
+        def _(level=level, coefficient=coefficient):
+            x_first_ref[level] = jnp.where(row_ids == 7, coefficient, 0.0)
 
     def rows(i, carry):
         at = pl.multiple_of(8 + 8 * i, 8)
+        here = pl.ds(at, 8)
         own = pl.ds(pl.multiple_of(8 * i, 8), 8)
         at_end = jnp.logical_and(at_right, i == tile // 8 - 1)
-        mid, rho = field[0, pl.ds(at, 8)], dense[0, pl.ds(at, 8)]
-        up, rho_up = field[1, pl.ds(at, 8)], dense[1, pl.ds(at, 8)]
-        above = jnp.where(at_bottom, 0.0, face(mid, rho, up, rho_up))
+        mid, rho = field[0, here], dense[0, here]
+        up, rho_up = field[1, here], dense[1, here]
+        coefficient = jnp.where(at_bottom, 0.0, twice_inverse(rho + rho_up))
+        z_ref[0, own] = coefficient
+        above = coefficient * (mid - up)
         out_face_ref[0, own] = above
-        totals = [mid * above] + [jnp.zeros((8, lanes), F32)] * n_dots
-        if n_dots > 1:
-            totals[-1] = jnp.where(at_bottom, 0.0, mid * face_ref[0, own])
+        totals = [mid * above, jnp.zeros((8, lanes), F32)]
         for level in range(slab):
             below = above
             mid, rho = up, rho_up
             if level < slab - 1:
-                up, rho_up = field[level + 2, pl.ds(at, 8)], dense[level + 2, pl.ds(at, 8)]
-                above = face(mid, rho, up, rho_up)
+                up, rho_up = field[level + 2, here], dense[level + 2, here]
+                coefficient = twice_inverse(rho + rho_up)
+                above = coefficient * (mid - up)
             else:
-                above = jnp.where(at_top, twice_inverse(rho) * mid, 0.0)
-            after = face_after(level + 1, at, mid, rho)
-            after = jnp.where(jnp.logical_and(at_end, row_ids == 7), 0.0, after)
-            shifted = pltpu.roll(after, 1, 0)
-            before = jnp.where(row_ids == 0, before_ref[level], shifted)
-            before_ref[level] = shifted
-            right = has_right * face(
-                mid, rho, pltpu.roll(mid, lanes - 1, 1), pltpu.roll(rho, lanes - 1, 1)
-            )
+                coefficient = jnp.where(at_top, twice_inverse(rho), 0.0)
+                above = coefficient * mid
+            z_ref[level + 1, own] = coefficient
+            coefficient, drop = after_faces(level + 1, at, mid, rho)
+            coefficient = jnp.where(jnp.logical_and(at_end, row_ids == 7), 0.0, coefficient)
+            x_ref[level, own] = coefficient
+            after = coefficient * drop
+            before = previous_row(before_ref, level, after)
+            coefficient = has_right * twice_inverse(rho + pltpu.roll(rho, lanes - 1, 1))
+            y_ref[level, own] = coefficient
+            right = coefficient * (mid - pltpu.roll(mid, lanes - 1, 1))
             image = (above - below) + (after - before) + (right - pltpu.roll(right, 1, 1))
             image_ref[level, own] = image
             totals[0] = totals[0] + mid * image
-            for k in range(n_dots):
-                totals[k + 1] = totals[k + 1] + mid * dot_refs[k][level, own]
-        for k in range(n_dots + 1):
+            totals[1] = totals[1] + mid * residual_ref[level, own]
+        for k in range(2):
             sums_ref[k] += totals[k]
         return carry
 
@@ -867,73 +878,162 @@
 
     @pl.when(step == steps - 1)
     def _():
-        group_ids = lax.broadcasted_iota(jnp.int32, (1, 128), 1) // 16
-        packed = jnp.where(group_ids < n_kept, kept_ref[0], 0.0)
-        for k in range(n_dots + 1):
-            line = jnp.sum(sums_ref[k], axis=0, keepdims=True)
-            line = sum(line[:, j : j + 128] for j in range(0, lanes, 128))
-            for shift in (64, 32, 16):
-                line = line + pltpu.roll(line, shift, 1)
-            packed = jnp.where(group_ids == n_kept + k, line, packed)
-        for k in range(out_sums_ref.shape[0]):
-            out_sums_ref[k] = packed
-
-
-def apply_operator(fields, belows, sides, fraction, border, density, others, face, kept, n_kept, copies, order, place, name):
+        pack_sums(out_sums_ref, jnp.zeros((1, 128), F32), 0, sums_ref)
+
+
+def stencil_tile(width):
+    return divisor_of(width, 8, 48)
+
+
+def old_image(direction, belows, sides, fraction, fraction_below, density, residual, order, place):
     slab, width, lanes = fraction.shape
-    with_levels = len(fields) > 1
-    tile = divisor_of(width, 8, 48)
+    tile = stencil_tile(width)
     per = tile // 8
     last = width // 8 - 1
-
-    def triple(levels):
-        return [
-            pl.BlockSpec((levels, tile, lanes), lambda i, p: (0, i, 0)),
-            pl.BlockSpec((levels, 8, lanes), lambda i, p: (0, jnp.maximum(i * per - 1, 0), 0)),
-            pl.BlockSpec((levels, 8, lanes), lambda i, p: (0, jnp.minimum((i + 1) * per, last), 0)),
-        ]
-
     plane = pl.BlockSpec((1, tile, lanes), lambda i, p: (0, i, 0))
-
-    def borders(planes, *places):
-        return [plane] * planes + [
-            pl.BlockSpec((slab, 1, lanes), lambda i, p, k=k: (k, 0, 0)) for k in places
-        ]
-
     own = pl.BlockSpec((slab, tile, lanes), lambda i, p: (0, i, 0))
-    specs = [pl.BlockSpec(memory_space=pltpu.SMEM)]
-    for field in fields:
-        specs += triple(field.shape[0])
-    specs += borders(0, 0, 1) if with_levels else borders(2, 0, 0)
-    specs += triple(slab) + borders(1, 1, 1)
-    specs += [own] * len(others)
-    specs += [plane, fixed((1, 1, 128)), pl.BlockSpec(memory_space=pl.ANY)]
-    planes = slab * (3 + len(others)) + 1
-    operands = [field for field in fields for _ in range(3)] + ([] if with_levels else list(belows))
-    return pl.pallas_call(
-        functools.partial(operator_kernel, len(others), n_kept, with_levels),
+    triple = [
+        own,
+        pl.BlockSpec((slab, 8, lanes), lambda i, p: (0, jnp.maximum(i * per - 1, 0), 0)),
+        pl.BlockSpec((slab, 8, lanes), lambda i, p: (0, jnp.minimum((i + 1) * per, last), 0)),
+    ]
+
+    def side(k):
+        return [pl.BlockSpec((slab, 1, lanes), lambda i, p: (k, 0, 0))] * 2
+
+    specs = [pl.BlockSpec(memory_space=pltpu.SMEM)] + triple + [plane] * 2 + side(0)
+    specs += triple + [plane] + side(1) + [own, pl.BlockSpec(memory_space=pl.ANY)]
+    levels = pl.BlockSpec((slab + 1, tile, lanes), lambda i, p: (0, i, 0))
+    shape = (slab, width, lanes)
+    return pl.pallas_call(
+        old_image_kernel,
         grid_spec=pltpu.PrefetchScalarGridSpec(
             num_scalar_prefetch=1,
             grid=(width // tile,),
             in_specs=specs,
-            out_specs=[own, fixed((copies, 1, 128)), plane],
+            out_specs=[own, fixed((1, 1, 128)), plane, levels, own, fixed((slab, 8, lanes)), own],
             scratch_shapes=[pltpu.VMEM((slab + 1, tile + 16, lanes), F32)] * 2
-            + [
-                pltpu.VMEM((slab, 8, lanes), F32),
-                pltpu.VMEM((len(others) + 1, 8, lanes), F32),
-            ],
+            + [pltpu.VMEM((slab, 8, lanes), F32), pltpu.VMEM((2, 8, lanes), F32)],
         ),
         out_shape=[
-            hbm((slab, width, lanes)),
-            jax.ShapeDtypeStruct((copies, 1, 128), F32),
+            hbm(shape),
+            jax.ShapeDtypeStruct((1, 1, 128), F32),
             hbm((1, width, lanes)),
+            hbm((slab + 1, width, lanes)),
+            hbm(shape),
+            hbm((slab, 8, lanes)),
+            hbm(shape),
         ],
-        compiler_params=params(28),
-        cost_estimate=cost(100 * slab * width * lanes, planes * width * lanes),
-        name=name,
+        compiler_params=params(32),
+        cost_estimate=cost(100 * slab * width * lanes, 8 * slab * width * lanes),
+        name="old_image",
     )(
-        place, density, *operands, *sides,
-        fraction, fraction, fraction, *border, *others, face, kept, order,
+        place, density, direction, direction, direction, *belows, *sides,
+        fraction, fraction, fraction, fraction_below, *sides, residual, order,
+    )
+
+
+def new_image_kernel(
+    low_ref, low_next, high_ref, high_next, lo_ref, hi_ref, z_ref, x_ref, x_first_ref, y_ref,
+    residual_ref, old_ref, face_ref, kept_ref, image_ref, out_sums_ref, field, before_ref, sums_ref,
+):
+    slab, tile, lanes = image_ref.shape
+    step, steps = pl.program_id(0), pl.num_programs(0)
+    own = slice(8, 8 + tile)
+    field[0:2, own] = low_ref[...]
+    field[2:, own] = high_ref[...]
+
+    @pl.when(step == 0)
+    def _():
+        field[1:, 7:8] = field[1:, 8:9] + lo_ref[...]
+        sums_ref[...] = jnp.zeros_like(sums_ref)
+        for level in range(slab):
+            mid = field[level + 1, 0:8]
+            drop = mid - next_row(field[level + 1, 8:16], mid)
+            row_ids = lax.broadcasted_iota(jnp.int32, mid.shape, 0)
+            flux = jnp.where(row_ids == 7, x_first_ref[level] * drop, 0.0)
+            before_ref[level] = pltpu.roll(flux, 1, 0)
+
+    @pl.when(step == steps - 1)
+    def _():
+        field[1:, 8 + tile : 9 + tile] = field[1:, 7 + tile : 8 + tile] - hi_ref[...]
+
+    @pl.when(step < steps - 1)
+    def _():
+        field[1:2, 8 + tile : 9 + tile] = low_next[1:2, 0:1]
+        field[2:, 8 + tile : 9 + tile] = high_next[:, 0:1]
+
+    def rows(i, carry):
+        at = pl.multiple_of(8 + 8 * i, 8)
+        here = pl.ds(at, 8)
+        own = pl.ds(pl.multiple_of(8 * i, 8), 8)
+        mid, up = field[0, here], field[1, here]
+        above = z_ref[0, own] * (mid - up)
+        totals = [mid * above, jnp.zeros((8, lanes), F32), mid * face_ref[0, own]]
+        for level in range(slab):
+            below, mid = above, up
+            if level < slab - 1:
+                up = field[level + 2, here]
+                above = z_ref[level + 1, own] * (mid - up)
+            else:
+                above = z_ref[slab, own] * mid
+            after = x_ref[level, own] * (mid - next_row(field[level + 1, pl.ds(at + 8, 8)], mid))
+            before = previous_row(before_ref, level, after)
+            right = y_ref[level, own] * (mid - pltpu.roll(mid, lanes - 1, 1))
+            image = (above - below) + (after - before) + (right - pltpu.roll(right, 1, 1))
+            image_ref[level, own] = image
+            totals[0] = totals[0] + mid * image
+            totals[1] = totals[1] + mid * residual_ref[level, own]
+            totals[2] = totals[2] + mid * old_ref[level, own]
+        for k in range(3):
+            sums_ref[k] += totals[k]
+        return carry
+
+    lax.fori_loop(0, tile // 8, rows, 0)
+
+    @pl.when(step == steps - 1)
+    def _():
+        pack_sums(out_sums_ref, kept_ref[0], 2, sums_ref)
+
+
+def new_image(low, high, jump_rows, coefficients, residual, image_old, old_face, sums_old, copies):
+    slab, width, lanes = residual.shape
+    tile = stencil_tile(width)
+    per = tile // 8
+    last = width // 8 - 1
+
+    def pair(levels):
+        return [
+            pl.BlockSpec((levels, tile, lanes), lambda i: (0, i, 0)),
+            pl.BlockSpec((levels, 8, lanes), lambda i: (0, jnp.minimum((i + 1) * per, last), 0)),
+        ]
+
+    def side(k):
+        return pl.BlockSpec((slab, 1, lanes), lambda i: (k, 0, 0))
+
+    own = pl.BlockSpec((slab, tile, lanes), lambda i: (0, i, 0))
+    plane = pl.BlockSpec((1, tile, lanes), lambda i: (0, i, 0))
+    levels = pl.BlockSpec((slab + 1, tile, lanes), lambda i: (0, i, 0))
+    specs = pair(2) + pair(slab - 1) + [side(0), side(1), levels, own, fixed((slab, 8, lanes)), own]
+    specs += [own, own, plane, fixed((1, 1, 128))]
+    low, high = in_hbm(low), in_hbm(high)
+    return pl.pallas_call(
+        new_image_kernel,
+        grid=(width // tile,),
+        in_specs=specs,
+        out_specs=[own, fixed((copies, 1, 128))],
+        scratch_shapes=[
+            pltpu.VMEM((slab + 1, tile + 16, lanes), F32),
+            pltpu.VMEM((slab, 8, lanes), F32),
+            pltpu.VMEM((3, 8, lanes), F32),
+        ],
+        out_shape=[hbm((slab, width, lanes)), jax.ShapeDtypeStruct((copies, 1, 128), F32)],
+        compiler_params=params(32),
+        cost_estimate=cost(40 * slab * width * lanes, 8 * slab * width * lanes),
+        name="new_image",
+    )(
+        low, low, high, high, jump_rows, jump_rows, *[in_hbm(c) for c in coefficients],
+        in_hbm(residual), in_hbm(image_old), in_hbm(old_face), sums_old,
     )
 
 
@@ -1016,40 +1116,35 @@
     inward = [[(s - 1, s), (groups - s, groups - 1 - s)] for s in range(1, half)]
     outward = [[(j, i) for i, j in pairs] for pairs in reversed(inward)]
     across = [(half - 1, half), (half, half - 1)]
-    modes, last, outer, through = eliminate(spectral, ratios, fraction_below, place)
+    parts = end_responses(spectral, place, groups)
+    modes, last, outer, through = eliminate(spectral, ratios, (fraction_below, parts), place)
     zero = jnp.zeros_like(last)
-    parts = end_responses(spectral, last, place, groups)
-    late_top, parts = lax.optimization_barrier((top, parts))
+    ends = jnp.sum(lax.all_to_all(parts, "gz", 0, 0, tiled=True), axis=0)
+    late_top, ends = lax.optimization_barrier((top, ends))
     below_too = lax.ppermute(late_top, "gz", up[:1])
-    ends = jnp.sum(lax.all_to_all(parts, "gz", 0, 0, tiled=True), axis=0)
+    all_ends = lax.all_to_all(
+        jnp.broadcast_to(ends[None], (plane_parts,) + ends.shape), "xy", 0, 0, tiled=True
+    )
+    levels_jump = jumps(all_ends, place, width, groups)
+    all_jumps = lax.all_to_all(levels_jump, "gz", 0, 0, tiled=True)
     incoming, mine = zero, last
     for k, pairs in enumerate(inward):
         arrived = lax.ppermute(mine, "gz", pairs)
         incoming = incoming + arrived if k else arrived
-        mine = relay(last, through, incoming, below)
-    ends, mine = lax.optimization_barrier((ends, mine))
-    all_ends = lax.all_to_all(
-        jnp.broadcast_to(ends[None], (plane_parts,) + ends.shape), "xy", 0, 0, tiled=True
-    )
-    own_jumps = jumps(all_ends, sides, place, width, groups)
-    all_jumps = lax.all_to_all(own_jumps, "gz", 0, 0, tiled=True)
+        mine = relay(last, through, incoming, (below, levels_jump) + sides)
     theirs = lax.ppermute(mine, "gz", across)
-    orders = (below_too, all_jumps)
-    message, following = turn(mine, theirs, incoming, outer, zero, ratios, orders, place, 0)
+    message, following = turn(mine, theirs, incoming, outer, zero, ratios, (below_too,), place, 0)
     back = zero
     for k, pairs in enumerate(outward):
         if k:
             message, following = turn(
-                mine, theirs, incoming, outer, following + back, ratios, orders, place, 0
+                mine, theirs, incoming, outer, following + back, ratios, (below_too,), place, 0
             )
         back = lax.ppermute(message, "gz", pairs)
 
-    belows = (below, below_too)
-    border = (fraction_below,) + sides
-    nothing = jnp.zeros((1, 1, 128), F32)
-    image_old, sums_old, old_face = apply_operator(
-        [in_hbm(direction)], belows, sides, in_hbm(volume_fraction), border, density,
-        [in_hbm(residual)], below, nothing, 0, 1, message, place, "image_old"
+    image_old, sums_old, old_face, *coefficients = old_image(
+        in_hbm(direction), (below, below_too), sides, in_hbm(volume_fraction), fraction_below,
+        density, in_hbm(residual), message, place
     )
     old_above = lax.ppermute(old_face, "gz", down)
     jumped = border_solve(all_jumps, message, place, width, length, slab)
@@ -1059,10 +1154,9 @@
         in_hbm(volume_fraction), density, place, width
     )
     new_above = lax.ppermute(new_face, "gz", down)
-    image_new, sums, _ = apply_operator(
-        [in_hbm(precond_low), in_hbm(precond_high)], belows, (jump_rows, jump_rows),
-        in_hbm(volume_fraction), border, density, [in_hbm(residual), in_hbm(image_old)],
-        in_hbm(old_face), sums_old, 2, groups * plane_parts, sums_old, place, "image_new"
+    image_new, sums = new_image(
+        precond_low, precond_high, jump_rows, coefficients, residual, image_old, old_face, sums_old,
+        groups * plane_parts
     )
     gathered = lax.all_to_all(sums, ("gz", "xy"), 0, 0, tiled=True)
     new_solution, new_residual, new_direction = update(

time: 239 us -> 269 us (1.13)
  blocking collectives: 0 us -> 27.5 us
  starting transfers between devices: 46.4 us -> 54.8 us
  waiting for transfers between devices: 34.4 us -> 29.8 us
    all_to_all x0 -> x1, blocking collectives: none -> 27.5 us  [body(): ends = jnp.sum(lax.all_to_all(parts, 'gz', 0, 0, tiled=True), axis=0)]
    ppermute x1, waiting for transfers between devices: 0.01 us -> 14.6 us  [body(): below_too = lax.ppermute(late_top, 'gz', up[:1])]
    all_to_all x2 -> x1, waiting for transfers between devices: 15.2 us -> 4.37 us  [body(): all_jumps = lax.all_to_all(levels_jump, 'gz', 0, 0, tiled=True)]
    all_to_all x2 -> x1, starting transfers between devices: 9.19 us -> 19.1 us  [body(): all_jumps = lax.all_to_all(levels_jump, 'gz', 0, 0, tiled=True)]
    ppermute x1, waiting for transfers between devices: 3.12 us -> 0.01 us  [body(): fraction_below = lax.ppermute(fraction_top, 'gz', up)]
    all_to_all x1, starting transfers between devices: 7.46 us -> 4.56 us  [body(): gathered = lax.all_to_all(sums, ('gz', 'xy'), 0, 0, tiled=True)]
    unnamed x58 -> x42, local copies, waits for them, and re-layouts: 8.93 us -> 6.44 us
  transfers between devices with their start and end apart: 14 -> 13, of which waited for: 7 -> 4; matrix products, arithmetic and copies ran while one was open for 1% -> 1% of each run, Pallas kernels for 49% -> 44%
where the time goes in v3:
time: 269 us; the launch traced here: 267 us
  Pallas kernels  143 us (53%)
  starting transfers between devices  54.8 us (20%)
  waiting for transfers between devices  29.8 us (11%)
  blocking collectives  27.5 us (10%)
  local copies, waits for them, and re-layouts  8.82 us (3%)
    all_to_all x1, blocking collectives, body(): ends = jnp.sum(lax.all_to_all(parts, 'gz', 0, 0, tiled=True), axis=0)  27.5 us
    pallas_call x1, Pallas kernels, old_image(): pl.pallas_call(old_image_kernel, grid_spec=pltpu.PrefetchScalarGridSpec(n...  19.2 us
    all_to_all x1, starting transfers between devices, body(): all_jumps = lax.all_to_all(levels_jump, 'gz', 0, 0, tiled=True)  19.1 us
    pallas_call x1, Pallas kernels, update(): pl.pallas_call(update_kernel, grid=(width // tile,), in_specs=[fixed(sums...  15.9 us
    pallas_call x1, Pallas kernels, new_image(): pl.pallas_call(new_image_kernel, grid=(width // tile,), in_specs=specs, o...  14.6 us
    ppermute x1, waiting for transfers between devices, body(): below_too = lax.ppermute(late_top, 'gz', up[:1])  14.6 us
    pallas_call x1, Pallas kernels, forward_rows(): pl.pallas_call(forward_kernel, grid=(count // tile,), in_specs=[pl.BlockS...  11.7 us
    pallas_call x1, Pallas kernels, border_solve(): pl.pallas_call(functools.partial(border_kernel, rows), grid_spec=pltpu.Pr...  11 us
  transfers between devices with their start and end apart: 13, of which 4 were waited for; matrix products, arithmetic and copies ran while one was open for 1% of the time, Pallas kernels for 44%

profile of v3, /device:TPU:0, one launch (start us, length us, event | category | flops | bytes accessed | tf_op | source)
XLA Modules:
  0.0 267.4 jit_solution(5156130853593296652)
XLA Ops:
  0.6 0.0 copy-start.5
  0.7 3.3 %cut_borders.1 = (f32[1,192,1536]{2,1,0:T(8,128)}, f32[1,192,1536]{2,1,0:T(8,128)}, f32[8,1,1536]{2,1,0:T(1,128)S(1)}, f32[8,1,1536]{2,1,0:T(1,128)S(1)}) custom-call(f32[4,192,1536]{2,1,0:T(8,128)} %direction_ref.1, f32[4,192,1536]{2,1,0:T(8,128)} %refs_3_.1, f32[4,192,1536]{2,1,0:T(8,128)} %direction_ref.1, f32[4,192,1536]{2,1,0:T(8,128)} %refs_3_.1, ...), custom_call_target="tpu_custom_call" | custom-call | bytes 294912 | tf_op jit(solution)/shard_map/cut_borders/pallas_call | solution.py:728
  4.0 0.6 copy-done.19
  4.6 0.6 copy-done.20
  5.2 4.9 %collective-permute-start = (f32[1,192,1536]{2,1,0:T(8,128)}, f32[1,192,1536]{2,1,0:T(8,128)S(1)}, u32[]{:S(2)}, u32[]{:S(2)}) collective-permute-start(f32[1,192,1536]{2,1,0:T(8,128)} %get-tuple-element.27), channel_id=1, source_target_pairs={{0,8},{8,16},{16,24},{1,9},{9,17},{17,25},{2,10},{10,18},{18,26},{... | collective-permute-start | bytes 3538952 | tf_op jit(solution)/shard_map/ppermute | solution.py:1109
  10.2 0.7 collective-permute-start.2
  10.9 0.6 fusion
  12.9 0.1 stack.63.place_ref
  13.0 7.8 %ratios.1.ratio_ref.ratios_ref.prev_ratio_ref = f32[6,192,1536]{2,1,0:T(8,128)} custom-call(s32[9]{0:T(128)S(1)} %stack.63.place_ref, f32[192,1]{1,0:T(8,128)S(1)} %copy-done.5, f32[1,1536]{1,0:T(1,128)S(1)} %copy-done.14), custom_call_target="tpu_custom_call" | custom-call | flops 2211840 | bytes 442368 | tf_op jit(solution)/shard_map/ratios/pallas_call | solution.py:696
  20.8 11.7 %forward_rows.1 = f32[768,1536]{1,0:T(8,128)} custom-call(f32[1]{0:T(128)S(6)} %div.14.scale_ref, f32[768,1536]{1,0:T(8,128)} %bitcast.18, bf16[2,768,768]{2,1,0:T(8,128)(2,1)} %constant.60.clone.high_ref, bf16[2,768,768]{2,1,0:T(8,128)(2,1)} %constant.61.clone.low_ref, bf16[256,256]{1,0:T(8,128)(2,1)S(1)} %copy-done.1), custom_call_target="tpu_custom_call" | custom-call | flops 339738624 | bytes 589824 | tf_op jit(solution)/shard_map/forward_rows/pallas_call | solution.py:136
  32.5 7.3 %end_responses.1.refs_1_ = f32[4,2,16,384]{3,2,1,0:T(8,128)S(1)} custom-call(s32[9]{0:T(128)S(1)} %stack.63.place_ref, f32[4,192,1536]{2,1,0:T(8,128)} %bitcast.22, bf16[4,256,192]{2,1,0:T(8,128)(2,1)S(1)} %copy-done.4, f32[16,1536]{1,0:T(8,128)S(1)} %copy-done.11), custom_call_target="tpu_custom_call" | custom-call | flops 113246208 | bytes 294912 | tf_op jit(solution)/shard_map/end_responses/pallas_call | solution.py:291
  39.9 9.9 %eliminate.1 = (f32[4,192,1536]{2,1,0:T(8,128)}, f32[192,1536]{1,0:T(8,128)}, f32[192,1536]{1,0:T(8,128)}, f32[192,1536]{1,0:T(8,128)}) custom-call(s32[9]{0:T(128)S(1)} %stack.63.place_ref, f32[4,192,1536]{2,1,0:T(8,128)} %bitcast.23, f32[6,192,1536]{2,1,0:T(8,128)} %ratios.1.ratio_ref.ratios_ref.prev_ratio_ref, bf16[192,192]{1,0:T(8,128)(2,1)S(1)} %copy-done.13, ...), custom_call_target="tpu_custom_call" | custom-call | flops 84934656 | bytes 884736 | tf_op jit(solution)/shard_map/eliminate/pallas_call | solution.py:492
  49.8 6.9 %collective-permute-start.1 = (f32[192,1536]{1,0:T(8,128)}, f32[192,1536]{1,0:T(8,128)S(1)}, u32[]{:S(2)}, u32[]{:S(2)}) collective-permute-start(f32[192,1536]{1,0:T(8,128)} %get-tuple-element.29.last_ref), channel_id=1, source_target_pairs={{0,8},{24,16},{1,9},{25,17},{2,10},{26,18},{3,11},{27,19},{4,12},{... | collective-permute-start | bytes 3538952 | tf_op jit(solution)/shard_map/ppermute | solution.py:1132
  56.7 27.5 %all_to_all.20 = f32[4,2,16,384]{3,2,1,0:T(8,128)} all-to-all(f32[4,2,16,384]{3,2,1,0:T(8,128)S(1)} %end_responses.1.refs_1_), channel_id=1, replica_groups=mesh['gz'=4,'xy'=8] {'gz'}, dimensions={0} | all-to-all | bytes 393216 | tf_op jit(solution)/shard_map/all_to_all | solution.py:1122
  84.2 1.6 reduce_sum.9
  85.8 1.6 broadcast_in_dim.4
  87.4 4.9 %all-to-all-start.1 = ((f32[8,2,16,384]{3,2,1,0:T(8,128)}), f32[8,2,16,384]{3,2,1,0:T(8,128)}, u32[]{:S(2)}, u32[]{:S(2)}) async-start(f32[8,2,16,384]{3,2,1,0:T(8,128)} %broadcast_in_dim.4), calls=%async_computation.1 | async-start | bytes 786432 | tf_op jit(solution)/shard_map/all_to_all | solution.py:1125
  92.3 3.0 %collective-permute-start.3 = (f32[8,1,1536]{2,1,0:T(1,128)}, f32[8,1,1536]{2,1,0:T(1,128)}, u32[]{:S(2)}, u32[]{:S(2)}) collective-permute-start(f32[8,1,1536]{2,1,0:T(1,128)} %copy-done.20), channel_id=1, source_target_pairs={{0,1},{1,2},{2,3},{3,4},{4,5},{5,6},{6,7},{8,9},{9,10},{10,11},{11... | collective-permute-start | bytes 147464 | tf_op jit(solution)/shard_map/ppermute | solution.py:1111
  95.3 1.3 collective-permute-start.4
  96.6 4.7 %collective-permute-start.6 = (f32[1,192,1536]{2,1,0:T(8,128)}, f32[1,192,1536]{2,1,0:T(8,128)}, u32[]{:S(2)}, u32[]{:S(2)}) collective-permute-start(f32[1,192,1536]{2,1,0:T(8,128)} %get-tuple-element.36), channel_id=1, source_target_pairs={{0,8},{1,9},{2,10},{3,11},{4,12},{5,13},{6,14},{7,15}} | collective-permute-start | bytes 3538952 | tf_op jit(solution)/shard_map/ppermute | solution.py:1124
  101.3 3.7 %all-to-all-done.1.ends_ref = f32[8,2,16,384]{3,2,1,0:T(8,128)} async-done(((f32[8,2,16,384]{3,2,1,0:T(8,128)}), f32[8,2,16,384]{3,2,1,0:T(8,128)}, u32[]{:S(2)}, u32[]{:S(2)}) %all-to-all-start.1) | async-done | bytes 393248 | tf_op jit(solution)/shard_map/all_to_all | solution.py:1125
  104.9 0.9 copy-done.10
  105.8 0.7 copy-done.16
  106.5 1.8 jumps.1.refs_1_
  108.4 0.0 collective-permute-done.3.refs_2_.f_lo.d_lo
  108.4 2.5 relay.1.mine_ref
  110.9 0.7 collective-permute-start.5
  111.6 14.6 %collective-permute-done.6.refs_0_.f_below_too = f32[1,192,1536]{2,1,0:T(8,128)} collective-permute-done((f32[1,192,1536]{2,1,0:T(8,128)}, f32[1,192,1536]{2,1,0:T(8,128)}, u32[]{:S(2)}, u32[]{:S(2)}) %collective-permute-start.6) | collective-permute-done | bytes 1179680 | tf_op jit(solution)/shard_map/ppermute | solution.py:1124
  126.2 0.1 broadcast_in_dim.10.next_ref
  126.4 6.1 %turn.1 = (f32[192,1536]{1,0:T(8,128)}, f32[192,1536]{1,0:T(8,128)}) custom-call(s32[9]{0:T(128)S(1)} %stack.63.place_ref, f32[192,1536]{1,0:T(8,128)S(1)} %relay.1.mine_ref, f32[192,1536]{1,0:T(8,128)S(1)} %collective-permute-done.5.theirs_ref, f32[192,1536]{1,0:T(8,128)S(1)} %collective-permute-done.1.in_ref, f32[192,1536]{1,0:T(8,128)} %get-tuple-element.35.outer_ref, ...), custom_call_target="tpu_custom_call" | custom-call | flops 221184 | bytes 884736 | tf_op jit(solution)/shard_map/turn/pallas_call | solution.py:630
  132.5 1.3 collective-permute-start.7
  133.8 19.1 %all-to-all-start.2 = ((f32[4,2,16,384]{3,2,1,0:T(8,128)}), f32[4,2,16,384]{3,2,1,0:T(8,128)}, u32[]{:S(2)}, u32[]{:S(2)}) async-start(f32[4,2,16,384]{3,2,1,0:T(8,128)} %copy-done), calls=%async_computation.2 | async-start | bytes 393216 | tf_op jit(solution)/shard_map/all_to_all | solution.py:1129
  152.8 19.2 %old_image.1 = (f32[4,192,1536]{2,1,0:T(8,128)}, f32[1,1,128]{2,1,0:T(1,128)S(1)}, f32[1,192,1536]{2,1,0:T(8,128)}, f32[5,192,1536]{2,1,0:T(8,128)}, f32[4,192,1...) custom-call(s32[9]{0:T(128)S(1)} %stack.63.place_ref, f32[2]{0:T(128)S(1)} %copy-done.15, ...), custom_call_target="tpu_custom_call" | custom-call | flops 7372800 | bytes 2359296 | tf_op jit(solution)/shard_map/old_image/pallas_call | solution.py:908
  172.0 0.5 copy-done.17
  172.5 1.5 collective-permute-start.8
  174.0 4.4 %all-to-all-done.2.jump_ref.refs_0_.refs_1_ = f32[4,2,16,384]{3,2,1,0:T(8,128)} async-done(((f32[4,2,16,384]{3,2,1,0:T(8,128)}), f32[4,2,16,384]{3,2,1,0:T(8,128)}, u32[]{:S(2)}, u32[]{:S(2)}) %all-to-all-start.2) | async-done | bytes 196640 | tf_op jit(solution)/shard_map/all_to_all | solution.py:1129
  178.4 0.9 copy-done.6
  179.3 0.9 copy-done.9
  180.2 11.0 %border_solve.1.border_ref = f32[5,192,1536]{2,1,0:T(8,128)S(1)} custom-call(s32[9]{0:T(128)S(1)} %stack.63.place_ref, f32[4,2,16,384]{3,2,1,0:T(8,128)} %all-to-all-done.2.jump_ref.refs_0_.refs_1_, f32[192,1]{1,0:T(8,128)S(1)} %copy-done.6, f32[1,1536]{1,0:T(1,128)S(1)} %copy-done.14, f32[192,1]{1,0:T(8,128)S(1)} %copy-done.9, ...), custom_call_target="tpu_custom_call" | custom-call | flops 5898240 | bytes 368640 | tf_op jit(solution)/shard_map/border_solve/pallas_call | solution.py:429
  191.2 1.3 copy-done.3
  192.5 9.9 %substitute.1 = f32[5,192,1536]{2,1,0:T(8,128)} custom-call(s32[9]{0:T(128)S(1)} %stack.63.place_ref, f32[4,192,1536]{2,1,0:T(8,128)} %get-tuple-element.28.modes_ref, f32[6,192,1536]{2,1,0:T(8,128)} %ratios.1.ratio_ref.ratios_ref.prev_ratio_ref, f32[6,192,1536]{2,1,0:T(8,128)} %ratios.1.ratio_ref.ratios_ref.prev_ratio_ref, ...), custom_call_target="tpu_custom_call" | custom-call | flops 127401984 | bytes 1179648 | tf_op jit(solution)/shard_map/substitute/pallas_call | solution.py:545
  202.3 10.8 %inverse_lower.1 = (f32[384,1536]{1,0:T(8,128)}, f32[8,1,1536]{2,1,0:T(1,128)S(1)}, f32[1,192,1536]{2,1,0:T(8,128)}) custom-call(s32[9]{0:T(128)S(1)} %stack.63.place_ref, f32[2]{0:T(128)S(1)} %copy-done.15, f32[960,1536]{1,0:T(8,128)} %bitcast.14, f32[960,1536]{1,0:T(8,128)} %bitcast.15, bf16[2,768,768]{2,1,0:T(8,128)(2,1)} %constant.74.clone.high_ref, ...), custom_call_target="tpu_custom_call" | custom-call | flops 198180864 | bytes 294912 | tf_op jit(solution)/shard_map/inverse_lower/pallas_call | solution.py:204
  213.1 1.3 collective-permute-start.9
  214.4 10.7 %inverse_upper.1 = f32[576,1536]{1,0:T(8,128)} custom-call(s32[9]{0:T(128)S(1)} %stack.63.place_ref, f32[2]{0:T(128)S(1)} %copy-done.15, f32[960,1536]{1,0:T(8,128)} %bitcast.16, f32[960,1536]{1,0:T(8,128)} %bitcast.17, bf16[2,768,768]{2,1,0:T(8,128)(2,1)} %constant.74.clone.high_ref, bf16[2,768,768]{2,1,0:T(8,128)(2,1)} %constant.75.clone.low_ref, ...), custom_call_target="tpu_custom_call" | custom-call | flops 297271296 | bytes 442368 | tf_op jit(solution)/shard_map/inverse_upper/pallas_call | solution.py:227
  225.1 14.6 %new_image.1 = (f32[4,192,1536]{2,1,0:T(8,128)}, f32[32,1,128]{2,1,0:T(1,128)}) custom-call(f32[2,192,1536]{2,1,0:T(8,128)} %bitcast.24, f32[2,192,1536]{2,1,0:T(8,128)} %bitcast.25, f32[3,192,1536]{2,1,0:T(8,128)} %bitcast.19, f32[3,192,1536]{2,1,0:T(8,128)} %bitcast.20, f32[8,1,1536]{2,1,0:T(1,128)S(1)} %get-tuple-element.41.lo_ref.hi_ref, ...), custom_call_target="tpu_custom_call" | custom-call | flops 2949120 | bytes 2359296 | tf_op jit(solution)/shard_map/new_image/pallas_call | solution.py:1020
  239.8 4.6 %all-to-all-start.3 = ((f32[32,1,128]{2,1,0:T(1,128)}), f32[32,1,128]{2,1,0:T(1,128)S(1)}, u32[]{:S(2)}, u32[]{:S(2)}) async-start(f32[32,1,128]{2,1,0:T(1,128)} %get-tuple-element.48), calls=%async_computation.3 | async-start | bytes 32768 | tf_op jit(solution)/shard_map/all_to_all | solution.py:1161
  244.3 7.1 %all-to-all-done.3.sums_ref = f32[32,1,128]{2,1,0:T(1,128)S(1)} async-done(((f32[32,1,128]{2,1,0:T(1,128)}), f32[32,1,128]{2,1,0:T(1,128)S(1)}, u32[]{:S(2)}, u32[]{:S(2)}) %all-to-all-start.3) | async-done | bytes 16416 | tf_op jit(solution)/shard_map/all_to_all | solution.py:1161
  251.5 15.9 %update.1 = (f32[4,192,1536]{2,1,0:T(8,128)}, f32[4,192,1536]{2,1,0:T(8,128)}, f32[4,192,1536]{2,1,0:T(8,128)}) custom-call(f32[32,1,128]{2,1,0:T(1,128)S(1)} %all-to-all-done.3.sums_ref, f32[2,192,1536]{2,1,0:T(8,128)} %bitcast.26, f32[3,192,1536]{2,1,0:T(8,128)} %bitcast.21, f32[4,192,1536]{2,1,0:T(8,128)} %direction_ref.1, f32[4,192,1536]{2,1,0:T(8,128)} %solution_ref.1, ...), custom_call_target="tpu_custom_call" | custom-call | flops 737280 | bytes 2949120 | tf_op jit(solution)/shard_map/update/pallas_call | solution.py:1073
  (41 shorter events, 0.1 us)
Async XLA Ops:
  0.6 12.4 %copy-start.5 = (f32[192,1]{1,0:T(8,128)S(1)}, f32[192,1]{1,0:T(8,128)}, u32[]{:S(2)}) copy-start(f32[192,1]{1,0:T(8,128)} %constant.63.clone.nu_ref) | copy-start | bytes 2308
  0.6 12.4 %copy-start.14 = (f32[1,1536]{1,0:T(1,128)S(1)}, f32[1,1536]{1,0:T(1,128)}, u32[]{:S(2)}) copy-start(f32[1,1536]{1,0:T(1,128)} %constant.64.clone.mu_ref) | copy-start | bytes 18436
  0.7 10.3 %copy-start.15 = (f32[2]{0:T(128)S(1)}, f32[2]{0:T(128)}, u32[]{:S(2)}) copy-start(f32[2]{0:T(128)} %density_ref.5) | copy-start | bytes 28
  4.0 0.6 copy-start.19
  4.6 0.6 copy-start.20
  5.2 34.6 %collective-permute-start = (f32[1,192,1536]{2,1,0:T(8,128)}, f32[1,192,1536]{2,1,0:T(8,128)S(1)}, u32[]{:S(2)}, u32[]{:S(2)}) collective-permute-start(f32[1,192,1536]{2,1,0:T(8,128)} %get-tuple-element.27), channel_id=1, source_target_pairs={{0,8},{8,16},{16,24},{1,9},{9,17},{17,25},{2,10},{10,18},{18,26},{... | collective-permute-start | bytes 3538952 | tf_op jit(solution)/shard_map/ppermute | solution.py:1109
  10.2 98.2 %collective-permute-start.2 = (f32[1,192,1536]{2,1,0:T(8,128)}, f32[1,192,1536]{2,1,0:T(8,128)S(1)}, u32[]{:S(2)}, u32[]{:S(2)}) collective-permute-start(f32[1,192,1536]{2,1,0:T(8,128)} %get-tuple-element.36), channel_id=1, source_target_pairs={{8,16},{16,24},{9,17},{17,25},{10,18},{18,26},{11,19},{19,27},{12,... | collective-permute-start | bytes 3538952 | tf_op jit(solution)/shard_map/ppermute | solution.py:1110
  13.0 7.8 %copy-start.1 = (bf16[256,256]{1,0:T(8,128)(2,1)S(1)}, bf16[256,256]{1,0:T(8,128)(2,1)}, u32[]{:S(2)}) copy-start(bf16[256,256]{1,0:T(8,128)(2,1)} %constant.62.clone.flip_ref) | copy-start | bytes 393220
  20.8 11.7 %copy-start.4 = (bf16[4,256,192]{2,1,0:T(8,128)(2,1)S(1)}, bf16[4,256,192]{2,1,0:T(8,128)(2,1)}, u32[]{:S(2)}) copy-start(bf16[4,256,192]{2,1,0:T(8,128)(2,1)} %constant.65.clone.mixer_ref) | copy-start | bytes 1179652
  20.8 11.7 %copy-start.11 = (f32[16,1536]{1,0:T(8,128)S(1)}, f32[16,1536]{1,0:T(8,128)}, u32[]{:S(2)}) copy-start(f32[16,1536]{1,0:T(8,128)} %constant.66.clone.ratio_ref) | copy-start | bytes 294916
  32.5 7.4 %copy-start.12 = (bf16[192,192]{1,0:T(8,128)(2,1)S(1)}, bf16[192,192]{1,0:T(8,128)(2,1)}, u32[]{:S(2)}) copy-start(bf16[192,192]{1,0:T(8,128)(2,1)} %constant.68.clone.low_ref) | copy-start | bytes 221188
  32.5 7.4 %copy-start.13 = (bf16[192,192]{1,0:T(8,128)(2,1)S(1)}, bf16[192,192]{1,0:T(8,128)(2,1)}, u32[]{:S(2)}) copy-start(bf16[192,192]{1,0:T(8,128)(2,1)} %constant.67.clone.high_ref) | copy-start | bytes 221188
  49.8 58.6 %collective-permute-start.1 = (f32[192,1536]{1,0:T(8,128)}, f32[192,1536]{1,0:T(8,128)S(1)}, u32[]{:S(2)}, u32[]{:S(2)}) collective-permute-start(f32[192,1536]{1,0:T(8,128)} %get-tuple-element.29.last_ref), channel_id=1, source_target_pairs={{0,8},{24,16},{1,9},{25,17},{2,10},{26,18},{3,11},{27,19},{4,12},{... | collective-permute-start | bytes 3538952 | tf_op jit(solution)/shard_map/ppermute | solution.py:1132
  87.4 17.5 %all-to-all-start.1 = ((f32[8,2,16,384]{3,2,1,0:T(8,128)}), f32[8,2,16,384]{3,2,1,0:T(8,128)}, u32[]{:S(2)}, u32[]{:S(2)}) async-start(f32[8,2,16,384]{3,2,1,0:T(8,128)} %broadcast_in_dim.4), calls=%async_computation.1 | async-start | bytes 786432 | tf_op jit(solution)/shard_map/all_to_all | solution.py:1125
  92.3 16.1 %collective-permute-start.3 = (f32[8,1,1536]{2,1,0:T(1,128)}, f32[8,1,1536]{2,1,0:T(1,128)}, u32[]{:S(2)}, u32[]{:S(2)}) collective-permute-start(f32[8,1,1536]{2,1,0:T(1,128)} %copy-done.20), channel_id=1, source_target_pairs={{0,1},{1,2},{2,3},{3,4},{4,5},{5,6},{6,7},{8,9},{9,10},{10,11},{11... | collective-permute-start | bytes 147464 | tf_op jit(solution)/shard_map/ppermute | solution.py:1111
  95.3 13.1 %collective-permute-start.4 = (f32[8,1,1536]{2,1,0:T(1,128)}, f32[8,1,1536]{2,1,0:T(1,128)}, u32[]{:S(2)}, u32[]{:S(2)}) collective-permute-start(f32[8,1,1536]{2,1,0:T(1,128)} %copy-done.19), channel_id=1, source_target_pairs={{1,0},{2,1},{3,2},{4,3},{5,4},{6,5},{7,6},{9,8},{10,9},{11,10},{12... | collective-permute-start | bytes 147464 | tf_op jit(solution)/shard_map/ppermute | solution.py:1111
  96.6 29.7 %collective-permute-start.6 = (f32[1,192,1536]{2,1,0:T(8,128)}, f32[1,192,1536]{2,1,0:T(8,128)}, u32[]{:S(2)}, u32[]{:S(2)}) collective-permute-start(f32[1,192,1536]{2,1,0:T(8,128)} %get-tuple-element.36), channel_id=1, source_target_pairs={{0,8},{1,9},{2,10},{3,11},{4,12},{5,13},{6,14},{7,15}} | collective-permute-start | bytes 3538952 | tf_op jit(solution)/shard_map/ppermute | solution.py:1124
  104.9 0.9 copy-start.10
  105.8 0.7 copy-start.16
  108.3 2.5 copy-start
  110.9 15.3 %collective-permute-start.5 = (f32[192,1536]{1,0:T(8,128)S(1)}, f32[192,1536]{1,0:T(8,128)S(1)}, u32[]{:S(2)}, u32[]{:S(2)}) collective-permute-start(f32[192,1536]{1,0:T(8,128)S(1)} %relay.1.mine_ref), channel_id=1, source_target_pairs={{8,16},{16,8},{9,17},{17,9},{10,18},{18,10},{11,19},{19,11},{12,20... | collective-permute-start | bytes 3538952 | tf_op jit(solution)/shard_map/ppermute | solution.py:1135
  132.5 58.7 %collective-permute-start.7 = (f32[192,1536]{1,0:T(8,128)}, f32[192,1536]{1,0:T(8,128)}, u32[]{:S(2)}, u32[]{:S(2)}) collective-permute-start(f32[192,1536]{1,0:T(8,128)} %get-tuple-element.38.order_ref), channel_id=1, source_target_pairs={{8,0},{16,24},{9,1},{17,25},{10,2},{18,26},{11,3},{19,27},{12,4},{... | collective-permute-start | bytes 3538952 | tf_op jit(solution)/shard_map/ppermute | solution.py:1143
  133.8 44.6 %all-to-all-start.2 = ((f32[4,2,16,384]{3,2,1,0:T(8,128)}), f32[4,2,16,384]{3,2,1,0:T(8,128)}, u32[]{:S(2)}, u32[]{:S(2)}) async-start(f32[4,2,16,384]{3,2,1,0:T(8,128)} %copy-done), calls=%async_computation.2 | async-start | bytes 393216 | tf_op jit(solution)/shard_map/all_to_all | solution.py:1129
  172.0 0.5 copy-start.17
  172.5 71.8 %collective-permute-start.8 = (f32[1,192,1536]{2,1,0:T(8,128)}, f32[1,192,1536]{2,1,0:T(8,128)}, u32[]{:S(2)}, u32[]{:S(2)}) collective-permute-start(f32[1,192,1536]{2,1,0:T(8,128)} %get-tuple-element.47.face_ref), channel_id=1, source_target_pairs={{8,0},{16,8},{24,16},{9,1},{17,9},{25,17},{10,2},{18,10},{26,18},{... | collective-permute-start | bytes 3538952 | tf_op jit(solution)/shard_map/ppermute | solution.py:1149
  178.4 0.9 copy-start.6
  179.3 0.9 copy-start.9
  180.1 11.0 %copy-start.7 = (bf16[192,192]{1,0:T(8,128)(2,1)S(1)}, bf16[192,192]{1,0:T(8,128)(2,1)}, u32[]{:S(2)}) copy-start(bf16[192,192]{1,0:T(8,128)(2,1)} %constant.73.clone.low_ref) | copy-start | bytes 221188
  180.2 11.0 %copy-start.8 = (bf16[192,192]{1,0:T(8,128)(2,1)S(1)}, bf16[192,192]{1,0:T(8,128)(2,1)}, u32[]{:S(2)}) copy-start(bf16[192,192]{1,0:T(8,128)(2,1)} %constant.72.clone.high_ref) | copy-start | bytes 221188
  180.2 11.0 %copy-start.18 = (f32[1,1,128]{2,1,0:T(1,128)S(1)}, f32[1,1,128]{2,1,0:T(1,128)}, u32[]{:S(2)}) copy-start(f32[1,1,128]{2,1,0:T(1,128)} %copy-done.17) | copy-start | bytes 1540
  191.2 1.3 copy-start.3
  192.5 9.9 %copy-start.2 = (bf16[256,256]{1,0:T(8,128)(2,1)S(1)}, bf16[256,256]{1,0:T(8,128)(2,1)}, u32[]{:S(2)}) copy-start(bf16[256,256]{1,0:T(8,128)(2,1)} %constant.62.clone.flip_ref) | copy-start | bytes 393220
  213.1 38.3 %collective-permute-start.9 = (f32[1,192,1536]{2,1,0:T(8,128)}, f32[1,192,1536]{2,1,0:T(8,128)S(1)}, u32[]{:S(2)}, u32[]{:S(2)}) collective-permute-start(f32[1,192,1536]{2,1,0:T(8,128)} %get-tuple-element.50), channel_id=1, source_target_pairs={{8,0},{16,8},{24,16},{9,1},{17,9},{25,17},{10,2},{18,10},{26,18},{... | collective-permute-start | bytes 3538952 | tf_op jit(solution)/shard_map/ppermute | solution.py:1156
  239.8 11.7 %all-to-all-start.3 = ((f32[32,1,128]{2,1,0:T(1,128)}), f32[32,1,128]{2,1,0:T(1,128)S(1)}, u32[]{:S(2)}, u32[]{:S(2)}) async-start(f32[32,1,128]{2,1,0:T(1,128)} %get-tuple-element.48), calls=%async_computation.3 | async-start | bytes 32768 | tf_op jit(solution)/shard_map/all_to_all | solution.py:1161
